TPU v7x, 32 devices: a whole 2x2x4 slice. The times are simulated.
32 devices in a mesh: lag: 4 (over y, core), col: 8 (over z, x).
Axes of the slice: x: 2, y: 2, z: 4, core: 2. Of those that a mesh axis runs over, the one named last changes fastest.
Arguments:
- lag_matrices: float32 [64, 2048, 2048], P('lag', None, 'col'), may hold values from -0.03125 to 0.03125
- history: float32 [64, 2048, 256], P('lag', 'col'), may hold values from -6 to 6
- excitation: float32 [4, 2048, 256], P(None, 'col'), may hold values from -6 to 6
Outputs:
- densities: float32 [4, 2048, 256], P(None, 'col')
All inputs are finite; a program needn't handle non-finite values.
Results may differ from a plain program's by a relative error of at most 0.0001.
Values sent between devices are 32-bit elements; how exact they have to be, the bound alone decides.
No kernel may reach another device: no remote copies, remote signals or barrier semaphores. Data moves between devices by JAX's collectives and lax.ppermute only.
A program may use at most 128 MiB of HBM per device.

v0:
```python
import jax
import jax.numpy as jnp
from jax import lax
from jax.sharding import PartitionSpec as P


def passed_along(value, axis, steps):
    count = lax.axis_size(axis)
    first, last = (max(0, -steps), min(count, count - steps))
    return lax.ppermute(value, axis, [(source, source + steps) for source in range(first, last)])


def apply_lags(matrices, sources):
    return jnp.einsum("jab,jbs->as", matrices, sources, precision=lax.Precision.HIGHEST)


def local(lag_matrices, history, excitation):
    lag_count = lag_matrices.shape[0]
    block_rows = lag_matrices.shape[2]
    total_steps = excitation.shape[0]
    back_steps = total_steps - 1
    owner_index = lax.axis_index("lag")
    is_head = (owner_index == 0).astype(jnp.float32)
    carried = passed_along(history[lag_count - back_steps :], "lag", 1)
    blank = jnp.zeros_like(history[0])
    newest = []
    for moment in range(total_steps):
        pre_new = jnp.stack(
            [
                newest[back_steps - 1 - offset] if back_steps - 1 - offset < moment else blank
                for offset in range(back_steps)
            ]
        )
        extended = jnp.concatenate([carried + is_head * pre_new, history], axis=0)
        sources = extended[back_steps - moment : back_steps - moment + lag_count]

        def step_term(row_start, row_count, sources=sources):
            return apply_lags(lag_matrices, sources)

        summed = lax.psum_scatter(
            step_term(jnp.int32(0), block_rows * lax.axis_size("col")),
            "col",
            scatter_dimension=0,
            tiled=True,
        )
        summed = lax.psum(summed, "lag")
        newest.append(excitation[moment] - summed)
    return jnp.stack(newest)


def solution(mesh):
    return jax.shard_map(
        local,
        mesh=mesh,
        in_specs=(P("lag", None, "col"), P("lag", "col", None), P(None, "col", None)),
        out_specs=P(None, "col", None),
        check_vma=False,
    )
```

profile of v0, /device:TPU:0, one launch (start us, length us, event | category | flops | bytes accessed | tf_op | source)
XLA Modules:
  0.0 555.5 jit_solution(5949560813634068522)
XLA Ops:
  6.5 31.5 %convolution_bitcast_fusion = f32[2048,256]{1,0:T(8,128)} fusion(f32[16,2048,256]{2,1,0:T(8,128)} %param.3, f32[16,256,256]{2,1,0:T(8,128)} %param.4), kind=kOutput, calls=%fused_computation.12 | convolution fusion | flops 25769803776 | bytes 39845888 | tf_op jit(solution)/shard_map/jab,jbs->as/dot_general | solution.py:14
  38.0 0.0 all-reduce.6.cloned.1.call-start
  38.1 1.2 slice.26
  39.3 2.4 collective-permute-start
  41.7 66.9 %reduce-scatter.5.cloned.1.call-done = f32[256,256]{1,0:T(8,128)} async-done(((f32[2048,256]{1,0:T(8,128)}), f32[256,256]{1,0:T(8,128)}) %reduce-scatter.5.cloned.1.call-update) | async-done | bytes 262160 | tf_op jit(solution)/shard_map/reduce_scatter | solution.py:40
  108.6 0.2 reduce-scatter.7.cloned.1.call-start
  108.8 5.4 copy.5
  114.2 27.8 %all-reduce.6.cloned.1.call-done = f32[256,256]{1,0:T(8,128)} async-done(((f32[256,256]{1,0:T(8,128)}), f32[256,256]{1,0:T(8,128)}) %all-reduce.6.cloned.1.call-update) | async-done | bytes 262160 | tf_op jit(solution)/shard_map/psum | solution.py:46
  141.9 1.1 fusion.16
  143.0 0.1 multiply_add_fusion
  143.1 0.3 copy.4
  143.3 31.9 %fusion.8 = f32[2048,256]{1,0:T(8,128)} fusion(f32[16,2048,256]{2,1,0:T(8,128)} %param.3, f32[16,256,256]{1,2,0:T(8,128)} %copy.5, f32[3,256,256]{1,2,0:T(8,128)S(1)} %copy.4), kind=kOutput, calls=%fused_computation.11 | convolution fusion | flops 25771048960 | bytes 40632320 | tf_op jit(solution)/shard_map/jab,jbs->as/dot_general | solution.py:14
  175.2 0.0 all-reduce.8.cloned.1.call-start
  175.3 67.9 %reduce-scatter.7.cloned.1.call-done = f32[256,256]{1,0:T(8,128)} async-done(((f32[2048,256]{1,0:T(8,128)}), f32[256,256]{1,0:T(8,128)}) %reduce-scatter.7.cloned.1.call-update) | async-done | bytes 262160 | tf_op jit(solution)/shard_map/reduce_scatter | solution.py:40
  243.2 0.0 reduce-scatter.9.cloned.1.call-start
  243.3 33.2 %all-reduce.8.cloned.1.call-done = f32[256,256]{1,0:T(8,128)} async-done(((f32[256,256]{1,0:T(8,128)}), f32[256,256]{1,0:T(8,128)}) %all-reduce.8.cloned.1.call-update) | async-done | bytes 262160 | tf_op jit(solution)/shard_map/psum | solution.py:46
  276.5 1.1 fusion.15
  277.5 0.1 fusion.10
  277.7 0.3 copy.7
  278.0 32.6 %fusion.7 = f32[2048,256]{1,0:T(8,128)} fusion(f32[16,2048,256]{2,1,0:T(8,128)} %param.3, f32[16,256,256]{1,2,0:T(8,128)} %copy.5, f32[3,256,256]{1,2,0:T(8,128)S(1)} %copy.7), kind=kOutput, calls=%fused_computation.10 | convolution fusion | flops 25771048960 | bytes 40632320 | tf_op jit(solution)/shard_map/jab,jbs->as/dot_general | solution.py:14
  310.6 0.3 all-reduce.10.cloned.1.call-start
  310.9 67.6 %reduce-scatter.9.cloned.1.call-done = f32[256,256]{1,0:T(8,128)} async-done(((f32[2048,256]{1,0:T(8,128)}), f32[256,256]{1,0:T(8,128)}) %reduce-scatter.9.cloned.1.call-update) | async-done | bytes 262160 | tf_op jit(solution)/shard_map/reduce_scatter | solution.py:40
  378.6 33.1 %all-reduce.10.cloned.1.call-done = f32[256,256]{1,0:T(8,128)} async-done(((f32[256,256]{1,0:T(8,128)}), f32[256,256]{1,0:T(8,128)}) %all-reduce.10.cloned.1.call-update) | async-done | bytes 262160 | tf_op jit(solution)/shard_map/psum | solution.py:46
  411.7 1.1 fusion.14
  412.8 0.1 fusion.12
  412.9 0.3 copy.10
  413.2 31.8 %fusion.6 = f32[2048,256]{1,0:T(8,128)} fusion(f32[16,2048,256]{2,1,0:T(8,128)} %param.3, f32[16,256,256]{1,2,0:T(8,128)} %copy.5, f32[3,256,256]{1,2,0:T(8,128)S(1)} %copy.10), kind=kOutput, calls=%fused_computation.9 | convolution fusion | flops 25771048960 | bytes 40632320 | tf_op jit(solution)/shard_map/jab,jbs->as/dot_general | solution.py:14
  445.0 0.0 all-reduce.12.cloned.1.call-start
  445.0 68.0 %reduce-scatter.11.cloned.1.call-done = f32[256,256]{1,0:T(8,128)} async-done(((f32[2048,256]{1,0:T(8,128)}), f32[256,256]{1,0:T(8,128)}) %reduce-scatter.11.cloned.1.call-update) | async-done | bytes 262160 | tf_op jit(solution)/shard_map/reduce_scatter | solution.py:40
  513.1 33.4 %all-reduce.12.cloned.1.call-done = f32[256,256]{1,0:T(8,128)} async-done(((f32[256,256]{1,0:T(8,128)}), f32[256,256]{1,0:T(8,128)}) %all-reduce.12.cloned.1.call-update) | async-done | bytes 262160 | tf_op jit(solution)/shard_map/psum | solution.py:46
  546.5 1.1 fusion.13
  547.6 1.1 pad_maximum_fusion.12
  (12 shorter events, 0.2 us)
Async XLA Ops:
  6.5 102.0 %reduce-scatter.5.cloned.1.call-start = ((), (), s32[]{:S(2)}) async-start(), calls=%async_computation.4 | async-start | bytes 2359296 | tf_op jit(solution)/shard_map/reduce_scatter | solution.py:40
  38.0 103.9 %all-reduce.6.cloned.1.call-start = ((), (), s32[]{:S(2)}) async-start(), calls=%async_computation.5 | async-start | bytes 524288 | tf_op jit(solution)/shard_map/psum | solution.py:46
  39.3 103.7 %collective-permute-start = (f32[3,256,256]{2,1,0:T(8,128)S(1)}, f32[3,256,256]{2,1,0:T(8,128)S(1)}, u32[]{:S(2)}, u32[]{:S(2)}) collective-permute-start(f32[3,256,256]{2,1,0:T(8,128)S(1)} %slice.26), channel_id=1, source_target_pairs={{0,8},{8,16},{16,24},{1,9},{9,17},{17,25},{2,10},{10,18},{18,26},{... | collective-permute-start | bytes 2359304 | tf_op jit(solution)/shard_map/ppermute | solution.py:10
  108.6 134.6 %reduce-scatter.7.cloned.1.call-start = ((), (), s32[]{:S(2)}) async-start(), calls=%async_computation.6 | async-start | bytes 2359296 | tf_op jit(solution)/shard_map/reduce_scatter | solution.py:40
  175.2 101.2 %all-reduce.8.cloned.1.call-start = ((), (), s32[]{:S(2)}) async-start(), calls=%async_computation.7 | async-start | bytes 524288 | tf_op jit(solution)/shard_map/psum | solution.py:46
  243.2 135.3 %reduce-scatter.9.cloned.1.call-start = ((), (), s32[]{:S(2)}) async-start(), calls=%async_computation.8 | async-start | bytes 2359296 | tf_op jit(solution)/shard_map/reduce_scatter | solution.py:40
  310.6 101.1 %all-reduce.10.cloned.1.call-start = ((), (), s32[]{:S(2)}) async-start(), calls=%async_computation.9 | async-start | bytes 524288 | tf_op jit(solution)/shard_map/psum | solution.py:46
  378.5 134.5 %reduce-scatter.11.cloned.1.call-start = ((), (), s32[]{:S(2)}) async-start(), calls=%async_computation.10 | async-start | bytes 2359296 | tf_op jit(solution)/shard_map/reduce_scatter | solution.py:40
  445.0 101.5 %all-reduce.12.cloned.1.call-start = ((), (), s32[]{:S(2)}) async-start(), calls=%async_computation.11 | async-start | bytes 524288 | tf_op jit(solution)/shard_map/psum | solution.py:46
Sparse Core Ops, SparseCore 0:
  38.1 70.3 reduce-scatter.4
  110.9 30.9 all-reduce.5
  175.4 67.7 reduce-scatter.6
  245.5 30.9 all-reduce.7
  310.7 67.7 reduce-scatter.8
  380.7 30.9 all-reduce.9
  445.1 67.8 reduce-scatter.10
  515.5 30.9 all-reduce.11
where the time goes:
time: 556 us; the launch traced here: 555 us
  waiting for transfers between devices  398 us (72%)
  matrix products  128 us (23%)
  between operations  13.6 us (2%)
  local copies, waits for them, and re-layouts  7.34 us (1%)
  other arithmetic  5.64 us (1%)
    reduce_scatter x4, waiting for transfers between devices, local(): lax.psum_scatter(step_term(jnp.int32(0), block_rows * lax.axis_size('col'...  270 us
    dot_general x4, matrix products, apply_lags(): jnp.einsum('jab,jbs->as', matrices, sources, precision=lax.Precision.HIGH...  128 us
    psum x4, waiting for transfers between devices, local(): summed = lax.psum(summed, 'lag')  127 us
  transfers between devices with their start and end apart: 9, of which 8 were waited for; matrix products, arithmetic and copies ran while one was open for 1% of the time, Pallas kernels for 0%

commit v1 on v0

v1 whole, which is shorter than its diff:
```python
import functools

import jax
import jax.numpy as jnp
from jax import lax
from jax.experimental import pallas as pl
from jax.experimental.pallas import tpu as pltpu
from jax.sharding import PartitionSpec as P

LANES = 128
BF = jnp.bfloat16
F32 = jnp.float32
FIRST = ((1, 1), (1, 2), (2, 1), (2, 2))
REST = ((1, 3), (2, 3), (3, 1), (3, 2), (3, 3))
MEMBERS = {1: (1,), 2: (0, 1), 3: (0,)}


def swap_pairs(axis, bit):
    return [(i, i ^ bit) for i in range(lax.axis_size(axis))]


def exchanged(value, axis, bit):
    return lax.ppermute(value, axis, swap_pairs(axis, bit))


def bit_count(n):
    return n.bit_length() - 1


def reversed_bits(n):
    bits = bit_count(n)
    return [sum(((i >> b) & 1) << (bits - 1 - b) for b in range(bits)) for i in range(n)]


def split(v):
    hi = v.astype(BF)
    return hi, (v - hi.astype(F32)).astype(BF)


def dot(a, b):
    return jnp.dot(a, b, preferred_element_type=F32)


def flipped(v, own, slices):
    cols = v.shape[-1]
    width = cols // slices
    for b in range(bit_count(slices)):
        step = width << b
        swapped = jnp.concatenate(
            [v[:, (start ^ step) : (start ^ step) + step] for start in range(0, cols, step)], axis=1
        )
        v = jnp.where(((own >> b) & 1) == 1, swapped, v)
    return v


def folded(v):
    rows, width = v.shape
    parts = LANES // width
    step = rows // parts
    return jnp.concatenate([v[s * step : (s + 1) * step] for s in range(parts)], axis=1) if parts > 1 else v


def unfolded(v, width):
    parts = LANES // width
    return jnp.concatenate([v[:, s * width : (s + 1) * width] for s in range(parts)], axis=0) if parts > 1 else v


def write_folded(y, block, keep_ref, send_ref, slices):
    width = y.shape[1] // slices
    small = block * width // LANES
    order = reversed_bits(slices)
    half = slices // 2
    for b in range(y.shape[0] // block):
        rows = y[b * block : (b + 1) * block]
        for i, p in enumerate(order):
            piece = folded(rows[:, p * width : (p + 1) * width])
            ref = keep_ref if i < half else send_ref
            ref[i % half, b * small : (b + 1) * small, :] = piece


def source_sums(get, outer, inner, base):
    def along(inner_offset):
        if outer == 1:
            return get(base + 2 + inner_offset) - get(base + inner_offset)
        if outer == 2:
            return get(base + inner_offset)
        return get(base + inner_offset) - get(base - 2 + inner_offset)

    if inner == 1:
        return along(1) - along(0)
    if inner == 2:
        return along(0)
    return along(0) - along(-1)


def prepare_sources(kinds, get, own, slices, groups, hi_ref, lo_ref):
    block = hi_ref.shape[1] // groups
    for i, (outer, inner) in enumerate(kinds):
        for g in range(groups):
            hi, lo = split(flipped(source_sums(get, outer, inner, 4 * g), own, slices))
            hi_ref[i, g * block : (g + 1) * block, :] = hi
            lo_ref[i, g * block : (g + 1) * block, :] = lo


def products(kinds, a_ref, hi_ref, lo_ref):
    groups = a_ref.shape[0] // 4
    out = []
    for i, (outer, inner) in enumerate(kinds):
        his, los = [], []
        for g in range(groups):
            total = None
            for u in MEMBERS[outer]:
                for v in MEMBERS[inner]:
                    term = a_ref[4 * g + 2 * u + v]
                    total = term if total is None else total + term
            hi, lo = split(total)
            his.append(hi)
            los.append(lo)
        hi, lo = jnp.concatenate(his, axis=1), jnp.concatenate(los, axis=1)
        out.append(dot(hi, hi_ref[i]) + dot(hi, lo_ref[i]) + dot(lo, hi_ref[i]))
    return out


def first_kernel(own_ref, history_ref, a_ref, keep_ref, send_ref, q1_ref, q2_ref, q3_ref, hi_ref, lo_ref, *, slices, block):
    groups = a_ref.shape[0] // 4

    @pl.when(pl.program_id(0) == 0)
    def _():
        prepare_sources(FIRST, lambda i: history_ref[i], own_ref[0], slices, groups, hi_ref, lo_ref)

    p11, p12, p21, p22 = products(FIRST, a_ref, hi_ref, lo_ref)
    q1 = p12 + p22
    q1_ref[...] = q1
    q2_ref[...] = p21 + p22
    q3_ref[...] = p22
    write_folded(q1 + (p11 + p21), block, keep_ref, send_ref, slices)


def rest_kernel(own_ref, history_ref, carried_ref, a_ref, q1_ref, q2_ref, q3_ref, *refs, slices, block):
    outs, (hi_ref, lo_ref) = refs[:-2], refs[-2:]
    groups = a_ref.shape[0] // 4
    back = carried_ref.shape[0]

    @pl.when(pl.program_id(0) == 0)
    def _():
        def get(i):
            return history_ref[i] if i >= 0 else carried_ref[back + i]

        prepare_sources(REST, get, own_ref[0], slices, groups, hi_ref, lo_ref)

    p13, p23, p31, p32, p33 = products(REST, a_ref, hi_ref, lo_ref)
    y1 = q1_ref[...] - (p13 + p23)
    y2 = q2_ref[...] - (p31 + p32)
    y3 = (q3_ref[...] - p23) - (p32 - p33)
    for n, y in enumerate((y1, y2, y3)):
        write_folded(y, block, outs[2 * n], outs[2 * n + 1], slices)


def smem():
    return pl.BlockSpec(memory_space=pltpu.SMEM)


def bulk(kernel, name, kinds, own, whole, matrices, partials, steps, slices, tile):
    lags, rows, block = matrices.shape
    cols = whole[0].shape[2]
    groups = lags // 4
    small = tile * (cols // slices) // LANES
    flat = jax.ShapeDtypeStruct((slices // 2, rows * (cols // slices) // LANES, LANES), F32)
    flat_spec = pl.BlockSpec((slices // 2, small, LANES), lambda i: (0, i, 0))
    row_spec = pl.BlockSpec((tile, cols), lambda i: (i, 0))
    saved = 0 if partials else 3
    return pl.pallas_call(
        functools.partial(kernel, slices=slices, block=block),
        grid=(rows // tile,),
        in_specs=[smem()]
        + [pl.BlockSpec(w.shape, lambda i: (0, 0, 0)) for w in whole]
        + [pl.BlockSpec((lags, tile, block), lambda i: (0, i, 0))]
        + [row_spec] * len(partials),
        out_specs=[flat_spec] * (2 * steps) + [row_spec] * saved,
        out_shape=[flat] * (2 * steps) + [jax.ShapeDtypeStruct((rows, cols), F32)] * saved,
        scratch_shapes=[pltpu.VMEM((len(kinds), groups * block, cols), BF)] * 2,
        compiler_params=pltpu.CompilerParams(vmem_limit_bytes=56 << 20),
        cost_estimate=pl.CostEstimate(
            flops=2 * 3 * len(kinds) * groups * rows * block * cols,
            bytes_accessed=4 * (matrices.size + 4 * rows * cols),
            transcendentals=0,
        ),
        name=name,
    )(own, *whole, matrices, *partials)


def merge_kernel(own_ref, a_ref, b_ref, keep_ref, send_ref):
    own = own_ref[0]
    for q in range(a_ref.shape[0]):
        c = own ^ q
        (send_ref if q % 2 else keep_ref)[q // 2] = a_ref[c] + b_ref[c]


def chain_kernel(own_ref, e_ref, a_ref, b_ref, m_ref, *refs, width):
    parts, (x_ref, keep_ref, send_ref) = refs[:-3], refs[-3:]
    own = own_ref[0]
    total = parts[0][...]
    for part in parts[1:]:
        total = total + part[...]
    x = e_ref[...] - total
    x_ref[...] = x
    block = m_ref.shape[1]
    x_hi, x_lo = split(unfolded(x, width))
    x_both = jnp.concatenate([x_hi, x_lo], axis=1)
    for q in range(a_ref.shape[0]):
        c = own ^ q
        m_hi, m_lo = split(m_ref[pl.ds(pl.multiple_of(c * block, block), block), :])
        both = dot(m_hi, x_both)
        y = both[:, :width] + both[:, width:] + dot(m_lo, x_hi)
        (send_ref if q % 2 else keep_ref)[q // 2] = folded(y) + (a_ref[c] + b_ref[c])


def late_kernel(own_ref, acc_ref, *refs, width, owners):
    out_ref, pairs = refs[-1], refs[:-1]
    half, rows, _ = acc_ref.shape

    @pl.when(own_ref[0] >= owners)
    def _():
        out_ref[...] = acc_ref[...]

    @pl.when(own_ref[0] < owners)
    def _():
        block = pairs[0].shape[1]
        small = block * width // LANES
        sources = []
        for i in range(0, len(pairs), 2):
            x = jnp.concatenate([unfolded(pairs[i + 1][p], width) for p in range(half)], axis=1)
            sources.append(split(x))
        for c in range(pairs[0].shape[0] // block):
            y = None
            for i, (x_hi, x_lo) in enumerate(sources):
                m_hi, m_lo = split(pairs[2 * i][c * block : (c + 1) * block, :])
                term = dot(m_hi, x_hi) + dot(m_hi, x_lo) + dot(m_lo, x_hi)
                y = term if y is None else y + term
            for p in range(half):
                at = (p, slice(c * small, (c + 1) * small))
                out_ref[at] = acc_ref[at] + folded(y[:, p * width : (p + 1) * width])


def fields_kernel(own_ref, e_ref, out_ref, *, slices):
    width = e_ref.shape[2] // slices
    for n in range(e_ref.shape[0]):
        out_ref[n] = folded(flipped(e_ref[n], own_ref[0], slices)[:, :width])


def assemble_kernel(own_ref, parts_ref, out_ref, *, slices):
    width = out_ref.shape[2] // slices
    order = reversed_bits(slices)
    for n in range(out_ref.shape[0]):
        pieces = [None] * slices
        for i, p in enumerate(order):
            pieces[p] = unfolded(parts_ref[i, n], width)
        out_ref[n] = flipped(jnp.concatenate(pieces, axis=1), own_ref[0], slices)


def whole_call(kernel, name, out_shapes, *args):
    vmem = pl.BlockSpec(memory_space=pltpu.VMEM)
    out = [jax.ShapeDtypeStruct(s, F32) for s in out_shapes]
    return pl.pallas_call(
        kernel,
        in_specs=[smem()] + [vmem] * (len(args) - 1),
        out_specs=[vmem] * len(out),
        out_shape=out,
        compiler_params=pltpu.CompilerParams(vmem_limit_bytes=40 << 20),
        name=name,
    )(*args)


def local(lag_matrices, history, excitation):
    owners, columns = lax.axis_size("lag"), lax.axis_size("col")
    owner, column = lax.axis_index("lag"), lax.axis_index("col")
    lags, rows, block = lag_matrices.shape
    steps, _, cols = excitation.shape
    width = cols // owners
    small = block * width // LANES
    bits = bit_count(owners)
    back = steps - 1
    own_lag = jnp.reshape(owner, (1,)).astype(jnp.int32)
    own_col = jnp.reshape(column, (1,)).astype(jnp.int32)
    tile = min(rows, 512)

    carried = lax.ppermute(history[lags - back :], "lag", [(i, i + 1) for i in range(owners - 1)])

    newest = lag_matrices[0]
    for b in reversed(range(1, bits)):
        pairs = [(i, i + (1 << b)) for i in range(0, owners, 2 << b)]
        got = lax.ppermute(newest, "lag", pairs)
        newest = jnp.where((owner >> b) & 1 == 1, got, newest)
    got = lax.ppermute(newest, "lag", [(i, i + 1) for i in range(0, owners, 2)])
    newest = jnp.where(owner & 1 == 1, got, newest)
    older = lag_matrices[1:back]
    got = lax.ppermute(older, "lag", [(0, 1)])
    older = jnp.where(owner & 1 == 1, got, older)

    field = whole_call(functools.partial(fields_kernel, slices=owners), "fields", [(steps, small, LANES)], own_lag, excitation)[0]
    keep0, send0, q1, q2, q3 = bulk(first_kernel, "first", FIRST, own_lag, [history], lag_matrices, [], 1, owners, tile)
    rest = bulk(rest_kernel, "rest", REST, own_lag, [history, carried], lag_matrices, [q1, q2, q3], back, owners, tile)
    keeps = [keep0, *rest[0::2]]
    sends = [send0, *rest[1::2]]

    def own_sums(n, gathered):
        acc = keeps[n] + exchanged(sends[n], "lag", 1)
        if n >= 2:
            args = []
            for k in range(2, n + 1):
                args += [older[k - 2], gathered[n - k]]
            acc = whole_call(functools.partial(late_kernel, width=width, owners=2), "late", [acc.shape], own_lag, acc, *args)[0]
        for b in range(1, bits):
            half = acc.shape[0] // 2
            got = exchanged(acc[half:], "lag", 1 << b)
            if half == 1:
                return acc[0], got[0]
            acc = acc[:half] + got
        return acc[0], jnp.zeros_like(acc[0])

    def scattered(keep, send):
        acc = keep + exchanged(send, "col", 1)
        bit = 2
        while acc.shape[0] > 4:
            got = exchanged(acc[1::2], "col", bit)
            acc = acc[0::2] + got
            bit *= 2
        return [acc[0]] + [exchanged(acc[d], "col", d * bit) for d in range(1, acc.shape[0])]

    halves = [(columns // 2, small, LANES)] * 2
    shaped = (columns, small, LANES)
    found, gathered = [], []
    a, b = own_sums(0, gathered)
    keep, send = whole_call(merge_kernel, "merge", halves, own_col, a.reshape(shaped), b.reshape(shaped))
    for n in range(1, steps):
        parts = scattered(keep, send)
        a, b = own_sums(n, gathered)
        x, keep, send = whole_call(
            functools.partial(chain_kernel, width=width), "chain", [(small, LANES), *halves],
            own_col, field[n - 1], a.reshape(shaped), b.reshape(shaped), newest, *parts,
        )
        found.append(x)
        near = x[None]
        for bit in reversed(range(1, bits)):
            near = jnp.concatenate([near, exchanged(near, "lag", 1 << bit)], axis=0)
        gathered.append(near)
    parts = scattered(keep, send)
    x = field[steps - 1] - functools.reduce(jnp.add, parts)
    near = x[None]
    for bit in reversed(range(1, bits)):
        near = jnp.concatenate([near, exchanged(near, "lag", 1 << bit)], axis=0)
    gathered.append(near)
    every = jnp.stack(gathered, axis=1)
    every = jnp.concatenate([every, exchanged(every, "lag", 1)], axis=0)
    return whole_call(functools.partial(assemble_kernel, slices=owners), "assemble", [excitation.shape], own_lag, every)[0]


def solution(mesh):
    return jax.shard_map(
        local,
        mesh=mesh,
        in_specs=(P("lag", None, "col"), P("lag", "col", None), P(None, "col", None)),
        out_specs=P(None, "col", None),
        check_vma=False,
    )
```

time: 556 us -> 180 us (0.32)
  waiting for transfers between devices: 398 us -> 57.7 us
  matrix products: 128 us -> 0 us
  Pallas kernels: 0 us -> 57.4 us
  starting transfers between devices: 3.09 us -> 42.4 us
  between operations: 13.6 us -> 0.37 us
  other arithmetic: 5.64 us -> 11.3 us
    reduce_scatter x4 -> x0, waiting for transfers between devices: 270 us -> none  [local(): lax.psum_scatter(step_term(jnp.int32(0), block_rows * lax.axis_size('col'...]
    dot_general x4 -> x0, matrix products: 128 us -> none  [apply_lags(): jnp.einsum('jab,jbs->as', matrices, sources, precision=lax.Precision.HIGH...]
    psum x4 -> x0, waiting for transfers between devices: 127 us -> none  [local(): summed = lax.psum(summed, 'lag')]
    ppermute x1 -> x33, waiting for transfers between devices: 0.01 us -> 57.7 us  [the longest x29 57.7 us: exchanged(): return lax.ppermute(value, axis, swap_pairs(axis, bit))]
    pallas_call x0 -> x10, Pallas kernels: none -> 57.4 us  [the longest x2 48.5 us: bulk(): pl.pallas_call(functools.partial(kernel, slices=slices, block=block), gri...]
    ppermute x1 -> x33, starting transfers between devices: 2.41 us -> 42.4 us  [the longest x29 28.1 us: exchanged(): return lax.ppermute(value, axis, swap_pairs(axis, bit))]
    select_n x0 -> x3, other arithmetic: none -> 7.76 us  [the longest x1 3.17 us: local(): newest = jnp.where(owner >> b & 1 == 1, got, newest)]
    slice x1 -> x6, local copies, waits for them, and re-layouts: 1.19 us -> 6.8 us  [the longest x1 4.44 us: local(): older = lag_matrices[1:back]]
  transfers between devices with their start and end apart: 9 -> 33, of which waited for: 8 -> 16; matrix products, arithmetic and copies ran while one was open for 1% -> 10% of each run, Pallas kernels for 0% -> 30%
where the time goes in v1:
time: 180 us; the launch traced here: 179 us
  waiting for transfers between devices  57.7 us (32%)
  Pallas kernels  57.4 us (32%)
  starting transfers between devices  42.4 us (24%)
  other arithmetic  11.3 us (6%)
  local copies, waits for them, and re-layouts  10.2 us (6%)
    ppermute x29, waiting for transfers between devices, exchanged(): return lax.ppermute(value, axis, swap_pairs(axis, bit))  57.7 us
    pallas_call x2, Pallas kernels, bulk(): pl.pallas_call(functools.partial(kernel, slices=slices, block=block), gri...  48.5 us
    ppermute x29, starting transfers between devices, exchanged(): return lax.ppermute(value, axis, swap_pairs(axis, bit))  28.1 us
    pallas_call x8, Pallas kernels, whole_call(): pl.pallas_call(kernel, in_specs=[smem()] + [vmem] * (len(args) - 1), out_...  8.91 us
    ppermute x1, starting transfers between devices, local(): got = lax.ppermute(newest, 'lag', pairs)  4.99 us
    slice x1, local copies, waits for them, and re-layouts, local(): older = lag_matrices[1:back]  4.44 us
    ppermute x1, starting transfers between devices, local(): got = lax.ppermute(older, 'lag', [(0, 1)])  4.42 us
  transfers between devices with their start and end apart: 33, of which 16 were waited for; matrix products, arithmetic and copies ran while one was open for 10% of the time, Pallas kernels for 30%

profile of v1, /device:TPU:0, one launch (start us, length us, event | category | flops | bytes accessed | tf_op | source)
XLA Modules:
  0.0 179.4 jit_solution(8281099438994957350)
XLA Ops:
  0.0 3.0 %slice_bitcast_fusion.2 = f32[2048,256]{1,0:T(8,128)} fusion(f32[16,2048,256]{2,1,0:T(8,128)} %a_ref.3), kind=kLoop, calls=%fused_computation.2 | loop fusion | bytes 4194304 | tf_op jit(solution)/shard_map/squeeze | solution.py:289
  3.0 5.0 %collective-permute-start.3 = (f32[2048,256]{1,0:T(8,128)}, f32[2048,256]{1,0:T(8,128)S(1)}, u32[]{:S(2)}, u32[]{:S(2)}) collective-permute-start(f32[2048,256]{1,0:T(8,128)} %slice_bitcast_fusion.2), channel_id=1, source_target_pairs={{0,16},{1,17},{2,18},{3,19},{4,20},{5,21},{6,22},{7,23}} | collective-permute-start | bytes 6291464 | tf_op jit(solution)/shard_map/ppermute | solution.py:292
  8.0 2.1 %slice.101 = f32[3,256,256]{2,1,0:T(8,128)} slice(f32[16,256,256]{2,1,0:T(8,128)} %history_ref.3), slice={[13:16], [0:256], [0:256]} | slice | bytes 1572864 | tf_op jit(solution)/shard_map/slice | solution.py:287
  10.1 2.2 %collective-permute-start = (f32[3,256,256]{2,1,0:T(8,128)}, f32[3,256,256]{2,1,0:T(8,128)}, u32[]{:S(2)}, u32[]{:S(2)}) collective-permute-start(f32[3,256,256]{2,1,0:T(8,128)} %slice.101), channel_id=1, source_target_pairs={{0,8},{8,16},{16,24},{1,9},{9,17},{17,25},{2,10},{10,18},{18,26},{... | collective-permute-start | bytes 2359304 | tf_op jit(solution)/shard_map/ppermute | solution.py:287
  12.3 22.1 %first.1 = (f32[2,1024,128]{2,1,0:T(8,128)}, f32[2,1024,128]{2,1,0:T(8,128)}, f32[2048,256]{1,0:T(8,128)}, f32[2048,256]{1,0:T(8,128)}, f32[2048,256]{1,0:T(8,128)}) custom-call(s32[1]{0:T(128)} %bitcast.own_ref, f32[16,256,256]{2,1,0:T(8,128)} %history_ref.3, f32[16,2048,256]{2,1,0:T(8,128)} %a_ref.3), custom_call_target="tpu_custom_call" | custom-call | flops 12884901888 | bytes 41943040 | tf_op jit(solution)/shard_map/first/pallas_call | solution.py:172
  34.4 4.4 %slice.112 = f32[2,2048,256]{2,1,0:T(8,128)} slice(f32[16,2048,256]{2,1,0:T(8,128)} %a_ref.3), slice={[1:3], [0:2048], [0:256]} | slice | bytes 8388608 | tf_op jit(solution)/shard_map/slice | solution.py:296
  38.9 4.4 %collective-permute-start.13 = (f32[2,2048,256]{2,1,0:T(8,128)}, f32[2,2048,256]{2,1,0:T(8,128)}, u32[]{:S(2)}, u32[]{:S(2)}) collective-permute-start(f32[2,2048,256]{2,1,0:T(8,128)} %slice.112), channel_id=1, source_target_pairs={{0,8},{1,9},{2,10},{3,11},{4,12},{5,13},{6,14},{7,15}} | collective-permute-start | bytes 12582920 | tf_op jit(solution)/shard_map/ppermute | solution.py:297
  43.3 3.2 %broadcast_select_fusion.1 = f32[2048,256]{1,0:T(8,128)} fusion(f32[2048,256]{1,0:T(8,128)S(1)} %collective-permute-done.3, pred[]{:T(512)S(6)} %eq.8, f32[16,2048,256]{2,1,0:T(8,128)} %a_ref.3), kind=kLoop, calls=%fused_computation.5 | loop fusion | flops 524288 | bytes 6291457 | tf_op jit(solution)/shard_map/jit(_where)/select_n | solution.py:293
  46.5 2.7 %collective-permute-start.4 = (f32[2048,256]{1,0:T(8,128)}, f32[2048,256]{1,0:T(8,128)}, u32[]{:S(2)}, u32[]{:S(2)}) collective-permute-start(f32[2048,256]{1,0:T(8,128)} %broadcast_select_fusion.1), channel_id=1, source_target_pairs={{0,8},{16,24},{1,9},{17,25},{2,10},{18,26},{3,11},{19,27},{4,12},{... | collective-permute-start | bytes 6291464 | tf_op jit(solution)/shard_map/ppermute | solution.py:294
  49.2 26.4 %rest.1 = (f32[2,1024,128]{2,1,0:T(8,128)}, f32[2,1024,128]{2,1,0:T(8,128)}, f32[2,1024,128]{2,1,0:T(8,128)}, f32[2,1024,128]{2,1,0:T(8,128)}, f32[2,1024,128]{2,1,0:T(8,128)}, /*index=5*/f32[2,1024,128]{2,1,0:T(8,128)}) custom-call(s32[1]{0:T(128)} %bitcast.own_ref, f32[16,256,256]{2,1,0:T(8,128)} %history_ref.3, ...), custom_call_target="tpu_custom_call" | custom-call | flops 16106127360 | bytes 41943040 | tf_op jit(solution)/shard_map/rest/pallas_call | solution.py:172
  76.5 13.9 %collective-permute-done.6 = f32[1,1024,128]{2,1,0:T(8,128)S(1)} collective-permute-done((f32[1,1024,128]{2,1,0:T(8,128)S(1)}, f32[1,1024,128]{2,1,0:T(8,128)S(1)}, u32[]{:S(2)}, u32[]{:S(2)}) %collective-permute-start.6) | collective-permute-done | bytes 524320 | tf_op jit(solution)/shard_map/ppermute | solution.py:23
  92.6 5.3 %collective-permute-done.7 = f32[4,128,128]{2,1,0:T(8,128)S(1)} collective-permute-done((f32[4,128,128]{2,1,0:T(8,128)S(1)}, f32[4,128,128]{2,1,0:T(8,128)S(1)}, u32[]{:S(2)}, u32[]{:S(2)}) %collective-permute-start.7) | collective-permute-done | bytes 262176 | tf_op jit(solution)/shard_map/ppermute | solution.py:23
  98.0 3.7 %collective-permute-start.10 = (f32[128,128]{1,0:T(8,128)S(1)}, f32[128,128]{1,0:T(8,128)S(1)}, u32[]{:S(2)}, u32[]{:S(2)}) collective-permute-start(f32[128,128]{1,0:T(8,128)S(1)} %get-tuple-element.70), channel_id=1, source_target_pairs={{0,6},{1,7},{2,4},{3,5},{4,2},{5,3},{6,0},{7,1},{8,14},{9,15},{10,... | collective-permute-start | bytes 196616 | tf_op jit(solution)/shard_map/ppermute | solution.py:23
  101.7 1.6 add.33
  106.3 1.9 %broadcast_select_fusion.2.m_ref = f32[2048,256]{1,0:T(8,128)S(1)} fusion(f32[2048,256]{1,0:T(8,128)} %collective-permute-done.4, f32[2048,256]{1,0:T(8,128)} %broadcast_select_fusion.1, pred[]{:T(512)S(6)} %eq.7), kind=kLoop, calls=%fused_computation.6 | loop fusion | flops 524288 | bytes 6291457 | tf_op jit(solution)/shard_map/jit(_where)/select_n | solution.py:295
  108.6 8.6 %collective-permute-done.2 = f32[1,1024,128]{2,1,0:T(8,128)S(1)} collective-permute-done((f32[1,1024,128]{2,1,0:T(8,128)S(1)}, f32[1,1024,128]{2,1,0:T(8,128)S(1)}, u32[]{:S(2)}, u32[]{:S(2)}) %collective-permute-start.2) | collective-permute-done | bytes 524320 | tf_op jit(solution)/shard_map/ppermute | solution.py:23
  120.6 2.7 %broadcast_select_fusion = f32[2,2048,256]{2,1,0:T(8,128)S(1)} fusion(f32[2,2048,256]{2,1,0:T(8,128)} %collective-permute-done.13, pred[]{:T(512)S(6)} %eq.7, f32[16,2048,256]{2,1,0:T(8,128)} %a_ref.3), kind=kLoop, calls=%fused_computation.3 | loop fusion | flops 1048576 | bytes 12582913 | tf_op jit(solution)/shard_map/jit(_where)/select_n | solution.py:298
  127.1 2.6 %collective-permute-start.17 = (f32[128,128]{1,0:T(8,128)S(1)}, f32[128,128]{1,0:T(8,128)S(1)}, u32[]{:S(2)}, u32[]{:S(2)}) collective-permute-start(f32[128,128]{1,0:T(8,128)S(1)} %get-tuple-element.67), channel_id=1, source_target_pairs={{0,4},{1,5},{2,6},{3,7},{4,0},{5,1},{6,2},{7,3},{8,12},{9,13},{10,... | collective-permute-start | bytes 196616 | tf_op jit(solution)/shard_map/ppermute | solution.py:23
  130.1 3.2 %collective-permute-done.17.refs_2_ = f32[128,128]{1,0:T(8,128)S(1)} collective-permute-done((f32[128,128]{1,0:T(8,128)S(1)}, f32[128,128]{1,0:T(8,128)S(1)}, u32[]{:S(2)}, u32[]{:S(2)}) %collective-permute-start.17) | collective-permute-done | bytes 65568 | tf_op jit(solution)/shard_map/ppermute | solution.py:23
  133.2 2.5 %collective-permute-done.18.refs_3_ = f32[128,128]{1,0:T(8,128)S(1)} collective-permute-done((f32[128,128]{1,0:T(8,128)S(1)}, f32[128,128]{1,0:T(8,128)S(1)}, u32[]{:S(2)}, u32[]{:S(2)}) %collective-permute-start.18) | collective-permute-done | bytes 65568 | tf_op jit(solution)/shard_map/ppermute | solution.py:23
  139.5 2.6 %collective-permute-done.19 = f32[1,128,128]{2,1,0:T(8,128)S(1)} collective-permute-done((f32[1,128,128]{2,1,0:T(8,128)S(1)}, f32[1,128,128]{2,1,0:T(8,128)S(1)}, u32[]{:S(2)}, u32[]{:S(2)}) %collective-permute-start.19) | collective-permute-done | bytes 65568 | tf_op jit(solution)/shard_map/ppermute | solution.py:23
  142.1 2.0 %late.3 = f32[2,1024,128]{2,1,0:T(8,128)S(1)} custom-call(s32[1]{0:T(128)} %bitcast.own_ref, f32[2,1024,128]{2,1,0:T(8,128)S(1)} %add.38.acc_ref, f32[2048,256]{1,0:T(8,128)S(1)} %get-tuple-element.50.refs_0_, f32[2,128,128]{2,1,0:T(8,128)S(1)} %get-tuple-element.80.refs_1_, f32[2048,256]{1,0:T(8,128)S(1)} %get-tuple-element.49.refs_2_, ...), custom_call_target="tpu_custom_call" | custom-call | tf_op jit(solution)/shard_map/late/pallas_call | solution.py:264
  146.3 2.3 %collective-permute-start.24 = (f32[128,128]{1,0:T(8,128)S(1)}, f32[128,128]{1,0:T(8,128)S(1)}, u32[]{:S(2)}, u32[]{:S(2)}) collective-permute-start(f32[128,128]{1,0:T(8,128)S(1)} %get-tuple-element.63), channel_id=1, source_target_pairs={{0,4},{1,5},{2,6},{3,7},{4,0},{5,1},{6,2},{7,3},{8,12},{9,13},{10,... | collective-permute-start | bytes 196616 | tf_op jit(solution)/shard_map/ppermute | solution.py:23
  151.5 3.2 %collective-permute-done.25.refs_3_ = f32[128,128]{1,0:T(8,128)S(1)} collective-permute-done((f32[128,128]{1,0:T(8,128)S(1)}, f32[128,128]{1,0:T(8,128)S(1)}, u32[]{:S(2)}, u32[]{:S(2)}) %collective-permute-start.25) | collective-permute-done | bytes 65568 | tf_op jit(solution)/shard_map/ppermute | solution.py:23
  156.3 5.8 %collective-permute-done.27 = f32[4,128,128]{2,1,0:T(8,128)S(1)} collective-permute-done((f32[4,128,128]{2,1,0:T(8,128)S(1)}, f32[4,128,128]{2,1,0:T(8,128)S(1)}, u32[]{:S(2)}, u32[]{:S(2)}) %collective-permute-start.27) | collective-permute-done | bytes 262176 | tf_op jit(solution)/shard_map/ppermute | solution.py:23
  162.7 2.2 %collective-permute-start.29 = (f32[128,128]{1,0:T(8,128)S(1)}, f32[128,128]{1,0:T(8,128)S(1)}, u32[]{:S(2)}, u32[]{:S(2)}) collective-permute-start(f32[128,128]{1,0:T(8,128)S(1)} %get-tuple-element.61), channel_id=1, source_target_pairs={{0,4},{1,5},{2,6},{3,7},{4,0},{5,1},{6,2},{7,3},{8,12},{9,13},{10,... | collective-permute-start | bytes 196616 | tf_op jit(solution)/shard_map/ppermute | solution.py:23
  164.9 1.8 collective-permute-start.30
  166.6 1.7 collective-permute-start.26
  168.4 2.6 %collective-permute-done.30 = f32[128,128]{1,0:T(8,128)S(1)} collective-permute-done((f32[128,128]{1,0:T(8,128)S(1)}, f32[128,128]{1,0:T(8,128)S(1)}, u32[]{:S(2)}, u32[]{:S(2)}) %collective-permute-start.30) | collective-permute-done | bytes 65568 | tf_op jit(solution)/shard_map/ppermute | solution.py:23
  171.5 3.8 %collective-permute-done.31 = f32[1,128,128]{2,1,0:T(8,128)S(1)} collective-permute-done((f32[1,128,128]{2,1,0:T(8,128)S(1)}, f32[1,128,128]{2,1,0:T(8,128)S(1)}, u32[]{:S(2)}, u32[]{:S(2)}) %collective-permute-start.31) | collective-permute-done | bytes 65568 | tf_op jit(solution)/shard_map/ppermute | solution.py:23
  175.4 1.9 %collective-permute-done.32 = f32[2,4,128,128]{3,2,1,0:T(8,128)S(1)} collective-permute-done((f32[2,4,128,128]{3,2,1,0:T(8,128)S(1)}, f32[2,4,128,128]{3,2,1,0:T(8,128)S(1)}, u32[]{:S(2)}, u32[]{:S(2)}) %collective-permute-start.32) | collective-permute-done | bytes 524320 | tf_op jit(solution)/shard_map/ppermute | solution.py:23
  177.4 1.9 %assemble.1 = f32[4,256,256]{2,1,0:T(8,128)} custom-call(s32[1]{0:T(128)} %bitcast.own_ref, f32[4,4,128,128]{3,2,1,0:T(8,128)S(1)} %pad_maximum_fusion.parts_ref), custom_call_target="tpu_custom_call" | custom-call | tf_op jit(solution)/shard_map/assemble/pallas_call | solution.py:264
  (85 shorter events, 25.6 us)
Async XLA Ops:
  3.0 40.3 %collective-permute-start.3 = (f32[2048,256]{1,0:T(8,128)}, f32[2048,256]{1,0:T(8,128)S(1)}, u32[]{:S(2)}, u32[]{:S(2)}) collective-permute-start(f32[2048,256]{1,0:T(8,128)} %slice_bitcast_fusion.2), channel_id=1, source_target_pairs={{0,16},{1,17},{2,18},{3,19},{4,20},{5,21},{6,22},{7,23}} | collective-permute-start | bytes 6291464 | tf_op jit(solution)/shard_map/ppermute | solution.py:292
  10.1 39.1 %collective-permute-start = (f32[3,256,256]{2,1,0:T(8,128)}, f32[3,256,256]{2,1,0:T(8,128)}, u32[]{:S(2)}, u32[]{:S(2)}) collective-permute-start(f32[3,256,256]{2,1,0:T(8,128)} %slice.101), channel_id=1, source_target_pairs={{0,8},{8,16},{16,24},{1,9},{9,17},{17,25},{2,10},{10,18},{18,26},{... | collective-permute-start | bytes 2359304 | tf_op jit(solution)/shard_map/ppermute | solution.py:287
  34.4 41.7 %collective-permute-start.5 = (f32[2,1024,128]{2,1,0:T(8,128)}, f32[2,1024,128]{2,1,0:T(8,128)S(1)}, u32[]{:S(2)}, u32[]{:S(2)}) collective-permute-start(f32[2,1024,128]{2,1,0:T(8,128)} %get-tuple-element.33), channel_id=1, source_target_pairs={{0,8},{8,0},{16,24},{24,16},{1,9},{9,1},{17,25},{25,17},{2,10},{10... | collective-permute-start | bytes 3145736 | tf_op jit(solution)/shard_map/ppermute | solution.py:23
  38.9 81.7 %collective-permute-start.13 = (f32[2,2048,256]{2,1,0:T(8,128)}, f32[2,2048,256]{2,1,0:T(8,128)}, u32[]{:S(2)}, u32[]{:S(2)}) collective-permute-start(f32[2,2048,256]{2,1,0:T(8,128)} %slice.112), channel_id=1, source_target_pairs={{0,8},{1,9},{2,10},{3,11},{4,12},{5,13},{6,14},{7,15}} | collective-permute-start | bytes 12582920 | tf_op jit(solution)/shard_map/ppermute | solution.py:297
  46.5 59.1 %collective-permute-start.4 = (f32[2048,256]{1,0:T(8,128)}, f32[2048,256]{1,0:T(8,128)}, u32[]{:S(2)}, u32[]{:S(2)}) collective-permute-start(f32[2048,256]{1,0:T(8,128)} %broadcast_select_fusion.1), channel_id=1, source_target_pairs={{0,8},{16,24},{1,9},{17,25},{2,10},{18,26},{3,11},{19,27},{4,12},{... | collective-permute-start | bytes 6291464 | tf_op jit(solution)/shard_map/ppermute | solution.py:294
  75.6 26.1 %collective-permute-start.1 = (f32[2,1024,128]{2,1,0:T(8,128)}, f32[2,1024,128]{2,1,0:T(8,128)}, u32[]{:S(2)}, u32[]{:S(2)}) collective-permute-start(f32[2,1024,128]{2,1,0:T(8,128)} %get-tuple-element.31), channel_id=1, source_target_pairs={{0,8},{8,0},{16,24},{24,16},{1,9},{9,1},{17,25},{25,17},{2,10},{10... | collective-permute-start | bytes 3145736 | tf_op jit(solution)/shard_map/ppermute | solution.py:23
  75.7 27.6 %collective-permute-start.12 = (f32[2,1024,128]{2,1,0:T(8,128)}, f32[2,1024,128]{2,1,0:T(8,128)}, u32[]{:S(2)}, u32[]{:S(2)}) collective-permute-start(f32[2,1024,128]{2,1,0:T(8,128)} %get-tuple-element.38), channel_id=1, source_target_pairs={{0,8},{8,0},{16,24},{24,16},{1,9},{9,1},{17,25},{25,17},{2,10},{10... | collective-permute-start | bytes 3145736 | tf_op jit(solution)/shard_map/ppermute | solution.py:23
  76.4 14.0 %collective-permute-start.6 = (f32[1,1024,128]{2,1,0:T(8,128)S(1)}, f32[1,1024,128]{2,1,0:T(8,128)S(1)}, u32[]{:S(2)}, u32[]{:S(2)}) collective-permute-start(f32[1,1024,128]{2,1,0:T(8,128)S(1)} %get-tuple-element.55), channel_id=1, source_target_pairs={{0,16},{8,24},{16,0},{24,8},{1,17},{9,25},{17,1},{25,9},{2,18},{10... | collective-permute-start | bytes 1572872 | tf_op jit(solution)/shard_map/ppermute | solution.py:23
  90.4 7.5 %collective-permute-start.7 = (f32[4,128,128]{2,1,0:T(8,128)S(1)}, f32[4,128,128]{2,1,0:T(8,128)S(1)}, u32[]{:S(2)}, u32[]{:S(2)}) collective-permute-start(f32[4,128,128]{2,1,0:T(8,128)S(1)} %get-tuple-element.35), channel_id=1, source_target_pairs={{0,1},{1,0},{2,3},{3,2},{4,5},{5,4},{6,7},{7,6},{8,9},{9,8},{10,11... | collective-permute-start | bytes 786440 | tf_op jit(solution)/shard_map/ppermute | solution.py:23
  98.0 10.2 %collective-permute-start.10 = (f32[128,128]{1,0:T(8,128)S(1)}, f32[128,128]{1,0:T(8,128)S(1)}, u32[]{:S(2)}, u32[]{:S(2)}) collective-permute-start(f32[128,128]{1,0:T(8,128)S(1)} %get-tuple-element.70), channel_id=1, source_target_pairs={{0,6},{1,7},{2,4},{3,5},{4,2},{5,3},{6,0},{7,1},{8,14},{9,15},{10,... | collective-permute-start | bytes 196616 | tf_op jit(solution)/shard_map/ppermute | solution.py:23
  101.7 6.6 %collective-permute-start.8 = (f32[128,128]{1,0:T(8,128)S(1)}, f32[128,128]{1,0:T(8,128)S(1)}, u32[]{:S(2)}, u32[]{:S(2)}) collective-permute-start(f32[128,128]{1,0:T(8,128)S(1)} %get-tuple-element.72), channel_id=1, source_target_pairs={{0,2},{1,3},{2,0},{3,1},{4,6},{5,7},{6,4},{7,5},{8,10},{9,11},{10,... | collective-permute-start | bytes 196616 | tf_op jit(solution)/shard_map/ppermute | solution.py:23
  103.3 5.2 %collective-permute-start.9 = (f32[128,128]{1,0:T(8,128)S(1)}, f32[128,128]{1,0:T(8,128)S(1)}, u32[]{:S(2)}, u32[]{:S(2)}) collective-permute-start(f32[128,128]{1,0:T(8,128)S(1)} %get-tuple-element.71), channel_id=1, source_target_pairs={{0,4},{1,5},{2,6},{3,7},{4,0},{5,1},{6,2},{7,3},{8,12},{9,13},{10,... | collective-permute-start | bytes 196616 | tf_op jit(solution)/shard_map/ppermute | solution.py:23
  105.6 11.5 %collective-permute-start.2 = (f32[1,1024,128]{2,1,0:T(8,128)S(1)}, f32[1,1024,128]{2,1,0:T(8,128)S(1)}, u32[]{:S(2)}, u32[]{:S(2)}) collective-permute-start(f32[1,1024,128]{2,1,0:T(8,128)S(1)} %get-tuple-element.57), channel_id=1, source_target_pairs={{0,16},{8,24},{16,0},{24,8},{1,17},{9,25},{17,1},{25,9},{2,18},{10... | collective-permute-start | bytes 1572872 | tf_op jit(solution)/shard_map/ppermute | solution.py:23
  108.2 30.6 %collective-permute-start.20 = (f32[2,1024,128]{2,1,0:T(8,128)S(1)}, f32[2,1024,128]{2,1,0:T(8,128)S(1)}, u32[]{:S(2)}, u32[]{:S(2)}) collective-permute-start(f32[2,1024,128]{2,1,0:T(8,128)S(1)} %copy-done.4), channel_id=1, source_target_pairs={{0,8},{8,0},{16,24},{24,16},{1,9},{9,1},{17,25},{25,17},{2,10},{10... | collective-permute-start | bytes 3145736 | tf_op jit(solution)/shard_map/ppermute | solution.py:23
  118.1 7.4 %collective-permute-start.15 = (f32[4,128,128]{2,1,0:T(8,128)S(1)}, f32[4,128,128]{2,1,0:T(8,128)S(1)}, u32[]{:S(2)}, u32[]{:S(2)}) collective-permute-start(f32[4,128,128]{2,1,0:T(8,128)S(1)} %get-tuple-element.40), channel_id=1, source_target_pairs={{0,1},{1,0},{2,3},{3,2},{4,5},{5,4},{6,7},{7,6},{8,9},{9,8},{10,11... | collective-permute-start | bytes 786440 | tf_op jit(solution)/shard_map/ppermute | solution.py:23
  119.7 4.3 %collective-permute-start.11 = (f32[1,128,128]{2,1,0:T(8,128)S(1)}, f32[1,128,128]{2,1,0:T(8,128)S(1)}, u32[]{:S(2)}, u32[]{:S(2)}) collective-permute-start(f32[1,128,128]{2,1,0:T(8,128)S(1)} %bitcast.93), channel_id=1, source_target_pairs={{0,16},{8,24},{16,0},{24,8},{1,17},{9,25},{17,1},{25,9},{2,18},{10... | collective-permute-start | bytes 196616 | tf_op jit(solution)/shard_map/ppermute | solution.py:23
  125.4 11.3 %collective-permute-start.14 = (f32[1,1024,128]{2,1,0:T(8,128)S(1)}, f32[1,1024,128]{2,1,0:T(8,128)S(1)}, u32[]{:S(2)}, u32[]{:S(2)}) collective-permute-start(f32[1,1024,128]{2,1,0:T(8,128)S(1)} %get-tuple-element.53), channel_id=1, source_target_pairs={{0,16},{8,24},{16,0},{24,8},{1,17},{9,25},{17,1},{25,9},{2,18},{10... | collective-permute-start | bytes 1572872 | tf_op jit(solution)/shard_map/ppermute | solution.py:23
  125.6 4.5 %collective-permute-start.16 = (f32[128,128]{1,0:T(8,128)S(1)}, f32[128,128]{1,0:T(8,128)S(1)}, u32[]{:S(2)}, u32[]{:S(2)}) collective-permute-start(f32[128,128]{1,0:T(8,128)S(1)} %get-tuple-element.68), channel_id=1, source_target_pairs={{0,2},{1,3},{2,0},{3,1},{4,6},{5,7},{6,4},{7,5},{8,10},{9,11},{10,... | collective-permute-start | bytes 196616 | tf_op jit(solution)/shard_map/ppermute | solution.py:23
  127.1 6.2 %collective-permute-start.17 = (f32[128,128]{1,0:T(8,128)S(1)}, f32[128,128]{1,0:T(8,128)S(1)}, u32[]{:S(2)}, u32[]{:S(2)}) collective-permute-start(f32[128,128]{1,0:T(8,128)S(1)} %get-tuple-element.67), channel_id=1, source_target_pairs={{0,4},{1,5},{2,6},{3,7},{4,0},{5,1},{6,2},{7,3},{8,12},{9,13},{10,... | collective-permute-start | bytes 196616 | tf_op jit(solution)/shard_map/ppermute | solution.py:23
  129.7 6.1 %collective-permute-start.18 = (f32[128,128]{1,0:T(8,128)S(1)}, f32[128,128]{1,0:T(8,128)S(1)}, u32[]{:S(2)}, u32[]{:S(2)}) collective-permute-start(f32[128,128]{1,0:T(8,128)S(1)} %get-tuple-element.66), channel_id=1, source_target_pairs={{0,6},{1,7},{2,4},{3,5},{4,2},{5,3},{6,0},{7,1},{8,14},{9,15},{10,... | collective-permute-start | bytes 196616 | tf_op jit(solution)/shard_map/ppermute | solution.py:23
  137.7 4.3 %collective-permute-start.19 = (f32[1,128,128]{2,1,0:T(8,128)S(1)}, f32[1,128,128]{2,1,0:T(8,128)S(1)}, u32[]{:S(2)}, u32[]{:S(2)}) collective-permute-start(f32[1,128,128]{2,1,0:T(8,128)S(1)} %bitcast.95), channel_id=1, source_target_pairs={{0,16},{8,24},{16,0},{24,8},{1,17},{9,25},{17,1},{25,9},{2,18},{10... | collective-permute-start | bytes 196616 | tf_op jit(solution)/shard_map/ppermute | solution.py:23
  138.9 6.4 %collective-permute-start.22 = (f32[4,128,128]{2,1,0:T(8,128)S(1)}, f32[4,128,128]{2,1,0:T(8,128)S(1)}, u32[]{:S(2)}, u32[]{:S(2)}) collective-permute-start(f32[4,128,128]{2,1,0:T(8,128)S(1)} %get-tuple-element.45), channel_id=1, source_target_pairs={{0,1},{1,0},{2,3},{3,2},{4,5},{5,4},{6,7},{7,6},{8,9},{9,8},{10,11... | collective-permute-start | bytes 786440 | tf_op jit(solution)/shard_map/ppermute | solution.py:23
  144.2 10.5 %collective-permute-start.21 = (f32[1,1024,128]{2,1,0:T(8,128)S(1)}, f32[1,1024,128]{2,1,0:T(8,128)S(1)}, u32[]{:S(2)}, u32[]{:S(2)}) collective-permute-start(f32[1,1024,128]{2,1,0:T(8,128)S(1)} %get-tuple-element.51), channel_id=1, source_target_pairs={{0,16},{8,24},{16,0},{24,8},{1,17},{9,25},{17,1},{25,9},{2,18},{10... | collective-permute-start | bytes 1572872 | tf_op jit(solution)/shard_map/ppermute | solution.py:23
  145.4 4.5 %collective-permute-start.23 = (f32[128,128]{1,0:T(8,128)S(1)}, f32[128,128]{1,0:T(8,128)S(1)}, u32[]{:S(2)}, u32[]{:S(2)}) collective-permute-start(f32[128,128]{1,0:T(8,128)S(1)} %get-tuple-element.64), channel_id=1, source_target_pairs={{0,2},{1,3},{2,0},{3,1},{4,6},{5,7},{6,4},{7,5},{8,10},{9,11},{10,... | collective-permute-start | bytes 196616 | tf_op jit(solution)/shard_map/ppermute | solution.py:23
  146.3 5.2 %collective-permute-start.24 = (f32[128,128]{1,0:T(8,128)S(1)}, f32[128,128]{1,0:T(8,128)S(1)}, u32[]{:S(2)}, u32[]{:S(2)}) collective-permute-start(f32[128,128]{1,0:T(8,128)S(1)} %get-tuple-element.63), channel_id=1, source_target_pairs={{0,4},{1,5},{2,6},{3,7},{4,0},{5,1},{6,2},{7,3},{8,12},{9,13},{10,... | collective-permute-start | bytes 196616 | tf_op jit(solution)/shard_map/ppermute | solution.py:23
  148.7 6.1 %collective-permute-start.25 = (f32[128,128]{1,0:T(8,128)S(1)}, f32[128,128]{1,0:T(8,128)S(1)}, u32[]{:S(2)}, u32[]{:S(2)}) collective-permute-start(f32[128,128]{1,0:T(8,128)S(1)} %get-tuple-element.62), channel_id=1, source_target_pairs={{0,6},{1,7},{2,4},{3,5},{4,2},{5,3},{6,0},{7,1},{8,14},{9,15},{10,... | collective-permute-start | bytes 196616 | tf_op jit(solution)/shard_map/ppermute | solution.py:23
  155.7 6.4 %collective-permute-start.27 = (f32[4,128,128]{2,1,0:T(8,128)S(1)}, f32[4,128,128]{2,1,0:T(8,128)S(1)}, u32[]{:S(2)}, u32[]{:S(2)}) collective-permute-start(f32[4,128,128]{2,1,0:T(8,128)S(1)} %get-tuple-element.48), channel_id=1, source_target_pairs={{0,1},{1,0},{2,3},{3,2},{4,5},{5,4},{6,7},{7,6},{8,9},{9,8},{10,11... | collective-permute-start | bytes 786440 | tf_op jit(solution)/shard_map/ppermute | solution.py:23
  162.2 6.2 %collective-permute-start.28 = (f32[128,128]{1,0:T(8,128)S(1)}, f32[128,128]{1,0:T(8,128)S(1)}, u32[]{:S(2)}, u32[]{:S(2)}) collective-permute-start(f32[128,128]{1,0:T(8,128)S(1)} %get-tuple-element.59), channel_id=1, source_target_pairs={{0,2},{1,3},{2,0},{3,1},{4,6},{5,7},{6,4},{7,5},{8,10},{9,11},{10,... | collective-permute-start | bytes 196616 | tf_op jit(solution)/shard_map/ppermute | solution.py:23
  162.7 5.7 %collective-permute-start.29 = (f32[128,128]{1,0:T(8,128)S(1)}, f32[128,128]{1,0:T(8,128)S(1)}, u32[]{:S(2)}, u32[]{:S(2)}) collective-permute-start(f32[128,128]{1,0:T(8,128)S(1)} %get-tuple-element.61), channel_id=1, source_target_pairs={{0,4},{1,5},{2,6},{3,7},{4,0},{5,1},{6,2},{7,3},{8,12},{9,13},{10,... | collective-permute-start | bytes 196616 | tf_op jit(solution)/shard_map/ppermute | solution.py:23
  164.9 6.1 %collective-permute-start.30 = (f32[128,128]{1,0:T(8,128)S(1)}, f32[128,128]{1,0:T(8,128)S(1)}, u32[]{:S(2)}, u32[]{:S(2)}) collective-permute-start(f32[128,128]{1,0:T(8,128)S(1)} %get-tuple-element.60), channel_id=1, source_target_pairs={{0,6},{1,7},{2,4},{3,5},{4,2},{5,3},{6,0},{7,1},{8,14},{9,15},{10,... | collective-permute-start | bytes 196616 | tf_op jit(solution)/shard_map/ppermute | solution.py:23
  166.6 4.9 %collective-permute-start.26 = (f32[1,128,128]{2,1,0:T(8,128)S(1)}, f32[1,128,128]{2,1,0:T(8,128)S(1)}, u32[]{:S(2)}, u32[]{:S(2)}) collective-permute-start(f32[1,128,128]{2,1,0:T(8,128)S(1)} %bitcast.91), channel_id=1, source_target_pairs={{0,16},{8,24},{16,0},{24,8},{1,17},{9,25},{17,1},{25,9},{2,18},{10... | collective-permute-start | bytes 196616 | tf_op jit(solution)/shard_map/ppermute | solution.py:23
  171.0 4.3 %collective-permute-start.31 = (f32[1,128,128]{2,1,0:T(8,128)S(1)}, f32[1,128,128]{2,1,0:T(8,128)S(1)}, u32[]{:S(2)}, u32[]{:S(2)}) collective-permute-start(f32[1,128,128]{2,1,0:T(8,128)S(1)} %fusion.4), channel_id=1, source_target_pairs={{0,16},{8,24},{16,0},{24,8},{1,17},{9,25},{17,1},{25,9},{2,18},{10... | collective-permute-start | bytes 196616 | tf_op jit(solution)/shard_map/ppermute | solution.py:23
  (6 other events, 66.7 us)

commit v2 on v1

v2 whole, which is shorter than its diff:
```python
import functools

import jax
import jax.numpy as jnp
from jax import lax
from jax.experimental import pallas as pl
from jax.experimental.pallas import tpu as pltpu
from jax.sharding import PartitionSpec as P

LANES = 128
BF = jnp.bfloat16
F32 = jnp.float32
LIGHT = pl.CostEstimate(flops=1, bytes_accessed=1, transcendentals=0)
KINDS = tuple((outer, inner) for outer in (1, 2, 3) for inner in (1, 2, 3))
MEMBERS = {1: (1,), 2: (0, 1), 3: (0,)}


def swap_pairs(axis, bit):
    return [(i, i ^ bit) for i in range(lax.axis_size(axis))]


def exchanged(value, axis, bit):
    return lax.ppermute(value, axis, swap_pairs(axis, bit))


def bit_count(n):
    return n.bit_length() - 1


def reversed_bits(n):
    bits = bit_count(n)
    return [sum(((i >> b) & 1) << (bits - 1 - b) for b in range(bits)) for i in range(n)]


def split(v):
    hi = v.astype(BF)
    return hi, (v - hi.astype(F32)).astype(BF)


def dot(a, b):
    return jnp.dot(a, b, preferred_element_type=F32)


def flipped(v, own, slices):
    cols = v.shape[-1]
    width = cols // slices
    for b in range(bit_count(slices)):
        step = width << b
        swapped = jnp.concatenate(
            [v[:, (start ^ step) : (start ^ step) + step] for start in range(0, cols, step)], axis=1
        )
        v = jnp.where(((own >> b) & 1) == 1, swapped, v)
    return v


def folded(v):
    rows, width = v.shape
    parts = LANES // width
    step = rows // parts
    return jnp.concatenate([v[s * step : (s + 1) * step] for s in range(parts)], axis=1) if parts > 1 else v


def unfolded(v, width):
    parts = LANES // width
    return jnp.concatenate([v[:, s * width : (s + 1) * width] for s in range(parts)], axis=0) if parts > 1 else v


def source_sums(get, outer, inner, base):
    def along(inner_offset):
        if outer == 1:
            return get(base + 2 + inner_offset) - get(base + inner_offset)
        if outer == 2:
            return get(base + inner_offset)
        return get(base + inner_offset) - get(base - 2 + inner_offset)

    if inner == 1:
        return along(1) - along(0)
    if inner == 2:
        return along(0)
    return along(0) - along(-1)


def prepare_sources(kinds, get, own, slices, groups, hi_ref, lo_ref):
    block = hi_ref.shape[1] // groups
    for i, (outer, inner) in enumerate(kinds):
        for g in range(groups):
            hi, lo = split(flipped(source_sums(get, outer, inner, 4 * g), own, slices))
            hi_ref[i, g * block : (g + 1) * block, :] = hi
            lo_ref[i, g * block : (g + 1) * block, :] = lo


def write_folded(y, block, keep_ref, send_ref, slices):
    width = y.shape[1] // slices
    small = block * width // LANES
    half = slices // 2
    for b in range(y.shape[0] // block):
        rows = y[b * block : (b + 1) * block]
        for i, p in enumerate(reversed_bits(slices)):
            piece = folded(rows[:, p * width : (p + 1) * width])
            (send_ref if i // half else keep_ref)[i % half, b * small : (b + 1) * small, :] = piece


def slot(core, x_part, y_part, half):
    top, low = y_part // (half // 2), y_part % (half // 2)
    return jnp.where(core == 0, (x_part * 2 + top) * (half // 2) + low, (top * 2 + x_part) * (half // 2) + low)


def write_slots(y, block, own_ref, keep_ref, send_ref, slices):
    width = y.shape[1] // slices
    half = slices // 2
    core, side = own_ref[0] & 1, own_ref[1] & 1
    for b in range(y.shape[0] // block):
        rows = y[b * block : (b + 1) * block]
        for i, p in enumerate(reversed_bits(slices)):
            piece = folded(rows[:, p * width : (p + 1) * width])
            at = slot(core ^ (i // half), (b & 1) ^ side, i % half, half)
            (send_ref if i // half else keep_ref)[at, b // 2, :, :] = piece


def products(kinds, a_ref, hi_ref, lo_ref):
    groups = a_ref.shape[0]
    out = []
    for i, (outer, inner) in enumerate(kinds):
        his, los = [], []
        for g in range(groups):
            total = None
            for u in MEMBERS[outer]:
                for v in MEMBERS[inner]:
                    term = a_ref[g, u, v]
                    total = term if total is None else total + term
            hi, lo = split(total)
            his.append(hi)
            los.append(lo)
        hi, lo = jnp.concatenate(his, axis=1), jnp.concatenate(los, axis=1)
        out.append(dot(hi, hi_ref[i]) + dot(hi, lo_ref[i]) + dot(lo, hi_ref[i]))
    return out


def bulk_kernel(own_ref, history_ref, a_ref, *refs, slices, block):
    outs, (second_ref, third_ref, hi_ref, lo_ref) = refs[:-4], refs[-4:]

    @pl.when(pl.program_id(0) == 0)
    def _():
        def get(i):
            return history_ref[i] if i >= 0 else jnp.zeros(history_ref.shape[1:], F32)

        prepare_sources(KINDS, get, own_ref[0], slices, a_ref.shape[0], hi_ref, lo_ref)

    second_ref[...] = a_ref[0, 0, 1]
    third_ref[...] = a_ref[0, 1, 0]
    p11, p12, p13, p21, p22, p23, p31, p32, p33 = products(KINDS, a_ref, hi_ref, lo_ref)
    write_slots((p12 + p22) + (p11 + p21), block, own_ref, outs[0], outs[1], slices)
    times = ((p12 + p22) - (p13 + p23), (p21 + p22) - (p31 + p32), (p22 - p23) - (p32 - p33))
    for n, y in enumerate(times):
        write_folded(y, block, outs[2 * n + 2], outs[2 * n + 3], slices)


def carried_kernel(own_ref, tail_ref, keep_in, send_in, *refs, slices):
    matrices, (keep_ref, send_ref) = refs[:-2], refs[-2:]
    back, block = tail_ref.shape[:2]
    count = len(matrices)
    width = tail_ref.shape[2] // slices
    small = block * width // LANES
    half = slices // 2
    x = jnp.concatenate([flipped(tail_ref[back - count + j], own_ref[0], slices) for j in range(count)], axis=0)
    x_hi, x_lo = split(x)
    for c in range(matrices[0].shape[1] // block):
        m_hi, m_lo = split(jnp.concatenate([r[0, c * block : (c + 1) * block, :] for r in matrices], axis=1))
        y = dot(m_hi, x_hi) + dot(m_hi, x_lo) + dot(m_lo, x_hi)
        for i, p in enumerate(reversed_bits(slices)):
            at = (i % half, slice(c * small, (c + 1) * small))
            from_ref, to_ref = (send_in, send_ref) if i // half else (keep_in, keep_ref)
            to_ref[at] = from_ref[at] + folded(y[:, p * width : (p + 1) * width])


def with_carried(own, tail, keep, send, matrices, count, slices):
    lags, rows, block = matrices.shape
    return pl.pallas_call(
        functools.partial(carried_kernel, slices=slices),
        grid=(1,),
        in_specs=[smem()]
        + [pl.BlockSpec(v.shape, lambda i: (0, 0, 0)) for v in (tail, keep, send)]
        + [pl.BlockSpec((1, rows, block), lambda i, j=j: (j, 0, 0)) for j in range(count)],
        out_specs=[pl.BlockSpec(keep.shape, lambda i: (0, 0, 0))] * 2,
        out_shape=[jax.ShapeDtypeStruct(keep.shape, F32)] * 2,
        compiler_params=pltpu.CompilerParams(vmem_limit_bytes=40 << 20),
        cost_estimate=LIGHT,
        name="carried",
    )(own, tail, keep, send, *[matrices] * count)


def smem():
    return pl.BlockSpec(memory_space=pltpu.SMEM)


def bulk(own, history, matrices, steps, slices, tiles):
    lags, rows, block = matrices.shape
    cols = history.shape[2]
    groups = lags // 4
    tile = rows // tiles
    small = block * (cols // slices) // LANES
    pairs = rows // block // 2
    flat = jax.ShapeDtypeStruct((slices // 2, 2 * pairs * small, LANES), F32)
    flat_spec = pl.BlockSpec((slices // 2, 2 * pairs * small // tiles, LANES), lambda i: (0, i, 0))
    slots = jax.ShapeDtypeStruct((slices, pairs, small, LANES), F32)
    slots_spec = pl.BlockSpec((slices, pairs // tiles, small, LANES), lambda i: (0, i, 0, 0))
    return pl.pallas_call(
        functools.partial(bulk_kernel, slices=slices, block=block),
        grid=(tiles,),
        in_specs=[
            smem(),
            pl.BlockSpec(history.shape, lambda i: (0, 0, 0)),
            pl.BlockSpec((groups, 2, 2, tile, block), lambda i: (0, 0, 0, i, 0)),
        ],
        out_specs=[slots_spec] * 2 + [flat_spec] * (2 * steps - 2) + [pl.BlockSpec((tile, block), lambda i: (i, 0))] * 2,
        out_shape=[slots] * 2 + [flat] * (2 * steps - 2) + [jax.ShapeDtypeStruct((rows, block), F32)] * 2,
        scratch_shapes=[pltpu.VMEM((len(KINDS), groups * block, cols), BF)] * 2,
        compiler_params=pltpu.CompilerParams(vmem_limit_bytes=61 << 20),
        cost_estimate=pl.CostEstimate(
            flops=2 * 4 * len(KINDS) * groups * rows * block * cols,
            bytes_accessed=4 * matrices.size,
            transcendentals=0,
        ),
        name="bulk",
    )(own, history, matrices.reshape(groups, 2, 2, rows, block))


def stage_kernel(own_ref, a_ref, *refs):
    slabs, (newest_ref, tail_ref) = refs[:-2], refs[-2:]
    newest_ref[...] = a_ref[0]
    for i, slab in enumerate(slabs):
        tail_ref[i] = slab[0]


def staged(own, matrices, history, back):
    lags, rows, block = matrices.shape
    cols = history.shape[2]
    shapes = [(rows, block), (back, block, cols)]
    return pl.pallas_call(
        stage_kernel,
        grid=(1,),
        in_specs=[smem(), pl.BlockSpec((1, rows, block), lambda i: (0, 0, 0))]
        + [pl.BlockSpec((1, block, cols), lambda i, at=lags - back + k: (at, 0, 0)) for k in range(back)],
        out_specs=[pl.BlockSpec(s, lambda i, r=len(s): (0,) * r) for s in shapes],
        out_shape=[jax.ShapeDtypeStruct(s, F32) for s in shapes],
        compiler_params=pltpu.CompilerParams(vmem_limit_bytes=61 << 20),
        cost_estimate=LIGHT,
        name="stage",
    )(own, matrices, *[history] * back)


def merge_kernel(own_ref, a_ref, *out_refs):
    for d, out_ref in enumerate(out_refs):
        out_ref[...] = a_ref[(own_ref[1] >> 1) ^ d]


def chain_kernel(own_ref, e_ref, a_ref, b_ref, m_ref, got_ref, *refs, width):
    parts, (x_ref, keep_ref, send_ref) = refs[:-3], refs[-3:]
    core, own = own_ref[0] & 1, own_ref[1]
    total = parts[0][...]
    for part in parts[1:]:
        total = total + part[...]
    x = e_ref[...] - total
    x_ref[...] = x
    block = m_ref.shape[1]
    x_hi, x_lo = split(unfolded(x, width))
    x_both = jnp.concatenate([x_hi, x_lo], axis=1)
    for q in range(a_ref.shape[0]):
        c = own ^ q
        at = pl.ds(pl.multiple_of(c * block, block), block)
        m_hi, m_lo = split(jnp.where(core == 1, got_ref[at, :], m_ref[at, :]))
        both = dot(m_hi, x_both)
        y = both[:, :width] + both[:, width:] + dot(m_lo, x_hi)
        (send_ref if q % 2 else keep_ref)[q // 2] = folded(y) + (a_ref[c] + b_ref[c])


def late_kernel(own_ref, acc_ref, *refs, width):
    out_ref, terms = refs[-1], [refs[i : i + 3] for i in range(0, len(refs) - 1, 3)]
    half = acc_ref.shape[0]

    @pl.when(own_ref[0] >= 2)
    def _():
        out_ref[...] = acc_ref[...]

    @pl.when(own_ref[0] < 2)
    def _():
        rows, block = terms[0][0].shape
        small = block * width // LANES
        sources = [split(jnp.concatenate([unfolded(r[p], width) for p in range(half)], axis=1)) for _, _, r in terms]
        for c in range(rows // block):
            y = None
            at = slice(c * block, (c + 1) * block)
            for (mine_ref, got_ref, _), (x_hi, x_lo) in zip(terms, sources, strict=True):
                m_hi, m_lo = split(jnp.where((own_ref[0] & 1) == 1, got_ref[at], mine_ref[at]))
                term = dot(m_hi, x_hi) + dot(m_hi, x_lo) + dot(m_lo, x_hi)
                y = term if y is None else y + term
            for p in range(half):
                at = (p, slice(c * small, (c + 1) * small))
                out_ref[at] = acc_ref[at] + folded(y[:, p * width : (p + 1) * width])


def fields_kernel(own_ref, e_ref, out_ref, *, slices):
    width = e_ref.shape[2] // slices
    for n in range(e_ref.shape[0]):
        out_ref[n] = folded(flipped(e_ref[n], own_ref[0], slices)[:, :width])


def assemble_kernel(own_ref, parts_ref, *refs, slices):
    out_ref = refs[-1]
    width = out_ref.shape[2] // slices
    order = reversed_bits(slices)
    for n in range(out_ref.shape[0]):
        pieces = [None] * slices
        for i, p in enumerate(order):
            pieces[p] = unfolded(parts_ref[i, n], width)
        out_ref[n] = flipped(jnp.concatenate(pieces, axis=1), own_ref[0], slices)


def assembled(own, every, shape, begin, onto=()):
    owners, count, small, _ = every.shape
    steps, block, cols = shape
    return pl.pallas_call(
        functools.partial(assemble_kernel, slices=owners),
        grid=(1,),
        in_specs=[smem(), pl.BlockSpec(every.shape, lambda i: (0, 0, 0, 0))] + [pl.BlockSpec(memory_space=pl.ANY)] * len(onto),
        out_specs=pl.BlockSpec((count, block, cols), lambda i: (begin // count, 0, 0)),
        out_shape=jax.ShapeDtypeStruct(shape, F32),
        input_output_aliases={2: 0} if onto else {},
        compiler_params=pltpu.CompilerParams(vmem_limit_bytes=24 << 20),
        cost_estimate=LIGHT,
        name="assemble",
    )(own, every, *onto)


def whole_call(kernel, name, out_shapes, *args, scratch=()):
    vmem = pl.BlockSpec(memory_space=pltpu.VMEM)
    out = [jax.ShapeDtypeStruct(s, F32) for s in out_shapes]
    return pl.pallas_call(
        kernel,
        in_specs=[smem()] + [vmem] * (len(args) - 1),
        out_specs=[vmem] * len(out),
        out_shape=out,
        scratch_shapes=[pltpu.VMEM(s, F32) for s in scratch],
        compiler_params=pltpu.CompilerParams(vmem_limit_bytes=40 << 20),
        cost_estimate=LIGHT,
        name=name,
    )(*args)


def sealed(held, *names):
    names = names or tuple(held)
    held.update(zip(names, lax.optimization_barrier(tuple(held[k] for k in names)), strict=True))


def local(lag_matrices, history, excitation):
    owners, columns = lax.axis_size("lag"), lax.axis_size("col")
    owner, column = lax.axis_index("lag"), lax.axis_index("col")
    lags, rows, block = lag_matrices.shape
    steps, _, cols = excitation.shape
    width = cols // owners
    small = block * width // LANES
    bits = bit_count(owners)
    back = steps - 1
    own = jnp.stack([owner, column]).astype(jnp.int32)
    tiles = max(1, rows // 512)
    held = {}

    def stage_pairs(stage):
        def partner(i):
            lag, col = divmod(i, columns)
            if stage < 2:
                return lag * columns + (col ^ 1) if (lag & 1) == stage else (lag ^ 2) * columns + col
            return (lag ^ (1 << stage)) * columns + col

        return [(i, partner(i)) for i in range(owners * columns)]

    def offered(slots):
        return jnp.stack(slots[len(slots) // 2 :])

    def taken(slots, offer, stage):
        got = lax.ppermute(offer, ("lag", "col"), stage_pairs(stage))
        return [slots[i] + got[i] for i in range(len(slots) // 2)]

    def owners_sum(acc):
        for b in range(1, bits):
            half = acc.shape[0] // 2
            got = exchanged(acc[half:], "lag", 1 << b)
            if half == 1:
                return acc[0], got[0]
            acc = acc[:half] + got
        return acc[0], jnp.zeros_like(acc[0])

    def scattered(acc, bit):
        while len(acc) > 4:
            got = exchanged(jnp.stack(acc[1::2]), "col", bit)
            acc = [a + got[i] for i, a in enumerate(acc[0::2])]
            bit *= 2
        return [acc[0]] + [exchanged(acc[d], "col", d * bit) for d in range(1, len(acc))]

    def gathered(x):
        for b in reversed(range(1, bits)):
            x = jnp.concatenate([x, exchanged(x, "lag", 1 << b)], axis=0)
        return x

    def partner_sum(n):
        return held[f"keep{n}"] + exchanged(held[f"send{n}"], "lag", 1)

    def with_tail(n):
        pair = with_carried(own, held["carried"], held[f"keep{n}"], held[f"send{n}"], lag_matrices, n, owners)
        held[f"keep{n}"], held[f"send{n}"] = pair

    newest, tail = staged(own, lag_matrices, history, back)
    top = 1 << (bits - 1)
    held["newest"], held["got"] = newest, lax.ppermute(newest, "lag", [(0, top)])
    held["carried"] = lax.ppermute(tail, "lag", [(i, i + 1) for i in range(owners - 1)])
    partials = bulk(lax.optimization_barrier((own, tail))[0], history, lag_matrices, steps, owners, tiles)
    for n in range(steps):
        held[f"keep{n}"], held[f"send{n}"] = partials[2 * n : 2 * n + 2]
    held["lag2"], held["lag3"] = partials[-2:]
    sealed(held, "send0", "got", "carried")

    got = exchanged(held["send0"], "lag", 1)
    slots = [held["keep0"][i] + got[i] for i in range(owners)]
    held["offer"] = offered(slots)
    sealed(held, "offer", "keep1", "newest")
    slots = taken(slots, held["offer"], 0)
    with_tail(1)
    held["field"] = whole_call(functools.partial(fields_kernel, slices=owners), "fields", [(steps, small, LANES)], own, excitation)[0]
    newest = jnp.where((owner & top) != 0, held["got"], held["newest"])
    for b in reversed(range(1, bits - 1)):
        got = lax.ppermute(newest, "lag", [(i, i + (1 << b)) for i in range(0, owners, 2 << b)])
        newest = jnp.where((owner >> b) & 1 == 1, got, newest)
    held["newest"] = newest
    held["offer"] = offered(slots)
    sealed(held, "offer", "keep1", "send1", "field", "keep2", "newest")
    held["odd"] = lax.ppermute(held["newest"], "lag", [(i, i + 1) for i in range(0, owners, 2)])
    slots = taken(slots, held["offer"], 1)
    for b in range(2, bits):
        slots = taken(slots, offered(slots), b)
    with_tail(2)
    held["past1"] = partner_sum(1)
    held["acc0"] = slots[0]
    sealed(held, "acc0", "keep2", "send2", "past1", "keep3", "odd")
    acc = whole_call(merge_kernel, "merge", [(small, LANES)] * (columns // 2), own, held["acc0"])
    parts = scattered(acc, 2)
    held["mine1"], held["got1"] = owners_sum(held["past1"])
    with_tail(3)
    held["past2"] = partner_sum(2)
    held.update((f"part{i}", part) for i, part in enumerate(parts))
    sealed(held, "keep3", "send3", "past2", "lag2", "mine1", "got1", *(f"part{i}" for i in range(len(parts))))
    a, b = held["mine1"], held["got1"]
    parts = [held[f"part{i}"] for i in range(len(parts))]
    held["past3"] = partner_sum(3)

    shaped = (columns, small, LANES)
    halves = [(columns // 2, small, LANES)] * 2
    shown = []
    for n in range(1, steps):
        x, keep, send = whole_call(
            functools.partial(chain_kernel, width=width), "chain", [(small, LANES), *halves],
            own, held["field"][n - 1], a.reshape(shaped), b.reshape(shaped), held["newest"], held["odd"], *parts,
        )
        shown.append(gathered(x[None]))
        if n + 1 < steps:
            own_lag = lax.optimization_barrier((held[f"lag{n + 1}"], x))[0]
            held[f"odd{n + 1}"] = lax.ppermute(own_lag, "lag", [(0, 1)])
            terms = [v for k in range(2, n + 2) for v in (held[f"lag{k}"], held[f"odd{k}"], shown[n + 1 - k])]
            past = whole_call(
                functools.partial(late_kernel, width=width), "late", [held[f"past{n + 1}"].shape],
                own, held[f"past{n + 1}"], *terms,
            )[0]
            a, b = owners_sum(past)
        acc = keep + exchanged(send, "col", 1)
        parts = scattered([acc[i] for i in range(columns // 2)], 2)
    early = jnp.stack(shown, axis=1)
    early = jnp.concatenate([early, exchanged(early, "lag", 1)], axis=0)
    held["dens"] = assembled(own, early, excitation.shape, 0)
    held.update((f"part{i}", part) for i, part in enumerate(parts))
    sealed(held, "dens", *(f"part{i}" for i in range(len(parts))))
    x = held["field"][steps - 1] - functools.reduce(jnp.add, [held[f"part{i}"] for i in range(len(parts))])
    newest = gathered(x[None])
    newest = jnp.concatenate([newest, exchanged(newest, "lag", 1)], axis=0)
    return assembled(own, newest[:, None], excitation.shape, steps - 1, [held["dens"]])


def solution(mesh):
    return jax.shard_map(
        local,
        mesh=mesh,
        in_specs=(P("lag", None, "col"), P("lag", "col", None), P(None, "col", None)),
        out_specs=P(None, "col", None),
        check_vma=False,
    )
```

time: 180 us -> 169 us (0.939)
  Pallas kernels: 57.4 us -> 72.5 us
  local copies, waits for them, and re-layouts: 10.2 us -> 1.72 us
  waiting for transfers between devices: 57.7 us -> 50 us
  other arithmetic: 11.3 us -> 4.83 us
  starting transfers between devices: 42.4 us -> 38.6 us
    ppermute x29 -> x28, waiting for transfers between devices: 57.7 us -> 43.6 us  [exchanged(): return lax.ppermute(value, axis, swap_pairs(axis, bit))]
    pallas_call x2 -> x7, Pallas kernels: 48.5 us -> 61.6 us  [the longest x1 41.4 us: bulk(): pl.pallas_call(functools.partial(bulk_kernel, slices=slices, block=block)...]
    select_n x3 -> x1, other arithmetic: 7.76 us -> 0.28 us  [local(): newest = jnp.where(owner & top != 0, held['got'], held['newest'])]
    slice x6 -> x3, local copies, waits for them, and re-layouts: 6.8 us -> 0.21 us  [owners_sum(): got = exchanged(acc[half:], 'lag', 1 << b)]
    ppermute x4 -> x7, waiting for transfers between devices: 0.01 us -> 6.37 us  [the longest x2 6.36 us: taken(): got = lax.ppermute(offer, ('lag', 'col'), stage_pairs(stage))]
    ppermute x29 -> x28, starting transfers between devices: 28.1 us -> 24.6 us  [exchanged(): return lax.ppermute(value, axis, swap_pairs(axis, bit))]
    squeeze x7 -> x4, local copies, waits for them, and re-layouts: 3.4 us -> 0.07 us  [the longest x3 0.06 us: local(): parts = scattered([acc[i] for i in range(columns // 2)], 2)]
    pallas_call x8 -> x7, Pallas kernels: 8.91 us -> 10.9 us  [whole_call(): pl.pallas_call(kernel, in_specs=[smem()] + [vmem] * (len(args) - 1), out_...]
  transfers between devices with their start and end apart: 33 -> 35, of which waited for: 16 -> 20; matrix products, arithmetic and copies ran while one was open for 10% -> 1% of each run, Pallas kernels for 30% -> 37%
where the time goes in v2:
time: 169 us; the launch traced here: 168 us
  Pallas kernels  72.5 us (43%)
  waiting for transfers between devices  50 us (30%)
  starting transfers between devices  38.6 us (23%)
  other arithmetic  4.83 us (3%)
  local copies, waits for them, and re-layouts  1.72 us (1%)
    ppermute x28, waiting for transfers between devices, exchanged(): return lax.ppermute(value, axis, swap_pairs(axis, bit))  43.6 us
    pallas_call x1, Pallas kernels, bulk(): pl.pallas_call(functools.partial(bulk_kernel, slices=slices, block=block)...  41.4 us
    ppermute x28, starting transfers between devices, exchanged(): return lax.ppermute(value, axis, swap_pairs(axis, bit))  24.6 us
    pallas_call x3, Pallas kernels, with_carried(): pl.pallas_call(functools.partial(carried_kernel, slices=slices), grid=(1,...  13.1 us
    pallas_call x7, Pallas kernels, whole_call(): pl.pallas_call(kernel, in_specs=[smem()] + [vmem] * (len(args) - 1), out_...  10.9 us
    ppermute x2, waiting for transfers between devices, taken(): got = lax.ppermute(offer, ('lag', 'col'), stage_pairs(stage))  6.36 us
    ppermute x1, starting transfers between devices, local(): lax.ppermute(newest, 'lag', [(0, top)])  6.23 us
    pallas_call x2, Pallas kernels, assembled(): pl.pallas_call(functools.partial(assemble_kernel, slices=owners), grid=(1...  3.68 us
  transfers between devices with their start and end apart: 35, of which 20 were waited for; matrix products, arithmetic and copies ran while one was open for 1% of the time, Pallas kernels for 37%

profile of v2, /device:TPU:0, one launch (start us, length us, event | category | flops | bytes accessed | tf_op | source)
XLA Modules:
  0.0 168.3 jit_solution(4082108888084337231)
XLA Ops:
  0.6 3.5 %stage.1 = (f32[2048,256]{1,0:T(8,128)}, f32[3,256,256]{2,1,0:T(8,128)}) custom-call(s32[2]{0:T(128)} %pad_add_fusion.own_ref, f32[16,2048,256]{2,1,0:T(8,128)} %refs_2_.3, f32[16,256,256]{2,1,0:T(8,128)} %history_ref.1, f32[16,256,256]{2,1,0:T(8,128)} %history_ref.1, f32[16,256,256]{2,1,0:T(8,128)} %history_ref.1), custom_call_target="tpu_custom_call" | custom-call | flops 1 | bytes 1 | tf_op jit(solution)/shard_map/stage/pallas_call | solution.py:239
  4.1 6.2 %collective-permute-start = (f32[2048,256]{1,0:T(8,128)}, f32[2048,256]{1,0:T(8,128)}, u32[]{:S(2)}, u32[]{:S(2)}) collective-permute-start(f32[2048,256]{1,0:T(8,128)} %get-tuple-element.87), channel_id=1, source_target_pairs={{0,16},{1,17},{2,18},{3,19},{4,20},{5,21},{6,22},{7,23}} | collective-permute-start | bytes 6291464 | tf_op jit(solution)/shard_map/ppermute | solution.py:414
  11.7 41.4 %bulk.1 = (f32[4,4,128,128]{3,2,1,0:T(8,128)}, f32[4,4,128,128]{3,2,1,0:T(8,128)}, f32[2,1024,128]{2,1,0:T(8,128)}, f32[2,1024,128]{2,1,0:T(8,128)}, f32[2,1024,...) custom-call(s32[2]{0:T(128)} %pad_add_fusion.own_ref, ...), custom_call_target="tpu_custom_call" | custom-call | flops 38654705664 | bytes 33554432 | tf_op jit(solution)/shard_map/bulk/pallas_call | solution.py:207
  59.0 3.0 %carried.3 = (f32[2,1024,128]{2,1,0:T(8,128)S(1)}, f32[2,1024,128]{2,1,0:T(8,128)S(1)}) custom-call(s32[2]{0:T(128)S(1)} %copy-done.9, f32[3,256,256]{2,1,0:T(8,128)S(1)} %collective-permute-done.1.tail_ref, f32[2,1024,128]{2,1,0:T(8,128)S(1)} %copy-done.4, f32[2,1024,128]{2,1,0:T(8,128)S(1)} %copy-done.5, f32[16,2048,256]{2,1,0:T(8,128)} %refs_2_.3), custom_call_target="tpu_custom_call" | custom-call | flops 1 | bytes 1 | tf_op jit(solution)/shard_map/carried/pallas_call | solution.py:178
  62.3 4.4 %collective-permute-done.3 = f32[2,4,128,128]{3,2,1,0:T(8,128)S(1)} collective-permute-done((f32[2,4,128,128]{3,2,1,0:T(8,128)S(1)}, f32[2,4,128,128]{3,2,1,0:T(8,128)S(1)}, u32[]{:S(2)}, u32[]{:S(2)}) %collective-permute-start.3) | collective-permute-done | bytes 524320 | tf_op jit(solution)/shard_map/ppermute | solution.py:381
  69.3 4.3 %carried.4 = (f32[2,1024,128]{2,1,0:T(8,128)S(1)}, f32[2,1024,128]{2,1,0:T(8,128)S(1)}) custom-call(s32[2]{0:T(128)S(1)} %copy-done.9, f32[3,256,256]{2,1,0:T(8,128)S(1)} %collective-permute-done.1.tail_ref, f32[2,1024,128]{2,1,0:T(8,128)S(1)} %copy-done.7, f32[2,1024,128]{2,1,0:T(8,128)S(1)} %copy-done.8, f32[16,2048,256]{2,1,0:T(8,128)} %refs_2_.3, ...), custom_call_target="tpu_custom_call" | custom-call | flops 1 | bytes 1 | tf_op jit(solution)/shard_map/carried/pallas_call | solution.py:178
  73.6 2.0 %collective-permute-done.4 = f32[1,4,128,128]{3,2,1,0:T(8,128)S(1)} collective-permute-done((f32[1,4,128,128]{3,2,1,0:T(8,128)S(1)}, f32[1,4,128,128]{3,2,1,0:T(8,128)S(1)}, u32[]{:S(2)}, u32[]{:S(2)}) %collective-permute-start.4) | collective-permute-done | bytes 262176 | tf_op jit(solution)/shard_map/ppermute | solution.py:381
  77.6 2.6 %collective-permute-start.10 = (f32[128,128]{1,0:T(8,128)S(1)}, f32[128,128]{1,0:T(8,128)S(1)}, u32[]{:S(2)}, u32[]{:S(2)}) collective-permute-start(f32[128,128]{1,0:T(8,128)S(1)} %get-tuple-element.109), channel_id=1, source_target_pairs={{0,4},{1,5},{2,6},{3,7},{4,0},{5,1},{6,2},{7,3},{8,12},{9,13},{10,... | collective-permute-start | bytes 196616 | tf_op jit(solution)/shard_map/ppermute | solution.py:23
  81.9 5.8 %carried.5 = (f32[2,1024,128]{2,1,0:T(8,128)S(1)}, f32[2,1024,128]{2,1,0:T(8,128)S(1)}) custom-call(s32[2]{0:T(128)S(1)} %copy-done.9, f32[3,256,256]{2,1,0:T(8,128)S(1)} %collective-permute-done.1.tail_ref, f32[2,1024,128]{2,1,0:T(8,128)S(1)} %copy-done.2, f32[2,1024,128]{2,1,0:T(8,128)S(1)} %copy-done.3, f32[16,2048,256]{2,1,0:T(8,128)} %refs_2_.3, ...), custom_call_target="tpu_custom_call" | custom-call | flops 1 | bytes 1 | tf_op jit(solution)/shard_map/carried/pallas_call | solution.py:178
  87.9 3.5 %collective-permute-done.8 = f32[1,1024,128]{2,1,0:T(8,128)S(1)} collective-permute-done((f32[1,1024,128]{2,1,0:T(8,128)S(1)}, f32[1,1024,128]{2,1,0:T(8,128)S(1)}, u32[]{:S(2)}, u32[]{:S(2)}) %collective-permute-start.8) | collective-permute-done | bytes 524320 | tf_op jit(solution)/shard_map/ppermute | solution.py:23
  93.0 1.7 %collective-permute-start.13 = (f32[2048,256]{1,0:T(8,128)S(1)}, f32[2048,256]{1,0:T(8,128)S(1)}, u32[]{:S(2)}, u32[]{:S(2)}) collective-permute-start(f32[2048,256]{1,0:T(8,128)S(1)} %copy-done), channel_id=1, source_target_pairs={{0,8},{1,9},{2,10},{3,11},{4,12},{5,13},{6,14},{7,15}} | collective-permute-start | bytes 6291464 | tf_op jit(solution)/shard_map/ppermute | solution.py:466
  96.3 2.7 %collective-permute-done.12 = f32[1,128,128]{2,1,0:T(8,128)S(1)} collective-permute-done((f32[1,128,128]{2,1,0:T(8,128)S(1)}, f32[1,128,128]{2,1,0:T(8,128)S(1)}, u32[]{:S(2)}, u32[]{:S(2)}) %collective-permute-start.12) | collective-permute-done | bytes 65568 | tf_op jit(solution)/shard_map/ppermute | solution.py:23
  99.1 1.8 %late.2 = f32[2,1024,128]{2,1,0:T(8,128)S(1)} custom-call(s32[2]{0:T(128)S(1)} %copy-done.9, f32[2,1024,128]{2,1,0:T(8,128)S(1)} %add.66.acc_ref, f32[2048,256]{1,0:T(8,128)S(1)} %copy-done, f32[2048,256]{1,0:T(8,128)S(1)} %collective-permute-done.13.refs_1_, f32[2,128,128]{2,1,0:T(8,128)S(1)} %get-tuple-element.163.refs_2_.refs_5_), custom_call_target="tpu_custom_call" | custom-call | flops 1 | bytes 1 | tf_op jit(solution)/shard_map/late/pallas_call | solution.py:338
  102.4 1.6 collective-permute-start.16
  104.0 2.6 %collective-permute-start.17 = (f32[128,128]{1,0:T(8,128)S(1)}, f32[128,128]{1,0:T(8,128)S(1)}, u32[]{:S(2)}, u32[]{:S(2)}) collective-permute-start(f32[128,128]{1,0:T(8,128)S(1)} %get-tuple-element.156), channel_id=1, source_target_pairs={{0,4},{1,5},{2,6},{3,7},{4,0},{5,1},{6,2},{7,3},{8,12},{9,13},{10,... | collective-permute-start | bytes 196616 | tf_op jit(solution)/shard_map/ppermute | solution.py:23
  107.0 3.6 %collective-permute-done.17.refs_2_ = f32[128,128]{1,0:T(8,128)S(1)} collective-permute-done((f32[128,128]{1,0:T(8,128)S(1)}, f32[128,128]{1,0:T(8,128)S(1)}, u32[]{:S(2)}, u32[]{:S(2)}) %collective-permute-start.17) | collective-permute-done | bytes 65568 | tf_op jit(solution)/shard_map/ppermute | solution.py:23
  110.6 2.1 %collective-permute-done.18.refs_3_ = f32[128,128]{1,0:T(8,128)S(1)} collective-permute-done((f32[128,128]{1,0:T(8,128)S(1)}, f32[128,128]{1,0:T(8,128)S(1)}, u32[]{:S(2)}, u32[]{:S(2)}) %collective-permute-start.18) | collective-permute-done | bytes 65568 | tf_op jit(solution)/shard_map/ppermute | solution.py:23
  112.7 1.8 %collective-permute-done.14 = f32[1,1024,128]{2,1,0:T(8,128)S(1)} collective-permute-done((f32[1,1024,128]{2,1,0:T(8,128)S(1)}, f32[1,1024,128]{2,1,0:T(8,128)S(1)}, u32[]{:S(2)}, u32[]{:S(2)}) %collective-permute-start.14) | collective-permute-done | bytes 524320 | tf_op jit(solution)/shard_map/ppermute | solution.py:23
  117.9 4.8 %collective-permute-done.20 = f32[2,1024,128]{2,1,0:T(8,128)S(1)} collective-permute-done((f32[2,1024,128]{2,1,0:T(8,128)S(1)}, f32[2,1024,128]{2,1,0:T(8,128)S(1)}, u32[]{:S(2)}, u32[]{:S(2)}) %collective-permute-start.20) | collective-permute-done | bytes 1048608 | tf_op jit(solution)/shard_map/ppermute | solution.py:23
  124.4 2.7 %late.3 = f32[2,1024,128]{2,1,0:T(8,128)S(1)} custom-call(s32[2]{0:T(128)S(1)} %copy-done.9, f32[2,1024,128]{2,1,0:T(8,128)S(1)} %add.68.acc_ref, f32[2048,256]{1,0:T(8,128)S(1)} %copy-done, f32[2048,256]{1,0:T(8,128)S(1)} %collective-permute-done.13.refs_1_, f32[2,128,128]{2,1,0:T(8,128)S(1)} %get-tuple-element.165.refs_2_, f32[2048,256]{1,0:T(8,128)S(1)} %copy-done.1, ...), custom_call_target="tpu_custom_call" | custom-call | flops 1 | bytes 1 | tf_op jit(solution)/shard_map/late/pallas_call | solution.py:338
  127.3 4.1 %collective-permute-done.23 = f32[4,128,128]{2,1,0:T(8,128)S(1)} collective-permute-done((f32[4,128,128]{2,1,0:T(8,128)S(1)}, f32[4,128,128]{2,1,0:T(8,128)S(1)}, u32[]{:S(2)}, u32[]{:S(2)}) %collective-permute-start.23) | collective-permute-done | bytes 262176 | tf_op jit(solution)/shard_map/ppermute | solution.py:23
  131.5 1.6 collective-permute-start.24
  133.1 2.6 %collective-permute-start.25 = (f32[128,128]{1,0:T(8,128)S(1)}, f32[128,128]{1,0:T(8,128)S(1)}, u32[]{:S(2)}, u32[]{:S(2)}) collective-permute-start(f32[128,128]{1,0:T(8,128)S(1)} %get-tuple-element.152), channel_id=1, source_target_pairs={{0,4},{1,5},{2,6},{3,7},{4,0},{5,1},{6,2},{7,3},{8,12},{9,13},{10,... | collective-permute-start | bytes 196616 | tf_op jit(solution)/shard_map/ppermute | solution.py:23
  135.9 4.2 %collective-permute-done.25.refs_2_ = f32[128,128]{1,0:T(8,128)S(1)} collective-permute-done((f32[128,128]{1,0:T(8,128)S(1)}, f32[128,128]{1,0:T(8,128)S(1)}, u32[]{:S(2)}, u32[]{:S(2)}) %collective-permute-start.25) | collective-permute-done | bytes 65568 | tf_op jit(solution)/shard_map/ppermute | solution.py:23
  140.1 1.7 collective-permute-done.26.refs_3_
  145.0 2.7 %collective-permute-done.27 = f32[1,128,128]{2,1,0:T(8,128)S(1)} collective-permute-done((f32[1,128,128]{2,1,0:T(8,128)S(1)}, f32[1,128,128]{2,1,0:T(8,128)S(1)}, u32[]{:S(2)}, u32[]{:S(2)}) %collective-permute-start.27) | collective-permute-done | bytes 65568 | tf_op jit(solution)/shard_map/ppermute | solution.py:23
  147.8 2.8 %collective-permute-done.29 = f32[4,128,128]{2,1,0:T(8,128)S(1)} collective-permute-done((f32[4,128,128]{2,1,0:T(8,128)S(1)}, f32[4,128,128]{2,1,0:T(8,128)S(1)}, u32[]{:S(2)}, u32[]{:S(2)}) %collective-permute-start.29) | collective-permute-done | bytes 262176 | tf_op jit(solution)/shard_map/ppermute | solution.py:23
  150.7 1.6 collective-permute-start.30
  152.3 2.6 %collective-permute-start.31 = (f32[128,128]{1,0:T(8,128)S(1)}, f32[128,128]{1,0:T(8,128)S(1)}, u32[]{:S(2)}, u32[]{:S(2)}) collective-permute-start(f32[128,128]{1,0:T(8,128)S(1)} %get-tuple-element.148), channel_id=1, source_target_pairs={{0,4},{1,5},{2,6},{3,7},{4,0},{5,1},{6,2},{7,3},{8,12},{9,13},{10,... | collective-permute-start | bytes 196616 | tf_op jit(solution)/shard_map/ppermute | solution.py:23
  155.2 2.1 %assemble.2.refs_0_ = f32[4,256,256]{2,1,0:T(8,128)} custom-call(s32[2]{0:T(128)S(1)} %copy-done.9, f32[4,3,128,128]{3,2,1,0:T(8,128)S(1)} %pad_maximum_fusion.parts_ref), custom_call_target="tpu_custom_call" | custom-call | flops 1 | bytes 1 | tf_op jit(solution)/shard_map/assemble/pallas_call | solution.py:322
  158.9 2.1 %collective-permute-done.32 = f32[128,128]{1,0:T(8,128)S(1)} collective-permute-done((f32[128,128]{1,0:T(8,128)S(1)}, f32[128,128]{1,0:T(8,128)S(1)}, u32[]{:S(2)}, u32[]{:S(2)}) %collective-permute-start.32) | collective-permute-done | bytes 65568 | tf_op jit(solution)/shard_map/ppermute | solution.py:23
  162.5 2.8 %collective-permute-done.33 = f32[1,128,128]{2,1,0:T(8,128)S(1)} collective-permute-done((f32[1,128,128]{2,1,0:T(8,128)S(1)}, f32[1,128,128]{2,1,0:T(8,128)S(1)}, u32[]{:S(2)}, u32[]{:S(2)}) %collective-permute-start.33) | collective-permute-done | bytes 65568 | tf_op jit(solution)/shard_map/ppermute | solution.py:23
  (103 shorter events, 34.6 us)
Async XLA Ops:
  4.1 49.0 %collective-permute-start = (f32[2048,256]{1,0:T(8,128)}, f32[2048,256]{1,0:T(8,128)}, u32[]{:S(2)}, u32[]{:S(2)}) collective-permute-start(f32[2048,256]{1,0:T(8,128)} %get-tuple-element.87), channel_id=1, source_target_pairs={{0,16},{1,17},{2,18},{3,19},{4,20},{5,21},{6,22},{7,23}} | collective-permute-start | bytes 6291464 | tf_op jit(solution)/shard_map/ppermute | solution.py:414
  10.3 42.8 %collective-permute-start.1 = (f32[3,256,256]{2,1,0:T(8,128)}, f32[3,256,256]{2,1,0:T(8,128)S(1)}, u32[]{:S(2)}, u32[]{:S(2)}) collective-permute-start(f32[3,256,256]{2,1,0:T(8,128)} %get-tuple-element.72), channel_id=1, source_target_pairs={{0,8},{8,16},{16,24},{1,9},{9,17},{17,25},{2,10},{10,18},{18,26},{... | collective-permute-start | bytes 2359304 | tf_op jit(solution)/shard_map/ppermute | solution.py:415
  57.4 9.2 %collective-permute-start.3 = (f32[2,4,128,128]{3,2,1,0:T(8,128)S(1)}, f32[2,4,128,128]{3,2,1,0:T(8,128)S(1)}, u32[]{:S(2)}, u32[]{:S(2)}) collective-permute-start(f32[2,4,128,128]{3,2,1,0:T(8,128)S(1)} %pad_maximum_fusion.1), channel_id=1, source_target_pairs={{0,1},{1,0},{2,3},{3,2},{4,5},{5,4},{6,7},{7,6},{8,24},{9,25},{10,... | collective-permute-start | bytes 1572872 | tf_op jit(solution)/shard_map/ppermute | solution.py:381
  67.7 9.1 %collective-permute-start.6 = (f32[2048,256]{1,0:T(8,128)S(1)}, f32[2048,256]{1,0:T(8,128)S(1)}, u32[]{:S(2)}, u32[]{:S(2)}) collective-permute-start(f32[2048,256]{1,0:T(8,128)S(1)} %broadcast_select_fusion.m_ref), channel_id=1, source_target_pairs={{0,8},{16,24},{1,9},{17,25},{2,10},{18,26},{3,11},{19,27},{4,12},{... | collective-permute-start | bytes 6291464 | tf_op jit(solution)/shard_map/ppermute | solution.py:436
  69.1 7.5 %collective-permute-start.5 = (f32[2,1024,128]{2,1,0:T(8,128)S(1)}, f32[2,1024,128]{2,1,0:T(8,128)S(1)}, u32[]{:S(2)}, u32[]{:S(2)}) collective-permute-start(f32[2,1024,128]{2,1,0:T(8,128)S(1)} %get-tuple-element.95), channel_id=1, source_target_pairs={{0,8},{8,0},{16,24},{24,16},{1,9},{9,1},{17,25},{25,17},{2,10},{10... | collective-permute-start | bytes 3145736 | tf_op jit(solution)/shard_map/ppermute | solution.py:23
  69.2 6.4 %collective-permute-start.4 = (f32[1,4,128,128]{3,2,1,0:T(8,128)S(1)}, f32[1,4,128,128]{3,2,1,0:T(8,128)S(1)}, u32[]{:S(2)}, u32[]{:S(2)}) collective-permute-start(f32[1,4,128,128]{3,2,1,0:T(8,128)S(1)} %slice_add_fusion.2), channel_id=1, source_target_pairs={{0,16},{1,17},{2,18},{3,19},{4,20},{5,21},{6,22},{7,23},{8,9},{9,8... | collective-permute-start | bytes 786440 | tf_op jit(solution)/shard_map/ppermute | solution.py:381
  76.8 10.9 %collective-permute-start.7 = (f32[2,1024,128]{2,1,0:T(8,128)S(1)}, f32[2,1024,128]{2,1,0:T(8,128)S(1)}, u32[]{:S(2)}, u32[]{:S(2)}) collective-permute-start(f32[2,1024,128]{2,1,0:T(8,128)S(1)} %get-tuple-element.103), channel_id=1, source_target_pairs={{0,8},{8,0},{16,24},{24,16},{1,9},{9,1},{17,25},{25,17},{2,10},{10... | collective-permute-start | bytes 3145736 | tf_op jit(solution)/shard_map/ppermute | solution.py:23
  77.0 14.4 %collective-permute-start.8 = (f32[1,1024,128]{2,1,0:T(8,128)S(1)}, f32[1,1024,128]{2,1,0:T(8,128)S(1)}, u32[]{:S(2)}, u32[]{:S(2)}) collective-permute-start(f32[1,1024,128]{2,1,0:T(8,128)S(1)} %get-tuple-element.145), channel_id=1, source_target_pairs={{0,16},{8,24},{16,0},{24,8},{1,17},{9,25},{17,1},{25,9},{2,18},{10... | collective-permute-start | bytes 1572872 | tf_op jit(solution)/shard_map/ppermute | solution.py:23
  77.6 10.2 %collective-permute-start.10 = (f32[128,128]{1,0:T(8,128)S(1)}, f32[128,128]{1,0:T(8,128)S(1)}, u32[]{:S(2)}, u32[]{:S(2)}) collective-permute-start(f32[128,128]{1,0:T(8,128)S(1)} %get-tuple-element.109), channel_id=1, source_target_pairs={{0,4},{1,5},{2,6},{3,7},{4,0},{5,1},{6,2},{7,3},{8,12},{9,13},{10,... | collective-permute-start | bytes 196616 | tf_op jit(solution)/shard_map/ppermute | solution.py:23
  80.3 7.6 %collective-permute-start.11 = (f32[128,128]{1,0:T(8,128)S(1)}, f32[128,128]{1,0:T(8,128)S(1)}, u32[]{:S(2)}, u32[]{:S(2)}) collective-permute-start(f32[128,128]{1,0:T(8,128)S(1)} %get-tuple-element.110), channel_id=1, source_target_pairs={{0,6},{1,7},{2,4},{3,5},{4,2},{5,3},{6,0},{7,1},{8,14},{9,15},{10,... | collective-permute-start | bytes 196616 | tf_op jit(solution)/shard_map/ppermute | solution.py:23
  81.6 6.2 %collective-permute-start.9 = (f32[128,128]{1,0:T(8,128)S(1)}, f32[128,128]{1,0:T(8,128)S(1)}, u32[]{:S(2)}, u32[]{:S(2)}) collective-permute-start(f32[128,128]{1,0:T(8,128)S(1)} %get-tuple-element.108), channel_id=1, source_target_pairs={{0,2},{1,3},{2,0},{3,1},{4,6},{5,7},{6,4},{7,5},{8,10},{9,11},{10,... | collective-permute-start | bytes 196616 | tf_op jit(solution)/shard_map/ppermute | solution.py:23
  93.0 6.1 %collective-permute-start.13 = (f32[2048,256]{1,0:T(8,128)S(1)}, f32[2048,256]{1,0:T(8,128)S(1)}, u32[]{:S(2)}, u32[]{:S(2)}) collective-permute-start(f32[2048,256]{1,0:T(8,128)S(1)} %copy-done), channel_id=1, source_target_pairs={{0,8},{1,9},{2,10},{3,11},{4,12},{5,13},{6,14},{7,15}} | collective-permute-start | bytes 6291464 | tf_op jit(solution)/shard_map/ppermute | solution.py:466
  94.7 4.3 %collective-permute-start.12 = (f32[1,128,128]{2,1,0:T(8,128)S(1)}, f32[1,128,128]{2,1,0:T(8,128)S(1)}, u32[]{:S(2)}, u32[]{:S(2)}) collective-permute-start(f32[1,128,128]{2,1,0:T(8,128)S(1)} %bitcast.69), channel_id=1, source_target_pairs={{0,16},{8,24},{16,0},{24,8},{1,17},{9,25},{17,1},{25,9},{2,18},{10... | collective-permute-start | bytes 196616 | tf_op jit(solution)/shard_map/ppermute | solution.py:23
  94.8 7.5 %collective-permute-start.15 = (f32[4,128,128]{2,1,0:T(8,128)S(1)}, f32[4,128,128]{2,1,0:T(8,128)S(1)}, u32[]{:S(2)}, u32[]{:S(2)}) collective-permute-start(f32[4,128,128]{2,1,0:T(8,128)S(1)} %get-tuple-element.123), channel_id=1, source_target_pairs={{0,1},{1,0},{2,3},{3,2},{4,5},{5,4},{6,7},{7,6},{8,9},{9,8},{10,11... | collective-permute-start | bytes 786440 | tf_op jit(solution)/shard_map/ppermute | solution.py:23
  101.0 13.5 %collective-permute-start.14 = (f32[1,1024,128]{2,1,0:T(8,128)S(1)}, f32[1,1024,128]{2,1,0:T(8,128)S(1)}, u32[]{:S(2)}, u32[]{:S(2)}) collective-permute-start(f32[1,1024,128]{2,1,0:T(8,128)S(1)} %get-tuple-element.143), channel_id=1, source_target_pairs={{0,16},{8,24},{16,0},{24,8},{1,17},{9,25},{17,1},{25,9},{2,18},{10... | collective-permute-start | bytes 1572872 | tf_op jit(solution)/shard_map/ppermute | solution.py:23
  102.4 4.6 %collective-permute-start.16 = (f32[128,128]{1,0:T(8,128)S(1)}, f32[128,128]{1,0:T(8,128)S(1)}, u32[]{:S(2)}, u32[]{:S(2)}) collective-permute-start(f32[128,128]{1,0:T(8,128)S(1)} %get-tuple-element.157), channel_id=1, source_target_pairs={{0,2},{1,3},{2,0},{3,1},{4,6},{5,7},{6,4},{7,5},{8,10},{9,11},{10,... | collective-permute-start | bytes 196616 | tf_op jit(solution)/shard_map/ppermute | solution.py:23
  104.0 6.6 %collective-permute-start.17 = (f32[128,128]{1,0:T(8,128)S(1)}, f32[128,128]{1,0:T(8,128)S(1)}, u32[]{:S(2)}, u32[]{:S(2)}) collective-permute-start(f32[128,128]{1,0:T(8,128)S(1)} %get-tuple-element.156), channel_id=1, source_target_pairs={{0,4},{1,5},{2,6},{3,7},{4,0},{5,1},{6,2},{7,3},{8,12},{9,13},{10,... | collective-permute-start | bytes 196616 | tf_op jit(solution)/shard_map/ppermute | solution.py:23
  106.6 6.1 %collective-permute-start.18 = (f32[128,128]{1,0:T(8,128)S(1)}, f32[128,128]{1,0:T(8,128)S(1)}, u32[]{:S(2)}, u32[]{:S(2)}) collective-permute-start(f32[128,128]{1,0:T(8,128)S(1)} %get-tuple-element.155), channel_id=1, source_target_pairs={{0,6},{1,7},{2,4},{3,5},{4,2},{5,3},{6,0},{7,1},{8,14},{9,15},{10,... | collective-permute-start | bytes 196616 | tf_op jit(solution)/shard_map/ppermute | solution.py:23
  116.1 8.3 %collective-permute-start.21 = (f32[2048,256]{1,0:T(8,128)S(1)}, f32[2048,256]{1,0:T(8,128)S(1)}, u32[]{:S(2)}, u32[]{:S(2)}) collective-permute-start(f32[2048,256]{1,0:T(8,128)S(1)} %copy-done.1), channel_id=1, source_target_pairs={{0,8},{1,9},{2,10},{3,11},{4,12},{5,13},{6,14},{7,15}} | collective-permute-start | bytes 6291464 | tf_op jit(solution)/shard_map/ppermute | solution.py:466
  117.7 4.9 %collective-permute-start.20 = (f32[2,1024,128]{2,1,0:T(8,128)S(1)}, f32[2,1024,128]{2,1,0:T(8,128)S(1)}, u32[]{:S(2)}, u32[]{:S(2)}) collective-permute-start(f32[2,1024,128]{2,1,0:T(8,128)S(1)} %get-tuple-element.126), channel_id=1, source_target_pairs={{0,8},{8,0},{16,24},{24,16},{1,9},{9,1},{17,25},{25,17},{2,10},{10... | collective-permute-start | bytes 3145736 | tf_op jit(solution)/shard_map/ppermute | solution.py:23
  117.8 6.5 %collective-permute-start.19 = (f32[1,128,128]{2,1,0:T(8,128)S(1)}, f32[1,128,128]{2,1,0:T(8,128)S(1)}, u32[]{:S(2)}, u32[]{:S(2)}) collective-permute-start(f32[1,128,128]{2,1,0:T(8,128)S(1)} %bitcast.67), channel_id=1, source_target_pairs={{0,16},{8,24},{16,0},{24,8},{1,17},{9,25},{17,1},{25,9},{2,18},{10... | collective-permute-start | bytes 196616 | tf_op jit(solution)/shard_map/ppermute | solution.py:23
  122.8 8.7 %collective-permute-start.23 = (f32[4,128,128]{2,1,0:T(8,128)S(1)}, f32[4,128,128]{2,1,0:T(8,128)S(1)}, u32[]{:S(2)}, u32[]{:S(2)}) collective-permute-start(f32[4,128,128]{2,1,0:T(8,128)S(1)} %get-tuple-element.130), channel_id=1, source_target_pairs={{0,1},{1,0},{2,3},{3,2},{4,5},{5,4},{6,7},{7,6},{8,9},{9,8},{10,11... | collective-permute-start | bytes 786440 | tf_op jit(solution)/shard_map/ppermute | solution.py:23
  127.2 14.6 %collective-permute-start.22 = (f32[1,1024,128]{2,1,0:T(8,128)S(1)}, f32[1,1024,128]{2,1,0:T(8,128)S(1)}, u32[]{:S(2)}, u32[]{:S(2)}) collective-permute-start(f32[1,1024,128]{2,1,0:T(8,128)S(1)} %get-tuple-element.141), channel_id=1, source_target_pairs={{0,16},{8,24},{16,0},{24,8},{1,17},{9,25},{17,1},{25,9},{2,18},{10... | collective-permute-start | bytes 1572872 | tf_op jit(solution)/shard_map/ppermute | solution.py:23
  131.5 4.5 %collective-permute-start.24 = (f32[128,128]{1,0:T(8,128)S(1)}, f32[128,128]{1,0:T(8,128)S(1)}, u32[]{:S(2)}, u32[]{:S(2)}) collective-permute-start(f32[128,128]{1,0:T(8,128)S(1)} %get-tuple-element.153), channel_id=1, source_target_pairs={{0,2},{1,3},{2,0},{3,1},{4,6},{5,7},{6,4},{7,5},{8,10},{9,11},{10,... | collective-permute-start | bytes 196616 | tf_op jit(solution)/shard_map/ppermute | solution.py:23
  133.1 7.0 %collective-permute-start.25 = (f32[128,128]{1,0:T(8,128)S(1)}, f32[128,128]{1,0:T(8,128)S(1)}, u32[]{:S(2)}, u32[]{:S(2)}) collective-permute-start(f32[128,128]{1,0:T(8,128)S(1)} %get-tuple-element.152), channel_id=1, source_target_pairs={{0,4},{1,5},{2,6},{3,7},{4,0},{5,1},{6,2},{7,3},{8,12},{9,13},{10,... | collective-permute-start | bytes 196616 | tf_op jit(solution)/shard_map/ppermute | solution.py:23
  135.7 6.1 %collective-permute-start.26 = (f32[128,128]{1,0:T(8,128)S(1)}, f32[128,128]{1,0:T(8,128)S(1)}, u32[]{:S(2)}, u32[]{:S(2)}) collective-permute-start(f32[128,128]{1,0:T(8,128)S(1)} %get-tuple-element.151), channel_id=1, source_target_pairs={{0,6},{1,7},{2,4},{3,5},{4,2},{5,3},{6,0},{7,1},{8,14},{9,15},{10,... | collective-permute-start | bytes 196616 | tf_op jit(solution)/shard_map/ppermute | solution.py:23
  143.4 4.3 %collective-permute-start.27 = (f32[1,128,128]{2,1,0:T(8,128)S(1)}, f32[1,128,128]{2,1,0:T(8,128)S(1)}, u32[]{:S(2)}, u32[]{:S(2)}) collective-permute-start(f32[1,128,128]{2,1,0:T(8,128)S(1)} %bitcast.71), channel_id=1, source_target_pairs={{0,16},{8,24},{16,0},{24,8},{1,17},{9,25},{17,1},{25,9},{2,18},{10... | collective-permute-start | bytes 196616 | tf_op jit(solution)/shard_map/ppermute | solution.py:23
  143.4 7.2 %collective-permute-start.29 = (f32[4,128,128]{2,1,0:T(8,128)S(1)}, f32[4,128,128]{2,1,0:T(8,128)S(1)}, u32[]{:S(2)}, u32[]{:S(2)}) collective-permute-start(f32[4,128,128]{2,1,0:T(8,128)S(1)} %get-tuple-element.133), channel_id=1, source_target_pairs={{0,1},{1,0},{2,3},{3,2},{4,5},{5,4},{6,7},{7,6},{8,9},{9,8},{10,11... | collective-permute-start | bytes 786440 | tf_op jit(solution)/shard_map/ppermute | solution.py:23
  147.7 7.4 %collective-permute-start.28 = (f32[2,3,128,128]{3,2,1,0:T(8,128)S(1)}, f32[2,3,128,128]{3,2,1,0:T(8,128)S(1)}, u32[]{:S(2)}, u32[]{:S(2)}) collective-permute-start(f32[2,3,128,128]{3,2,1,0:T(8,128)S(1)} %pad_maximum_fusion.2), channel_id=1, source_target_pairs={{0,8},{8,0},{16,24},{24,16},{1,9},{9,1},{17,25},{25,17},{2,10},{10... | collective-permute-start | bytes 1179656 | tf_op jit(solution)/shard_map/ppermute | solution.py:23
  150.7 6.7 %collective-permute-start.30 = (f32[128,128]{1,0:T(8,128)S(1)}, f32[128,128]{1,0:T(8,128)S(1)}, u32[]{:S(2)}, u32[]{:S(2)}) collective-permute-start(f32[128,128]{1,0:T(8,128)S(1)} %get-tuple-element.149), channel_id=1, source_target_pairs={{0,2},{1,3},{2,0},{3,1},{4,6},{5,7},{6,4},{7,5},{8,10},{9,11},{10,... | collective-permute-start | bytes 196616 | tf_op jit(solution)/shard_map/ppermute | solution.py:23
  152.3 6.6 %collective-permute-start.31 = (f32[128,128]{1,0:T(8,128)S(1)}, f32[128,128]{1,0:T(8,128)S(1)}, u32[]{:S(2)}, u32[]{:S(2)}) collective-permute-start(f32[128,128]{1,0:T(8,128)S(1)} %get-tuple-element.148), channel_id=1, source_target_pairs={{0,4},{1,5},{2,6},{3,7},{4,0},{5,1},{6,2},{7,3},{8,12},{9,13},{10,... | collective-permute-start | bytes 196616 | tf_op jit(solution)/shard_map/ppermute | solution.py:23
  154.9 6.1 %collective-permute-start.32 = (f32[128,128]{1,0:T(8,128)S(1)}, f32[128,128]{1,0:T(8,128)S(1)}, u32[]{:S(2)}, u32[]{:S(2)}) collective-permute-start(f32[128,128]{1,0:T(8,128)S(1)} %get-tuple-element.147), channel_id=1, source_target_pairs={{0,6},{1,7},{2,4},{3,5},{4,2},{5,3},{6,0},{7,1},{8,14},{9,15},{10,... | collective-permute-start | bytes 196616 | tf_op jit(solution)/shard_map/ppermute | solution.py:23
  (15 other events, 99.2 us)

commit v3 on v2

--- a/solution.py
+++ b/solution.py
@@ -137,15 +137,31 @@
 
 
 def bulk_kernel(own_ref, history_ref, a_ref, *refs, slices, block):
-    outs, (second_ref, third_ref, hi_ref, lo_ref) = refs[:-4], refs[-4:]
-
-    @pl.when(pl.program_id(0) == 0)
+    outs, (second_ref, third_ref, hi_ref, lo_ref, tiles_ref, sems) = refs[:-6], refs[-6:]
+    step, steps = pl.program_id(0), pl.num_programs(0)
+    tile = tiles_ref.shape[4]
+
+    def fetch(i):
+        rows = pl.ds(pl.multiple_of(i * tile, tile), tile)
+        return pltpu.make_async_copy(a_ref.at[:, :, :, rows, :], tiles_ref.at[i % 2], sems.at[i % 2])
+
+    @pl.when(step == 0)
+    def _():
+        fetch(0).start()
+
+    @pl.when(step + 1 < steps)
+    def _():
+        fetch(step + 1).start()
+
+    @pl.when(step == 0)
     def _():
         def get(i):
             return history_ref[i] if i >= 0 else jnp.zeros(history_ref.shape[1:], F32)
 
         prepare_sources(KINDS, get, own_ref[0], slices, a_ref.shape[0], hi_ref, lo_ref)
 
+    fetch(step).wait()
+    a_ref = tiles_ref.at[step % 2]
     second_ref[...] = a_ref[0, 0, 1]
     third_ref[...] = a_ref[0, 1, 0]
     p11, p12, p13, p21, p22, p23, p31, p32, p33 = products(KINDS, a_ref, hi_ref, lo_ref)
@@ -210,11 +226,15 @@
         in_specs=[
             smem(),
             pl.BlockSpec(history.shape, lambda i: (0, 0, 0)),
-            pl.BlockSpec((groups, 2, 2, tile, block), lambda i: (0, 0, 0, i, 0)),
+            pl.BlockSpec(memory_space=pl.ANY),
         ],
         out_specs=[slots_spec] * 2 + [flat_spec] * (2 * steps - 2) + [pl.BlockSpec((tile, block), lambda i: (i, 0))] * 2,
         out_shape=[slots] * 2 + [flat] * (2 * steps - 2) + [jax.ShapeDtypeStruct((rows, block), F32)] * 2,
-        scratch_shapes=[pltpu.VMEM((len(KINDS), groups * block, cols), BF)] * 2,
+        scratch_shapes=[
+            *[pltpu.VMEM((len(KINDS), groups * block, cols), BF)] * 2,
+            pltpu.VMEM((2, groups, 2, 2, tile, block), F32),
+            pltpu.SemaphoreType.DMA((2,)),
+        ],
         compiler_params=pltpu.CompilerParams(vmem_limit_bytes=61 << 20),
         cost_estimate=pl.CostEstimate(
             flops=2 * 4 * len(KINDS) * groups * rows * block * cols,
@@ -413,7 +433,7 @@
     top = 1 << (bits - 1)
     held["newest"], held["got"] = newest, lax.ppermute(newest, "lag", [(0, top)])
     held["carried"] = lax.ppermute(tail, "lag", [(i, i + 1) for i in range(owners - 1)])
-    partials = bulk(lax.optimization_barrier((own, tail))[0], history, lag_matrices, steps, owners, tiles)
+    partials = bulk(own, history, lag_matrices, steps, owners, tiles)
     for n in range(steps):
         held[f"keep{n}"], held[f"send{n}"] = partials[2 * n : 2 * n + 2]
     held["lag2"], held["lag3"] = partials[-2:]
@@ -440,7 +460,7 @@
     with_tail(2)
     held["past1"] = partner_sum(1)
     held["acc0"] = slots[0]
-    sealed(held, "acc0", "keep2", "send2", "past1", "keep3", "odd")
+    sealed(held, "acc0", "keep2", "send2", "keep3", "odd")
     acc = whole_call(merge_kernel, "merge", [(small, LANES)] * (columns // 2), own, held["acc0"])
     parts = scattered(acc, 2)
     held["mine1"], held["got1"] = owners_sum(held["past1"])
@@ -450,7 +470,6 @@
     sealed(held, "keep3", "send3", "past2", "lag2", "mine1", "got1", *(f"part{i}" for i in range(len(parts))))
     a, b = held["mine1"], held["got1"]
     parts = [held[f"part{i}"] for i in range(len(parts))]
-    held["past3"] = partner_sum(3)
 
     shaped = (columns, small, LANES)
     halves = [(columns // 2, small, LANES)] * 2
@@ -460,16 +479,26 @@
             functools.partial(chain_kernel, width=width), "chain", [(small, LANES), *halves],
             own, held["field"][n - 1], a.reshape(shaped), b.reshape(shaped), held["newest"], held["odd"], *parts,
         )
-        shown.append(gathered(x[None]))
         if n + 1 < steps:
-            own_lag = lax.optimization_barrier((held[f"lag{n + 1}"], x))[0]
-            held[f"odd{n + 1}"] = lax.ppermute(own_lag, "lag", [(0, 1)])
+            if n == 1:
+                held["x"] = x
+                sealed(held, "x", "lag2", "send3")
+                x = held["x"]
+                held["past3"] = partner_sum(3)
+            else:
+                held["x"] = x
+                sealed(held, "x", "lag3", "past3")
+                x = held["x"]
+            held[f"odd{n + 1}"] = lax.ppermute(held[f"lag{n + 1}"], "lag", [(0, 1)])
+            shown.append(gathered(x[None]))
             terms = [v for k in range(2, n + 2) for v in (held[f"lag{k}"], held[f"odd{k}"], shown[n + 1 - k])]
             past = whole_call(
                 functools.partial(late_kernel, width=width), "late", [held[f"past{n + 1}"].shape],
                 own, held[f"past{n + 1}"], *terms,
             )[0]
             a, b = owners_sum(past)
+        else:
+            shown.append(gathered(x[None]))
         acc = keep + exchanged(send, "col", 1)
         parts = scattered([acc[i] for i in range(columns // 2)], 2)
     early = jnp.stack(shown, axis=1)

time: 169 us -> 164 us (0.970)
  waiting for transfers between devices: 50 us -> 46.9 us
  Pallas kernels: 72.5 us -> 70.8 us
    ppermute x28, waiting for transfers between devices: 43.6 us -> 40.6 us  [exchanged(): return lax.ppermute(value, axis, swap_pairs(axis, bit))]
    pallas_call x1, Pallas kernels: 41.4 us -> 39.4 us  [bulk(): pl.pallas_call(functools.partial(bulk_kernel, slices=slices, block=block)...]
  transfers between devices with their start and end apart: 35 -> 35, of which waited for: 20 -> 19; matrix products, arithmetic and copies ran while one was open for 1% -> 1% of each run, Pallas kernels for 37% -> 37%
where the time goes in v3:
time: 164 us; the launch traced here: 163 us
  Pallas kernels  70.8 us (43%)
  waiting for transfers between devices  46.9 us (29%)
  starting transfers between devices  38.6 us (24%)
  other arithmetic  4.81 us (3%)
  local copies, waits for them, and re-layouts  1.7 us (1%)
    ppermute x28, waiting for transfers between devices, exchanged(): return lax.ppermute(value, axis, swap_pairs(axis, bit))  40.6 us
    pallas_call x1, Pallas kernels, bulk(): pl.pallas_call(functools.partial(bulk_kernel, slices=slices, block=block)...  39.4 us
    ppermute x28, starting transfers between devices, exchanged(): return lax.ppermute(value, axis, swap_pairs(axis, bit))  24.8 us
    pallas_call x3, Pallas kernels, with_carried(): pl.pallas_call(functools.partial(carried_kernel, slices=slices), grid=(1,...  13.1 us
    pallas_call x7, Pallas kernels, whole_call(): pl.pallas_call(kernel, in_specs=[smem()] + [vmem] * (len(args) - 1), out_...  11.2 us
    ppermute x2, waiting for transfers between devices, taken(): got = lax.ppermute(offer, ('lag', 'col'), stage_pairs(stage))  6.37 us
    ppermute x1, starting transfers between devices, local(): lax.ppermute(newest, 'lag', [(0, top)])  6.23 us
    pallas_call x2, Pallas kernels, assembled(): pl.pallas_call(functools.partial(assemble_kernel, slices=owners), grid=(1...  3.68 us
  transfers between devices with their start and end apart: 35, of which 19 were waited for; matrix products, arithmetic and copies ran while one was open for 1% of the time, Pallas kernels for 37%

profile of v3, /device:TPU:0, one launch (start us, length us, event | category | flops | bytes accessed | tf_op | source)
XLA Modules:
  0.0 163.3 jit_solution(1166780616012579760)
XLA Ops:
  0.6 3.5 %stage.1 = (f32[2048,256]{1,0:T(8,128)}, f32[3,256,256]{2,1,0:T(8,128)}) custom-call(s32[2]{0:T(128)} %pad_add_fusion.own_ref, f32[16,2048,256]{2,1,0:T(8,128)} %refs_2_.3, f32[16,256,256]{2,1,0:T(8,128)} %refs_2_.2, f32[16,256,256]{2,1,0:T(8,128)} %refs_2_.2, f32[16,256,256]{2,1,0:T(8,128)} %refs_2_.2), custom_call_target="tpu_custom_call" | custom-call | flops 1 | bytes 1 | tf_op jit(solution)/shard_map/stage/pallas_call | solution.py:259
  4.1 6.2 %collective-permute-start = (f32[2048,256]{1,0:T(8,128)}, f32[2048,256]{1,0:T(8,128)}, u32[]{:S(2)}, u32[]{:S(2)}) collective-permute-start(f32[2048,256]{1,0:T(8,128)} %get-tuple-element.88), channel_id=1, source_target_pairs={{0,16},{1,17},{2,18},{3,19},{4,20},{5,21},{6,22},{7,23}} | collective-permute-start | bytes 6291464 | tf_op jit(solution)/shard_map/ppermute | solution.py:434
  11.7 39.4 %bulk.1 = (f32[4,4,128,128]{3,2,1,0:T(8,128)}, f32[4,4,128,128]{3,2,1,0:T(8,128)}, f32[2,1024,128]{2,1,0:T(8,128)}, f32[2,1024,128]{2,1,0:T(8,128)}, f32[2,1024,...) custom-call(s32[2]{0:T(128)} %pad_add_fusion.own_ref, ...), custom_call_target="tpu_custom_call" | custom-call | flops 38654705664 | bytes 33554432 | tf_op jit(solution)/shard_map/bulk/pallas_call | solution.py:223
  57.0 3.0 %carried.3 = (f32[2,1024,128]{2,1,0:T(8,128)S(1)}, f32[2,1024,128]{2,1,0:T(8,128)S(1)}) custom-call(s32[2]{0:T(128)S(1)} %copy-done.9, f32[3,256,256]{2,1,0:T(8,128)S(1)} %collective-permute-done.1.tail_ref, f32[2,1024,128]{2,1,0:T(8,128)S(1)} %copy-done.4, f32[2,1024,128]{2,1,0:T(8,128)S(1)} %copy-done.5, f32[16,2048,256]{2,1,0:T(8,128)} %refs_2_.3), custom_call_target="tpu_custom_call" | custom-call | flops 1 | bytes 1 | tf_op jit(solution)/shard_map/carried/pallas_call | solution.py:194
  60.3 4.4 %collective-permute-done.3 = f32[2,4,128,128]{3,2,1,0:T(8,128)S(1)} collective-permute-done((f32[2,4,128,128]{3,2,1,0:T(8,128)S(1)}, f32[2,4,128,128]{3,2,1,0:T(8,128)S(1)}, u32[]{:S(2)}, u32[]{:S(2)}) %collective-permute-start.3) | collective-permute-done | bytes 524320 | tf_op jit(solution)/shard_map/ppermute | solution.py:401
  67.3 4.3 %carried.4 = (f32[2,1024,128]{2,1,0:T(8,128)S(1)}, f32[2,1024,128]{2,1,0:T(8,128)S(1)}) custom-call(s32[2]{0:T(128)S(1)} %copy-done.9, f32[3,256,256]{2,1,0:T(8,128)S(1)} %collective-permute-done.1.tail_ref, f32[2,1024,128]{2,1,0:T(8,128)S(1)} %copy-done.7, f32[2,1024,128]{2,1,0:T(8,128)S(1)} %copy-done.8, f32[16,2048,256]{2,1,0:T(8,128)} %refs_2_.3, ...), custom_call_target="tpu_custom_call" | custom-call | flops 1 | bytes 1 | tf_op jit(solution)/shard_map/carried/pallas_call | solution.py:194
  71.6 2.0 %collective-permute-done.4 = f32[1,4,128,128]{3,2,1,0:T(8,128)S(1)} collective-permute-done((f32[1,4,128,128]{3,2,1,0:T(8,128)S(1)}, f32[1,4,128,128]{3,2,1,0:T(8,128)S(1)}, u32[]{:S(2)}, u32[]{:S(2)}) %collective-permute-start.4) | collective-permute-done | bytes 262176 | tf_op jit(solution)/shard_map/ppermute | solution.py:401
  75.6 2.6 %collective-permute-start.10 = (f32[128,128]{1,0:T(8,128)S(1)}, f32[128,128]{1,0:T(8,128)S(1)}, u32[]{:S(2)}, u32[]{:S(2)}) collective-permute-start(f32[128,128]{1,0:T(8,128)S(1)} %get-tuple-element.109), channel_id=1, source_target_pairs={{0,4},{1,5},{2,6},{3,7},{4,0},{5,1},{6,2},{7,3},{8,12},{9,13},{10,... | collective-permute-start | bytes 196616 | tf_op jit(solution)/shard_map/ppermute | solution.py:23
  79.9 5.8 %carried.5 = (f32[2,1024,128]{2,1,0:T(8,128)S(1)}, f32[2,1024,128]{2,1,0:T(8,128)S(1)}) custom-call(s32[2]{0:T(128)S(1)} %copy-done.9, f32[3,256,256]{2,1,0:T(8,128)S(1)} %collective-permute-done.1.tail_ref, f32[2,1024,128]{2,1,0:T(8,128)S(1)} %copy-done.2, f32[2,1024,128]{2,1,0:T(8,128)S(1)} %copy-done.3, f32[16,2048,256]{2,1,0:T(8,128)} %refs_2_.3, ...), custom_call_target="tpu_custom_call" | custom-call | flops 1 | bytes 1 | tf_op jit(solution)/shard_map/carried/pallas_call | solution.py:194
  85.8 3.5 %collective-permute-done.8 = f32[1,1024,128]{2,1,0:T(8,128)S(1)} collective-permute-done((f32[1,1024,128]{2,1,0:T(8,128)S(1)}, f32[1,1024,128]{2,1,0:T(8,128)S(1)}, u32[]{:S(2)}, u32[]{:S(2)}) %collective-permute-start.8) | collective-permute-done | bytes 524320 | tf_op jit(solution)/shard_map/ppermute | solution.py:23
  90.9 1.7 %collective-permute-start.13 = (f32[2048,256]{1,0:T(8,128)S(1)}, f32[2048,256]{1,0:T(8,128)S(1)}, u32[]{:S(2)}, u32[]{:S(2)}) collective-permute-start(f32[2048,256]{1,0:T(8,128)S(1)} %copy-done), channel_id=1, source_target_pairs={{0,8},{1,9},{2,10},{3,11},{4,12},{5,13},{6,14},{7,15}} | collective-permute-start | bytes 6291464 | tf_op jit(solution)/shard_map/ppermute | solution.py:492
  94.4 2.9 %collective-permute-done.12 = f32[1,128,128]{2,1,0:T(8,128)S(1)} collective-permute-done((f32[1,128,128]{2,1,0:T(8,128)S(1)}, f32[1,128,128]{2,1,0:T(8,128)S(1)}, u32[]{:S(2)}, u32[]{:S(2)}) %collective-permute-start.12) | collective-permute-done | bytes 65568 | tf_op jit(solution)/shard_map/ppermute | solution.py:23
  97.3 2.0 %late.2 = f32[2,1024,128]{2,1,0:T(8,128)S(1)} custom-call(s32[2]{0:T(128)S(1)} %copy-done.9, f32[2,1024,128]{2,1,0:T(8,128)S(1)} %add.65.acc_ref, f32[2048,256]{1,0:T(8,128)S(1)} %copy-done, f32[2048,256]{1,0:T(8,128)S(1)} %collective-permute-done.13.refs_1_, f32[2,128,128]{2,1,0:T(8,128)S(1)} %get-tuple-element.167.refs_2_.refs_5_), custom_call_target="tpu_custom_call" | custom-call | flops 1 | bytes 1 | tf_op jit(solution)/shard_map/late/pallas_call | solution.py:358
  99.5 2.0 %collective-permute-done.15 = f32[4,128,128]{2,1,0:T(8,128)S(1)} collective-permute-done((f32[4,128,128]{2,1,0:T(8,128)S(1)}, f32[4,128,128]{2,1,0:T(8,128)S(1)}, u32[]{:S(2)}, u32[]{:S(2)}) %collective-permute-start.15) | collective-permute-done | bytes 262176 | tf_op jit(solution)/shard_map/ppermute | solution.py:23
  101.5 1.6 %collective-permute-start.16 = (f32[128,128]{1,0:T(8,128)S(1)}, f32[128,128]{1,0:T(8,128)S(1)}, u32[]{:S(2)}, u32[]{:S(2)}) collective-permute-start(f32[128,128]{1,0:T(8,128)S(1)} %get-tuple-element.161), channel_id=1, source_target_pairs={{0,2},{1,3},{2,0},{3,1},{4,6},{5,7},{6,4},{7,5},{8,10},{9,11},{10,... | collective-permute-start | bytes 196616 | tf_op jit(solution)/shard_map/ppermute | solution.py:23
  103.2 2.6 %collective-permute-start.17 = (f32[128,128]{1,0:T(8,128)S(1)}, f32[128,128]{1,0:T(8,128)S(1)}, u32[]{:S(2)}, u32[]{:S(2)}) collective-permute-start(f32[128,128]{1,0:T(8,128)S(1)} %get-tuple-element.160), channel_id=1, source_target_pairs={{0,4},{1,5},{2,6},{3,7},{4,0},{5,1},{6,2},{7,3},{8,12},{9,13},{10,... | collective-permute-start | bytes 196616 | tf_op jit(solution)/shard_map/ppermute | solution.py:23
  106.1 4.0 %collective-permute-done.17.refs_2_ = f32[128,128]{1,0:T(8,128)S(1)} collective-permute-done((f32[128,128]{1,0:T(8,128)S(1)}, f32[128,128]{1,0:T(8,128)S(1)}, u32[]{:S(2)}, u32[]{:S(2)}) %collective-permute-start.17) | collective-permute-done | bytes 65568 | tf_op jit(solution)/shard_map/ppermute | solution.py:23
  110.2 1.7 %collective-permute-done.18.refs_3_ = f32[128,128]{1,0:T(8,128)S(1)} collective-permute-done((f32[128,128]{1,0:T(8,128)S(1)}, f32[128,128]{1,0:T(8,128)S(1)}, u32[]{:S(2)}, u32[]{:S(2)}) %collective-permute-start.18) | collective-permute-done | bytes 65568 | tf_op jit(solution)/shard_map/ppermute | solution.py:23
  117.6 2.7 %collective-permute-done.20 = f32[1,128,128]{2,1,0:T(8,128)S(1)} collective-permute-done((f32[1,128,128]{2,1,0:T(8,128)S(1)}, f32[1,128,128]{2,1,0:T(8,128)S(1)}, u32[]{:S(2)}, u32[]{:S(2)}) %collective-permute-start.20) | collective-permute-done | bytes 65568 | tf_op jit(solution)/shard_map/ppermute | solution.py:23
  120.4 2.7 %late.3 = f32[2,1024,128]{2,1,0:T(8,128)S(1)} custom-call(s32[2]{0:T(128)S(1)} %copy-done.9, f32[2,1024,128]{2,1,0:T(8,128)S(1)} %add.68.acc_ref, f32[2048,256]{1,0:T(8,128)S(1)} %copy-done, f32[2048,256]{1,0:T(8,128)S(1)} %collective-permute-done.13.refs_1_, f32[2,128,128]{2,1,0:T(8,128)S(1)} %get-tuple-element.169.refs_2_, f32[2048,256]{1,0:T(8,128)S(1)} %copy-done.1, ...), custom_call_target="tpu_custom_call" | custom-call | flops 1 | bytes 1 | tf_op jit(solution)/shard_map/late/pallas_call | solution.py:358
  123.3 1.6 %collective-permute-start.24 = (f32[128,128]{1,0:T(8,128)S(1)}, f32[128,128]{1,0:T(8,128)S(1)}, u32[]{:S(2)}, u32[]{:S(2)}) collective-permute-start(f32[128,128]{1,0:T(8,128)S(1)} %get-tuple-element.157), channel_id=1, source_target_pairs={{0,2},{1,3},{2,0},{3,1},{4,6},{5,7},{6,4},{7,5},{8,10},{9,11},{10,... | collective-permute-start | bytes 196616 | tf_op jit(solution)/shard_map/ppermute | solution.py:23
  125.0 2.6 %collective-permute-start.25 = (f32[128,128]{1,0:T(8,128)S(1)}, f32[128,128]{1,0:T(8,128)S(1)}, u32[]{:S(2)}, u32[]{:S(2)}) collective-permute-start(f32[128,128]{1,0:T(8,128)S(1)} %get-tuple-element.156), channel_id=1, source_target_pairs={{0,4},{1,5},{2,6},{3,7},{4,0},{5,1},{6,2},{7,3},{8,12},{9,13},{10,... | collective-permute-start | bytes 196616 | tf_op jit(solution)/shard_map/ppermute | solution.py:23
  127.8 4.3 %collective-permute-done.25.refs_2_ = f32[128,128]{1,0:T(8,128)S(1)} collective-permute-done((f32[128,128]{1,0:T(8,128)S(1)}, f32[128,128]{1,0:T(8,128)S(1)}, u32[]{:S(2)}, u32[]{:S(2)}) %collective-permute-start.25) | collective-permute-done | bytes 65568 | tf_op jit(solution)/shard_map/ppermute | solution.py:23
  132.1 1.6 collective-permute-done.26.refs_3_
  133.6 3.1 %collective-permute-done.22 = f32[1,1024,128]{2,1,0:T(8,128)S(1)} collective-permute-done((f32[1,1024,128]{2,1,0:T(8,128)S(1)}, f32[1,1024,128]{2,1,0:T(8,128)S(1)}, u32[]{:S(2)}, u32[]{:S(2)}) %collective-permute-start.22) | collective-permute-done | bytes 524320 | tf_op jit(solution)/shard_map/ppermute | solution.py:23
  140.1 2.5 %collective-permute-done.27 = f32[1,128,128]{2,1,0:T(8,128)S(1)} collective-permute-done((f32[1,128,128]{2,1,0:T(8,128)S(1)}, f32[1,128,128]{2,1,0:T(8,128)S(1)}, u32[]{:S(2)}, u32[]{:S(2)}) %collective-permute-start.27) | collective-permute-done | bytes 65568 | tf_op jit(solution)/shard_map/ppermute | solution.py:23
  142.8 2.9 %collective-permute-done.29 = f32[4,128,128]{2,1,0:T(8,128)S(1)} collective-permute-done((f32[4,128,128]{2,1,0:T(8,128)S(1)}, f32[4,128,128]{2,1,0:T(8,128)S(1)}, u32[]{:S(2)}, u32[]{:S(2)}) %collective-permute-start.29) | collective-permute-done | bytes 262176 | tf_op jit(solution)/shard_map/ppermute | solution.py:23
  145.7 1.6 %collective-permute-start.30 = (f32[128,128]{1,0:T(8,128)S(1)}, f32[128,128]{1,0:T(8,128)S(1)}, u32[]{:S(2)}, u32[]{:S(2)}) collective-permute-start(f32[128,128]{1,0:T(8,128)S(1)} %get-tuple-element.153), channel_id=1, source_target_pairs={{0,2},{1,3},{2,0},{3,1},{4,6},{5,7},{6,4},{7,5},{8,10},{9,11},{10,... | collective-permute-start | bytes 196616 | tf_op jit(solution)/shard_map/ppermute | solution.py:23
  147.3 2.6 %collective-permute-start.31 = (f32[128,128]{1,0:T(8,128)S(1)}, f32[128,128]{1,0:T(8,128)S(1)}, u32[]{:S(2)}, u32[]{:S(2)}) collective-permute-start(f32[128,128]{1,0:T(8,128)S(1)} %get-tuple-element.152), channel_id=1, source_target_pairs={{0,4},{1,5},{2,6},{3,7},{4,0},{5,1},{6,2},{7,3},{8,12},{9,13},{10,... | collective-permute-start | bytes 196616 | tf_op jit(solution)/shard_map/ppermute | solution.py:23
  150.2 2.1 %assemble.2.refs_0_ = f32[4,256,256]{2,1,0:T(8,128)} custom-call(s32[2]{0:T(128)S(1)} %copy-done.9, f32[4,3,128,128]{3,2,1,0:T(8,128)S(1)} %pad_maximum_fusion.parts_ref), custom_call_target="tpu_custom_call" | custom-call | flops 1 | bytes 1 | tf_op jit(solution)/shard_map/assemble/pallas_call | solution.py:342
  153.8 2.2 %collective-permute-done.32 = f32[128,128]{1,0:T(8,128)S(1)} collective-permute-done((f32[128,128]{1,0:T(8,128)S(1)}, f32[128,128]{1,0:T(8,128)S(1)}, u32[]{:S(2)}, u32[]{:S(2)}) %collective-permute-start.32) | collective-permute-done | bytes 65568 | tf_op jit(solution)/shard_map/ppermute | solution.py:23
  157.5 2.8 %collective-permute-done.33 = f32[1,128,128]{2,1,0:T(8,128)S(1)} collective-permute-done((f32[1,128,128]{2,1,0:T(8,128)S(1)}, f32[1,128,128]{2,1,0:T(8,128)S(1)}, u32[]{:S(2)}, u32[]{:S(2)}) %collective-permute-start.33) | collective-permute-done | bytes 65568 | tf_op jit(solution)/shard_map/ppermute | solution.py:23
  (103 shorter events, 34.1 us)
Async XLA Ops:
  4.1 47.0 %collective-permute-start = (f32[2048,256]{1,0:T(8,128)}, f32[2048,256]{1,0:T(8,128)}, u32[]{:S(2)}, u32[]{:S(2)}) collective-permute-start(f32[2048,256]{1,0:T(8,128)} %get-tuple-element.88), channel_id=1, source_target_pairs={{0,16},{1,17},{2,18},{3,19},{4,20},{5,21},{6,22},{7,23}} | collective-permute-start | bytes 6291464 | tf_op jit(solution)/shard_map/ppermute | solution.py:434
  10.3 40.7 %collective-permute-start.1 = (f32[3,256,256]{2,1,0:T(8,128)}, f32[3,256,256]{2,1,0:T(8,128)S(1)}, u32[]{:S(2)}, u32[]{:S(2)}) collective-permute-start(f32[3,256,256]{2,1,0:T(8,128)} %get-tuple-element.77), channel_id=1, source_target_pairs={{0,8},{8,16},{16,24},{1,9},{9,17},{17,25},{2,10},{10,18},{18,26},{... | collective-permute-start | bytes 2359304 | tf_op jit(solution)/shard_map/ppermute | solution.py:435
  55.4 9.2 %collective-permute-start.3 = (f32[2,4,128,128]{3,2,1,0:T(8,128)S(1)}, f32[2,4,128,128]{3,2,1,0:T(8,128)S(1)}, u32[]{:S(2)}, u32[]{:S(2)}) collective-permute-start(f32[2,4,128,128]{3,2,1,0:T(8,128)S(1)} %pad_maximum_fusion.1), channel_id=1, source_target_pairs={{0,1},{1,0},{2,3},{3,2},{4,5},{5,4},{6,7},{7,6},{8,24},{9,25},{10,... | collective-permute-start | bytes 1572872 | tf_op jit(solution)/shard_map/ppermute | solution.py:401
  65.7 9.0 %collective-permute-start.5 = (f32[2048,256]{1,0:T(8,128)S(1)}, f32[2048,256]{1,0:T(8,128)S(1)}, u32[]{:S(2)}, u32[]{:S(2)}) collective-permute-start(f32[2048,256]{1,0:T(8,128)S(1)} %broadcast_select_fusion.m_ref), channel_id=1, source_target_pairs={{0,8},{16,24},{1,9},{17,25},{2,10},{18,26},{3,11},{19,27},{4,12},{... | collective-permute-start | bytes 6291464 | tf_op jit(solution)/shard_map/ppermute | solution.py:456
  67.1 7.6 %collective-permute-start.7 = (f32[2,1024,128]{2,1,0:T(8,128)S(1)}, f32[2,1024,128]{2,1,0:T(8,128)S(1)}, u32[]{:S(2)}, u32[]{:S(2)}) collective-permute-start(f32[2,1024,128]{2,1,0:T(8,128)S(1)} %get-tuple-element.105), channel_id=1, source_target_pairs={{0,8},{8,0},{16,24},{24,16},{1,9},{9,1},{17,25},{25,17},{2,10},{10... | collective-permute-start | bytes 3145736 | tf_op jit(solution)/shard_map/ppermute | solution.py:23
  67.2 6.4 %collective-permute-start.4 = (f32[1,4,128,128]{3,2,1,0:T(8,128)S(1)}, f32[1,4,128,128]{3,2,1,0:T(8,128)S(1)}, u32[]{:S(2)}, u32[]{:S(2)}) collective-permute-start(f32[1,4,128,128]{3,2,1,0:T(8,128)S(1)} %slice_add_fusion.2), channel_id=1, source_target_pairs={{0,16},{1,17},{2,18},{3,19},{4,20},{5,21},{6,22},{7,23},{8,9},{9,8... | collective-permute-start | bytes 786440 | tf_op jit(solution)/shard_map/ppermute | solution.py:401
  74.7 11.0 %collective-permute-start.6 = (f32[2,1024,128]{2,1,0:T(8,128)S(1)}, f32[2,1024,128]{2,1,0:T(8,128)S(1)}, u32[]{:S(2)}, u32[]{:S(2)}) collective-permute-start(f32[2,1024,128]{2,1,0:T(8,128)S(1)} %get-tuple-element.102), channel_id=1, source_target_pairs={{0,8},{8,0},{16,24},{24,16},{1,9},{9,1},{17,25},{25,17},{2,10},{10... | collective-permute-start | bytes 3145736 | tf_op jit(solution)/shard_map/ppermute | solution.py:23
  75.0 14.4 %collective-permute-start.8 = (f32[1,1024,128]{2,1,0:T(8,128)S(1)}, f32[1,1024,128]{2,1,0:T(8,128)S(1)}, u32[]{:S(2)}, u32[]{:S(2)}) collective-permute-start(f32[1,1024,128]{2,1,0:T(8,128)S(1)} %get-tuple-element.149), channel_id=1, source_target_pairs={{0,16},{8,24},{16,0},{24,8},{1,17},{9,25},{17,1},{25,9},{2,18},{10... | collective-permute-start | bytes 1572872 | tf_op jit(solution)/shard_map/ppermute | solution.py:23
  75.6 13.7 %collective-permute-start.10 = (f32[128,128]{1,0:T(8,128)S(1)}, f32[128,128]{1,0:T(8,128)S(1)}, u32[]{:S(2)}, u32[]{:S(2)}) collective-permute-start(f32[128,128]{1,0:T(8,128)S(1)} %get-tuple-element.109), channel_id=1, source_target_pairs={{0,4},{1,5},{2,6},{3,7},{4,0},{5,1},{6,2},{7,3},{8,12},{9,13},{10,... | collective-permute-start | bytes 196616 | tf_op jit(solution)/shard_map/ppermute | solution.py:23
  78.3 11.1 %collective-permute-start.11 = (f32[128,128]{1,0:T(8,128)S(1)}, f32[128,128]{1,0:T(8,128)S(1)}, u32[]{:S(2)}, u32[]{:S(2)}) collective-permute-start(f32[128,128]{1,0:T(8,128)S(1)} %get-tuple-element.110), channel_id=1, source_target_pairs={{0,6},{1,7},{2,4},{3,5},{4,2},{5,3},{6,0},{7,1},{8,14},{9,15},{10,... | collective-permute-start | bytes 196616 | tf_op jit(solution)/shard_map/ppermute | solution.py:23
  79.6 9.7 %collective-permute-start.9 = (f32[128,128]{1,0:T(8,128)S(1)}, f32[128,128]{1,0:T(8,128)S(1)}, u32[]{:S(2)}, u32[]{:S(2)}) collective-permute-start(f32[128,128]{1,0:T(8,128)S(1)} %get-tuple-element.108), channel_id=1, source_target_pairs={{0,2},{1,3},{2,0},{3,1},{4,6},{5,7},{6,4},{7,5},{8,10},{9,11},{10,... | collective-permute-start | bytes 196616 | tf_op jit(solution)/shard_map/ppermute | solution.py:23
  90.9 6.4 %collective-permute-start.13 = (f32[2048,256]{1,0:T(8,128)S(1)}, f32[2048,256]{1,0:T(8,128)S(1)}, u32[]{:S(2)}, u32[]{:S(2)}) collective-permute-start(f32[2048,256]{1,0:T(8,128)S(1)} %copy-done), channel_id=1, source_target_pairs={{0,8},{1,9},{2,10},{3,11},{4,12},{5,13},{6,14},{7,15}} | collective-permute-start | bytes 6291464 | tf_op jit(solution)/shard_map/ppermute | solution.py:492
  92.7 13.3 %collective-permute-start.19 = (f32[2,1024,128]{2,1,0:T(8,128)S(1)}, f32[2,1024,128]{2,1,0:T(8,128)S(1)}, u32[]{:S(2)}, u32[]{:S(2)}) collective-permute-start(f32[2,1024,128]{2,1,0:T(8,128)S(1)} %get-tuple-element.129), channel_id=1, source_target_pairs={{0,8},{8,0},{16,24},{24,16},{1,9},{9,1},{17,25},{25,17},{2,10},{10... | collective-permute-start | bytes 3145736 | tf_op jit(solution)/shard_map/ppermute | solution.py:23
  92.8 4.5 %collective-permute-start.12 = (f32[1,128,128]{2,1,0:T(8,128)S(1)}, f32[1,128,128]{2,1,0:T(8,128)S(1)}, u32[]{:S(2)}, u32[]{:S(2)}) collective-permute-start(f32[1,128,128]{2,1,0:T(8,128)S(1)} %bitcast.67), channel_id=1, source_target_pairs={{0,16},{8,24},{16,0},{24,8},{1,17},{9,25},{17,1},{25,9},{2,18},{10... | collective-permute-start | bytes 196616 | tf_op jit(solution)/shard_map/ppermute | solution.py:23
  92.9 8.6 %collective-permute-start.15 = (f32[4,128,128]{2,1,0:T(8,128)S(1)}, f32[4,128,128]{2,1,0:T(8,128)S(1)}, u32[]{:S(2)}, u32[]{:S(2)}) collective-permute-start(f32[4,128,128]{2,1,0:T(8,128)S(1)} %get-tuple-element.125), channel_id=1, source_target_pairs={{0,1},{1,0},{2,3},{3,2},{4,5},{5,4},{6,7},{7,6},{8,9},{9,8},{10,11... | collective-permute-start | bytes 786440 | tf_op jit(solution)/shard_map/ppermute | solution.py:23
  99.4 13.6 %collective-permute-start.14 = (f32[1,1024,128]{2,1,0:T(8,128)S(1)}, f32[1,1024,128]{2,1,0:T(8,128)S(1)}, u32[]{:S(2)}, u32[]{:S(2)}) collective-permute-start(f32[1,1024,128]{2,1,0:T(8,128)S(1)} %get-tuple-element.147), channel_id=1, source_target_pairs={{0,16},{8,24},{16,0},{24,8},{1,17},{9,25},{17,1},{25,9},{2,18},{10... | collective-permute-start | bytes 1572872 | tf_op jit(solution)/shard_map/ppermute | solution.py:23
  101.5 4.6 %collective-permute-start.16 = (f32[128,128]{1,0:T(8,128)S(1)}, f32[128,128]{1,0:T(8,128)S(1)}, u32[]{:S(2)}, u32[]{:S(2)}) collective-permute-start(f32[128,128]{1,0:T(8,128)S(1)} %get-tuple-element.161), channel_id=1, source_target_pairs={{0,2},{1,3},{2,0},{3,1},{4,6},{5,7},{6,4},{7,5},{8,10},{9,11},{10,... | collective-permute-start | bytes 196616 | tf_op jit(solution)/shard_map/ppermute | solution.py:23
  103.2 7.0 %collective-permute-start.17 = (f32[128,128]{1,0:T(8,128)S(1)}, f32[128,128]{1,0:T(8,128)S(1)}, u32[]{:S(2)}, u32[]{:S(2)}) collective-permute-start(f32[128,128]{1,0:T(8,128)S(1)} %get-tuple-element.160), channel_id=1, source_target_pairs={{0,4},{1,5},{2,6},{3,7},{4,0},{5,1},{6,2},{7,3},{8,12},{9,13},{10,... | collective-permute-start | bytes 196616 | tf_op jit(solution)/shard_map/ppermute | solution.py:23
  105.8 6.1 %collective-permute-start.18 = (f32[128,128]{1,0:T(8,128)S(1)}, f32[128,128]{1,0:T(8,128)S(1)}, u32[]{:S(2)}, u32[]{:S(2)}) collective-permute-start(f32[128,128]{1,0:T(8,128)S(1)} %get-tuple-element.159), channel_id=1, source_target_pairs={{0,6},{1,7},{2,4},{3,5},{4,2},{5,3},{6,0},{7,1},{8,14},{9,15},{10,... | collective-permute-start | bytes 196616 | tf_op jit(solution)/shard_map/ppermute | solution.py:23
  114.6 5.8 %collective-permute-start.21 = (f32[2048,256]{1,0:T(8,128)S(1)}, f32[2048,256]{1,0:T(8,128)S(1)}, u32[]{:S(2)}, u32[]{:S(2)}) collective-permute-start(f32[2048,256]{1,0:T(8,128)S(1)} %copy-done.1), channel_id=1, source_target_pairs={{0,8},{1,9},{2,10},{3,11},{4,12},{5,13},{6,14},{7,15}} | collective-permute-start | bytes 6291464 | tf_op jit(solution)/shard_map/ppermute | solution.py:492
  116.0 4.3 %collective-permute-start.20 = (f32[1,128,128]{2,1,0:T(8,128)S(1)}, f32[1,128,128]{2,1,0:T(8,128)S(1)}, u32[]{:S(2)}, u32[]{:S(2)}) collective-permute-start(f32[1,128,128]{2,1,0:T(8,128)S(1)} %bitcast.69), channel_id=1, source_target_pairs={{0,16},{8,24},{16,0},{24,8},{1,17},{9,25},{17,1},{25,9},{2,18},{10... | collective-permute-start | bytes 196616 | tf_op jit(solution)/shard_map/ppermute | solution.py:23
  116.1 7.2 %collective-permute-start.23 = (f32[4,128,128]{2,1,0:T(8,128)S(1)}, f32[4,128,128]{2,1,0:T(8,128)S(1)}, u32[]{:S(2)}, u32[]{:S(2)}) collective-permute-start(f32[4,128,128]{2,1,0:T(8,128)S(1)} %get-tuple-element.134), channel_id=1, source_target_pairs={{0,1},{1,0},{2,3},{3,2},{4,5},{5,4},{6,7},{7,6},{8,9},{9,8},{10,11... | collective-permute-start | bytes 786440 | tf_op jit(solution)/shard_map/ppermute | solution.py:23
  123.2 13.5 %collective-permute-start.22 = (f32[1,1024,128]{2,1,0:T(8,128)S(1)}, f32[1,1024,128]{2,1,0:T(8,128)S(1)}, u32[]{:S(2)}, u32[]{:S(2)}) collective-permute-start(f32[1,1024,128]{2,1,0:T(8,128)S(1)} %get-tuple-element.145), channel_id=1, source_target_pairs={{0,16},{8,24},{16,0},{24,8},{1,17},{9,25},{17,1},{25,9},{2,18},{10... | collective-permute-start | bytes 1572872 | tf_op jit(solution)/shard_map/ppermute | solution.py:23
  123.3 4.5 %collective-permute-start.24 = (f32[128,128]{1,0:T(8,128)S(1)}, f32[128,128]{1,0:T(8,128)S(1)}, u32[]{:S(2)}, u32[]{:S(2)}) collective-permute-start(f32[128,128]{1,0:T(8,128)S(1)} %get-tuple-element.157), channel_id=1, source_target_pairs={{0,2},{1,3},{2,0},{3,1},{4,6},{5,7},{6,4},{7,5},{8,10},{9,11},{10,... | collective-permute-start | bytes 196616 | tf_op jit(solution)/shard_map/ppermute | solution.py:23
  125.0 7.1 %collective-permute-start.25 = (f32[128,128]{1,0:T(8,128)S(1)}, f32[128,128]{1,0:T(8,128)S(1)}, u32[]{:S(2)}, u32[]{:S(2)}) collective-permute-start(f32[128,128]{1,0:T(8,128)S(1)} %get-tuple-element.156), channel_id=1, source_target_pairs={{0,4},{1,5},{2,6},{3,7},{4,0},{5,1},{6,2},{7,3},{8,12},{9,13},{10,... | collective-permute-start | bytes 196616 | tf_op jit(solution)/shard_map/ppermute | solution.py:23
  127.6 6.1 %collective-permute-start.26 = (f32[128,128]{1,0:T(8,128)S(1)}, f32[128,128]{1,0:T(8,128)S(1)}, u32[]{:S(2)}, u32[]{:S(2)}) collective-permute-start(f32[128,128]{1,0:T(8,128)S(1)} %get-tuple-element.155), channel_id=1, source_target_pairs={{0,6},{1,7},{2,4},{3,5},{4,2},{5,3},{6,0},{7,1},{8,14},{9,15},{10,... | collective-permute-start | bytes 196616 | tf_op jit(solution)/shard_map/ppermute | solution.py:23
  138.3 4.3 %collective-permute-start.27 = (f32[1,128,128]{2,1,0:T(8,128)S(1)}, f32[1,128,128]{2,1,0:T(8,128)S(1)}, u32[]{:S(2)}, u32[]{:S(2)}) collective-permute-start(f32[1,128,128]{2,1,0:T(8,128)S(1)} %bitcast.71), channel_id=1, source_target_pairs={{0,16},{8,24},{16,0},{24,8},{1,17},{9,25},{17,1},{25,9},{2,18},{10... | collective-permute-start | bytes 196616 | tf_op jit(solution)/shard_map/ppermute | solution.py:23
  138.6 7.0 %collective-permute-start.29 = (f32[4,128,128]{2,1,0:T(8,128)S(1)}, f32[4,128,128]{2,1,0:T(8,128)S(1)}, u32[]{:S(2)}, u32[]{:S(2)}) collective-permute-start(f32[4,128,128]{2,1,0:T(8,128)S(1)} %get-tuple-element.137), channel_id=1, source_target_pairs={{0,1},{1,0},{2,3},{3,2},{4,5},{5,4},{6,7},{7,6},{8,9},{9,8},{10,11... | collective-permute-start | bytes 786440 | tf_op jit(solution)/shard_map/ppermute | solution.py:23
  142.7 7.5 %collective-permute-start.28 = (f32[2,3,128,128]{3,2,1,0:T(8,128)S(1)}, f32[2,3,128,128]{3,2,1,0:T(8,128)S(1)}, u32[]{:S(2)}, u32[]{:S(2)}) collective-permute-start(f32[2,3,128,128]{3,2,1,0:T(8,128)S(1)} %pad_maximum_fusion.2), channel_id=1, source_target_pairs={{0,8},{8,0},{16,24},{24,16},{1,9},{9,1},{17,25},{25,17},{2,10},{10... | collective-permute-start | bytes 1179656 | tf_op jit(solution)/shard_map/ppermute | solution.py:23
  145.7 6.7 %collective-permute-start.30 = (f32[128,128]{1,0:T(8,128)S(1)}, f32[128,128]{1,0:T(8,128)S(1)}, u32[]{:S(2)}, u32[]{:S(2)}) collective-permute-start(f32[128,128]{1,0:T(8,128)S(1)} %get-tuple-element.153), channel_id=1, source_target_pairs={{0,2},{1,3},{2,0},{3,1},{4,6},{5,7},{6,4},{7,5},{8,10},{9,11},{10,... | collective-permute-start | bytes 196616 | tf_op jit(solution)/shard_map/ppermute | solution.py:23
  147.3 6.5 %collective-permute-start.31 = (f32[128,128]{1,0:T(8,128)S(1)}, f32[128,128]{1,0:T(8,128)S(1)}, u32[]{:S(2)}, u32[]{:S(2)}) collective-permute-start(f32[128,128]{1,0:T(8,128)S(1)} %get-tuple-element.152), channel_id=1, source_target_pairs={{0,4},{1,5},{2,6},{3,7},{4,0},{5,1},{6,2},{7,3},{8,12},{9,13},{10,... | collective-permute-start | bytes 196616 | tf_op jit(solution)/shard_map/ppermute | solution.py:23
  149.9 6.1 %collective-permute-start.32 = (f32[128,128]{1,0:T(8,128)S(1)}, f32[128,128]{1,0:T(8,128)S(1)}, u32[]{:S(2)}, u32[]{:S(2)}) collective-permute-start(f32[128,128]{1,0:T(8,128)S(1)} %get-tuple-element.151), channel_id=1, source_target_pairs={{0,6},{1,7},{2,4},{3,5},{4,2},{5,3},{6,0},{7,1},{8,14},{9,15},{10,... | collective-permute-start | bytes 196616 | tf_op jit(solution)/shard_map/ppermute | solution.py:23
  (15 other events, 97.0 us)

commit v4 on v3

--- a/solution.py
+++ b/solution.py
@@ -10,6 +10,7 @@
 LANES = 128
 BF = jnp.bfloat16
 F32 = jnp.float32
+PLACE = 16
 LIGHT = pl.CostEstimate(flops=1, bytes_accessed=1, transcendentals=0)
 KINDS = tuple((outer, inner) for outer in (1, 2, 3) for inner in (1, 2, 3))
 MEMBERS = {1: (1,), 2: (0, 1), 3: (0,)}
@@ -30,6 +31,14 @@
 def reversed_bits(n):
     bits = bit_count(n)
     return [sum(((i >> b) & 1) << (bits - 1 - b) for b in range(bits)) for i in range(n)]
+
+
+def owner_of(own_ref):
+    return own_ref[0] & ((1 << PLACE) - 1)
+
+
+def column_of(own_ref):
+    return own_ref[0] >> PLACE
 
 
 def split(v):
@@ -108,7 +117,7 @@
 def write_slots(y, block, own_ref, keep_ref, send_ref, slices):
     width = y.shape[1] // slices
     half = slices // 2
-    core, side = own_ref[0] & 1, own_ref[1] & 1
+    core, side = owner_of(own_ref) & 1, column_of(own_ref) & 1
     for b in range(y.shape[0] // block):
         rows = y[b * block : (b + 1) * block]
         for i, p in enumerate(reversed_bits(slices)):
@@ -158,7 +167,7 @@
         def get(i):
             return history_ref[i] if i >= 0 else jnp.zeros(history_ref.shape[1:], F32)
 
-        prepare_sources(KINDS, get, own_ref[0], slices, a_ref.shape[0], hi_ref, lo_ref)
+        prepare_sources(KINDS, get, owner_of(own_ref), slices, a_ref.shape[0], hi_ref, lo_ref)
 
     fetch(step).wait()
     a_ref = tiles_ref.at[step % 2]
@@ -178,7 +187,7 @@
     width = tail_ref.shape[2] // slices
     small = block * width // LANES
     half = slices // 2
-    x = jnp.concatenate([flipped(tail_ref[back - count + j], own_ref[0], slices) for j in range(count)], axis=0)
+    x = jnp.concatenate([flipped(tail_ref[back - count + j], owner_of(own_ref), slices) for j in range(count)], axis=0)
     x_hi, x_lo = split(x)
     for c in range(matrices[0].shape[1] // block):
         m_hi, m_lo = split(jnp.concatenate([r[0, c * block : (c + 1) * block, :] for r in matrices], axis=1))
@@ -271,12 +280,12 @@
 
 def merge_kernel(own_ref, a_ref, *out_refs):
     for d, out_ref in enumerate(out_refs):
-        out_ref[...] = a_ref[(own_ref[1] >> 1) ^ d]
+        out_ref[...] = a_ref[(column_of(own_ref) >> 1) ^ d]
 
 
 def chain_kernel(own_ref, e_ref, a_ref, b_ref, m_ref, got_ref, *refs, width):
     parts, (x_ref, keep_ref, send_ref) = refs[:-3], refs[-3:]
-    core, own = own_ref[0] & 1, own_ref[1]
+    core, own = owner_of(own_ref) & 1, column_of(own_ref)
     total = parts[0][...]
     for part in parts[1:]:
         total = total + part[...]
@@ -298,11 +307,11 @@
     out_ref, terms = refs[-1], [refs[i : i + 3] for i in range(0, len(refs) - 1, 3)]
     half = acc_ref.shape[0]
 
-    @pl.when(own_ref[0] >= 2)
+    @pl.when(owner_of(own_ref) >= 2)
     def _():
         out_ref[...] = acc_ref[...]
 
-    @pl.when(own_ref[0] < 2)
+    @pl.when(owner_of(own_ref) < 2)
     def _():
         rows, block = terms[0][0].shape
         small = block * width // LANES
@@ -311,7 +320,7 @@
             y = None
             at = slice(c * block, (c + 1) * block)
             for (mine_ref, got_ref, _), (x_hi, x_lo) in zip(terms, sources, strict=True):
-                m_hi, m_lo = split(jnp.where((own_ref[0] & 1) == 1, got_ref[at], mine_ref[at]))
+                m_hi, m_lo = split(jnp.where((owner_of(own_ref) & 1) == 1, got_ref[at], mine_ref[at]))
                 term = dot(m_hi, x_hi) + dot(m_hi, x_lo) + dot(m_lo, x_hi)
                 y = term if y is None else y + term
             for p in range(half):
@@ -322,7 +331,7 @@
 def fields_kernel(own_ref, e_ref, out_ref, *, slices):
     width = e_ref.shape[2] // slices
     for n in range(e_ref.shape[0]):
-        out_ref[n] = folded(flipped(e_ref[n], own_ref[0], slices)[:, :width])
+        out_ref[n] = folded(flipped(e_ref[n], owner_of(own_ref), slices)[:, :width])
 
 
 def assemble_kernel(own_ref, parts_ref, *refs, slices):
@@ -333,7 +342,7 @@
         pieces = [None] * slices
         for i, p in enumerate(order):
             pieces[p] = unfolded(parts_ref[i, n], width)
-        out_ref[n] = flipped(jnp.concatenate(pieces, axis=1), own_ref[0], slices)
+        out_ref[n] = flipped(jnp.concatenate(pieces, axis=1), owner_of(own_ref), slices)
 
 
 def assembled(own, every, shape, begin, onto=()):
@@ -381,7 +390,7 @@
     small = block * width // LANES
     bits = bit_count(owners)
     back = steps - 1
-    own = jnp.stack([owner, column]).astype(jnp.int32)
+    own = jnp.reshape(owner + (column << PLACE), (1,)).astype(jnp.int32)
     tiles = max(1, rows // 512)
     held = {}
 

time: 164 us -> 161 us (0.982)
  Pallas kernels: 70.8 us -> 65.8 us
    pallas_call x7, Pallas kernels: 11.2 us -> 7.39 us  [whole_call(): pl.pallas_call(kernel, in_specs=[smem()] + [vmem] * (len(args) - 1), out_...]
  transfers between devices with their start and end apart: 35 -> 35, of which waited for: 19 -> 20; matrix products, arithmetic and copies ran while one was open for 1% -> 1% of each run, Pallas kernels for 37% -> 36%
where the time goes in v4:
time: 161 us; the launch traced here: 160 us
  Pallas kernels  65.8 us (41%)
  waiting for transfers between devices  48.1 us (30%)
  starting transfers between devices  39 us (24%)
  other arithmetic  4.18 us (3%)
  local copies, waits for them, and re-layouts  2.78 us (2%)
    ppermute x28, waiting for transfers between devices, exchanged(): return lax.ppermute(value, axis, swap_pairs(axis, bit))  41.7 us
    pallas_call x1, Pallas kernels, bulk(): pl.pallas_call(functools.partial(bulk_kernel, slices=slices, block=block)...  39.3 us
    ppermute x28, starting transfers between devices, exchanged(): return lax.ppermute(value, axis, swap_pairs(axis, bit))  25.3 us
    pallas_call x3, Pallas kernels, with_carried(): pl.pallas_call(functools.partial(carried_kernel, slices=slices), grid=(1,...  13.1 us
    pallas_call x7, Pallas kernels, whole_call(): pl.pallas_call(kernel, in_specs=[smem()] + [vmem] * (len(args) - 1), out_...  7.39 us
    ppermute x2, waiting for transfers between devices, taken(): got = lax.ppermute(offer, ('lag', 'col'), stage_pairs(stage))  6.39 us
    ppermute x1, starting transfers between devices, local(): lax.ppermute(newest, 'lag', [(0, top)])  6.23 us
    pallas_call x1, Pallas kernels, staged(): pl.pallas_call(stage_kernel, grid=(1,), in_specs=[smem(), pl.BlockSpec((1...  3.44 us
  transfers between devices with their start and end apart: 35, of which 20 were waited for; matrix products, arithmetic and copies ran while one was open for 1% of the time, Pallas kernels for 36%

profile of v4, /device:TPU:0, one launch (start us, length us, event | category | flops | bytes accessed | tf_op | source)
XLA Modules:
  0.0 160.4 jit_solution(2642434190718798369)
XLA Ops:
  0.0 3.4 %stage.1 = (f32[2048,256]{1,0:T(8,128)}, f32[3,256,256]{2,1,0:T(8,128)}) custom-call(s32[1]{0:T(128)} %bitcast.own_ref, f32[16,2048,256]{2,1,0:T(8,128)} %refs_2_.3, f32[16,256,256]{2,1,0:T(8,128)} %refs_2_.2, f32[16,256,256]{2,1,0:T(8,128)} %refs_2_.2, f32[16,256,256]{2,1,0:T(8,128)} %refs_2_.2), custom_call_target="tpu_custom_call" | custom-call | flops 1 | bytes 1 | tf_op jit(solution)/shard_map/stage/pallas_call | solution.py:268
  3.4 6.2 %collective-permute-start = (f32[2048,256]{1,0:T(8,128)}, f32[2048,256]{1,0:T(8,128)}, u32[]{:S(2)}, u32[]{:S(2)}) collective-permute-start(f32[2048,256]{1,0:T(8,128)} %get-tuple-element.88), channel_id=1, source_target_pairs={{0,16},{1,17},{2,18},{3,19},{4,20},{5,21},{6,22},{7,23}} | collective-permute-start | bytes 6291464 | tf_op jit(solution)/shard_map/ppermute | solution.py:443
  11.0 39.3 %bulk.1 = (f32[4,4,128,128]{3,2,1,0:T(8,128)}, f32[4,4,128,128]{3,2,1,0:T(8,128)}, f32[2,1024,128]{2,1,0:T(8,128)}, f32[2,1024,128]{2,1,0:T(8,128)}, f32[2,1024,...) custom-call(s32[1]{0:T(128)} %bitcast.own_ref, ...), custom_call_target="tpu_custom_call" | custom-call | flops 38654705664 | bytes 33554432 | tf_op jit(solution)/shard_map/bulk/pallas_call | solution.py:232
  56.3 3.0 %carried.3 = (f32[2,1024,128]{2,1,0:T(8,128)S(1)}, f32[2,1024,128]{2,1,0:T(8,128)S(1)}) custom-call(s32[1]{0:T(128)} %bitcast.own_ref, f32[3,256,256]{2,1,0:T(8,128)S(1)} %collective-permute-done.1.tail_ref, f32[2,1024,128]{2,1,0:T(8,128)S(1)} %copy-done.4, f32[2,1024,128]{2,1,0:T(8,128)S(1)} %copy-done.5, f32[16,2048,256]{2,1,0:T(8,128)} %refs_2_.3), custom_call_target="tpu_custom_call" | custom-call | flops 1 | bytes 1 | tf_op jit(solution)/shard_map/carried/pallas_call | solution.py:203
  59.6 4.4 %collective-permute-done.3 = f32[2,4,128,128]{3,2,1,0:T(8,128)S(1)} collective-permute-done((f32[2,4,128,128]{3,2,1,0:T(8,128)S(1)}, f32[2,4,128,128]{3,2,1,0:T(8,128)S(1)}, u32[]{:S(2)}, u32[]{:S(2)}) %collective-permute-start.3) | collective-permute-done | bytes 524320 | tf_op jit(solution)/shard_map/ppermute | solution.py:410
  66.6 4.3 %carried.4 = (f32[2,1024,128]{2,1,0:T(8,128)S(1)}, f32[2,1024,128]{2,1,0:T(8,128)S(1)}) custom-call(s32[1]{0:T(128)} %bitcast.own_ref, f32[3,256,256]{2,1,0:T(8,128)S(1)} %collective-permute-done.1.tail_ref, f32[2,1024,128]{2,1,0:T(8,128)S(1)} %copy-done.7, f32[2,1024,128]{2,1,0:T(8,128)S(1)} %copy-done.8, f32[16,2048,256]{2,1,0:T(8,128)} %refs_2_.3, ...), custom_call_target="tpu_custom_call" | custom-call | flops 1 | bytes 1 | tf_op jit(solution)/shard_map/carried/pallas_call | solution.py:203
  70.9 2.0 %collective-permute-done.4 = f32[1,4,128,128]{3,2,1,0:T(8,128)S(1)} collective-permute-done((f32[1,4,128,128]{3,2,1,0:T(8,128)S(1)}, f32[1,4,128,128]{3,2,1,0:T(8,128)S(1)}, u32[]{:S(2)}, u32[]{:S(2)}) %collective-permute-start.4) | collective-permute-done | bytes 262176 | tf_op jit(solution)/shard_map/ppermute | solution.py:410
  74.4 2.7 %collective-permute-start.10 = (f32[128,128]{1,0:T(8,128)S(1)}, f32[128,128]{1,0:T(8,128)S(1)}, u32[]{:S(2)}, u32[]{:S(2)}) collective-permute-start(f32[128,128]{1,0:T(8,128)S(1)} %get-tuple-element.109), channel_id=1, source_target_pairs={{0,4},{1,5},{2,6},{3,7},{4,0},{5,1},{6,2},{7,3},{8,12},{9,13},{10,... | collective-permute-start | bytes 196616 | tf_op jit(solution)/shard_map/ppermute | solution.py:24
  78.7 5.8 %carried.5 = (f32[2,1024,128]{2,1,0:T(8,128)S(1)}, f32[2,1024,128]{2,1,0:T(8,128)S(1)}) custom-call(s32[1]{0:T(128)} %bitcast.own_ref, f32[3,256,256]{2,1,0:T(8,128)S(1)} %collective-permute-done.1.tail_ref, f32[2,1024,128]{2,1,0:T(8,128)S(1)} %copy-done.2, f32[2,1024,128]{2,1,0:T(8,128)S(1)} %copy-done.3, f32[16,2048,256]{2,1,0:T(8,128)} %refs_2_.3, ...), custom_call_target="tpu_custom_call" | custom-call | flops 1 | bytes 1 | tf_op jit(solution)/shard_map/carried/pallas_call | solution.py:203
  84.6 4.1 %collective-permute-done.8 = f32[1,1024,128]{2,1,0:T(8,128)S(1)} collective-permute-done((f32[1,1024,128]{2,1,0:T(8,128)S(1)}, f32[1,1024,128]{2,1,0:T(8,128)S(1)}, u32[]{:S(2)}, u32[]{:S(2)}) %collective-permute-start.8) | collective-permute-done | bytes 524320 | tf_op jit(solution)/shard_map/ppermute | solution.py:24
  90.3 1.7 %collective-permute-start.13 = (f32[2048,256]{1,0:T(8,128)S(1)}, f32[2048,256]{1,0:T(8,128)S(1)}, u32[]{:S(2)}, u32[]{:S(2)}) collective-permute-start(f32[2048,256]{1,0:T(8,128)S(1)} %copy-done), channel_id=1, source_target_pairs={{0,8},{1,9},{2,10},{3,11},{4,12},{5,13},{6,14},{7,15}} | collective-permute-start | bytes 6291464 | tf_op jit(solution)/shard_map/ppermute | solution.py:501
  93.7 2.9 %collective-permute-done.12 = f32[1,128,128]{2,1,0:T(8,128)S(1)} collective-permute-done((f32[1,128,128]{2,1,0:T(8,128)S(1)}, f32[1,128,128]{2,1,0:T(8,128)S(1)}, u32[]{:S(2)}, u32[]{:S(2)}) %collective-permute-start.12) | collective-permute-done | bytes 65568 | tf_op jit(solution)/shard_map/ppermute | solution.py:24
  98.3 2.5 %collective-permute-done.15 = f32[4,128,128]{2,1,0:T(8,128)S(1)} collective-permute-done((f32[4,128,128]{2,1,0:T(8,128)S(1)}, f32[4,128,128]{2,1,0:T(8,128)S(1)}, u32[]{:S(2)}, u32[]{:S(2)}) %collective-permute-start.15) | collective-permute-done | bytes 262176 | tf_op jit(solution)/shard_map/ppermute | solution.py:24
  100.8 1.6 %collective-permute-start.16 = (f32[128,128]{1,0:T(8,128)S(1)}, f32[128,128]{1,0:T(8,128)S(1)}, u32[]{:S(2)}, u32[]{:S(2)}) collective-permute-start(f32[128,128]{1,0:T(8,128)S(1)} %get-tuple-element.161), channel_id=1, source_target_pairs={{0,2},{1,3},{2,0},{3,1},{4,6},{5,7},{6,4},{7,5},{8,10},{9,11},{10,... | collective-permute-start | bytes 196616 | tf_op jit(solution)/shard_map/ppermute | solution.py:24
  102.5 2.6 %collective-permute-start.17 = (f32[128,128]{1,0:T(8,128)S(1)}, f32[128,128]{1,0:T(8,128)S(1)}, u32[]{:S(2)}, u32[]{:S(2)}) collective-permute-start(f32[128,128]{1,0:T(8,128)S(1)} %get-tuple-element.160), channel_id=1, source_target_pairs={{0,4},{1,5},{2,6},{3,7},{4,0},{5,1},{6,2},{7,3},{8,12},{9,13},{10,... | collective-permute-start | bytes 196616 | tf_op jit(solution)/shard_map/ppermute | solution.py:24
  105.4 4.0 %collective-permute-done.17.refs_2_ = f32[128,128]{1,0:T(8,128)S(1)} collective-permute-done((f32[128,128]{1,0:T(8,128)S(1)}, f32[128,128]{1,0:T(8,128)S(1)}, u32[]{:S(2)}, u32[]{:S(2)}) %collective-permute-start.17) | collective-permute-done | bytes 65568 | tf_op jit(solution)/shard_map/ppermute | solution.py:24
  109.5 1.7 %collective-permute-done.18.refs_3_ = f32[128,128]{1,0:T(8,128)S(1)} collective-permute-done((f32[128,128]{1,0:T(8,128)S(1)}, f32[128,128]{1,0:T(8,128)S(1)}, u32[]{:S(2)}, u32[]{:S(2)}) %collective-permute-start.18) | collective-permute-done | bytes 65568 | tf_op jit(solution)/shard_map/ppermute | solution.py:24
  116.8 2.3 %collective-permute-done.20 = f32[1,128,128]{2,1,0:T(8,128)S(1)} collective-permute-done((f32[1,128,128]{2,1,0:T(8,128)S(1)}, f32[1,128,128]{2,1,0:T(8,128)S(1)}, u32[]{:S(2)}, u32[]{:S(2)}) %collective-permute-start.20) | collective-permute-done | bytes 65568 | tf_op jit(solution)/shard_map/ppermute | solution.py:24
  119.1 2.2 %late.3 = f32[2,1024,128]{2,1,0:T(8,128)S(1)} custom-call(s32[1]{0:T(128)} %bitcast.own_ref, f32[2,1024,128]{2,1,0:T(8,128)S(1)} %add.72.acc_ref, f32[2048,256]{1,0:T(8,128)S(1)} %copy-done, f32[2048,256]{1,0:T(8,128)S(1)} %collective-permute-done.13.refs_1_, f32[2,128,128]{2,1,0:T(8,128)S(1)} %get-tuple-element.169.refs_2_, f32[2048,256]{1,0:T(8,128)S(1)} %copy-done.1, ...), custom_call_target="tpu_custom_call" | custom-call | flops 1 | bytes 1 | tf_op jit(solution)/shard_map/late/pallas_call | solution.py:367
  121.8 1.6 %collective-permute-start.24 = (f32[128,128]{1,0:T(8,128)S(1)}, f32[128,128]{1,0:T(8,128)S(1)}, u32[]{:S(2)}, u32[]{:S(2)}) collective-permute-start(f32[128,128]{1,0:T(8,128)S(1)} %get-tuple-element.157), channel_id=1, source_target_pairs={{0,2},{1,3},{2,0},{3,1},{4,6},{5,7},{6,4},{7,5},{8,10},{9,11},{10,... | collective-permute-start | bytes 196616 | tf_op jit(solution)/shard_map/ppermute | solution.py:24
  123.5 2.6 %collective-permute-start.25 = (f32[128,128]{1,0:T(8,128)S(1)}, f32[128,128]{1,0:T(8,128)S(1)}, u32[]{:S(2)}, u32[]{:S(2)}) collective-permute-start(f32[128,128]{1,0:T(8,128)S(1)} %get-tuple-element.156), channel_id=1, source_target_pairs={{0,4},{1,5},{2,6},{3,7},{4,0},{5,1},{6,2},{7,3},{8,12},{9,13},{10,... | collective-permute-start | bytes 196616 | tf_op jit(solution)/shard_map/ppermute | solution.py:24
  126.3 4.0 %collective-permute-done.25.refs_2_ = f32[128,128]{1,0:T(8,128)S(1)} collective-permute-done((f32[128,128]{1,0:T(8,128)S(1)}, f32[128,128]{1,0:T(8,128)S(1)}, u32[]{:S(2)}, u32[]{:S(2)}) %collective-permute-start.25) | collective-permute-done | bytes 65568 | tf_op jit(solution)/shard_map/ppermute | solution.py:24
  130.3 1.8 %collective-permute-done.26.refs_3_ = f32[128,128]{1,0:T(8,128)S(1)} collective-permute-done((f32[128,128]{1,0:T(8,128)S(1)}, f32[128,128]{1,0:T(8,128)S(1)}, u32[]{:S(2)}, u32[]{:S(2)}) %collective-permute-start.26) | collective-permute-done | bytes 65568 | tf_op jit(solution)/shard_map/ppermute | solution.py:24
  132.1 2.8 %collective-permute-done.22 = f32[1,1024,128]{2,1,0:T(8,128)S(1)} collective-permute-done((f32[1,1024,128]{2,1,0:T(8,128)S(1)}, f32[1,1024,128]{2,1,0:T(8,128)S(1)}, u32[]{:S(2)}, u32[]{:S(2)}) %collective-permute-start.22) | collective-permute-done | bytes 524320 | tf_op jit(solution)/shard_map/ppermute | solution.py:24
  137.8 2.5 %collective-permute-done.27 = f32[1,128,128]{2,1,0:T(8,128)S(1)} collective-permute-done((f32[1,128,128]{2,1,0:T(8,128)S(1)}, f32[1,128,128]{2,1,0:T(8,128)S(1)}, u32[]{:S(2)}, u32[]{:S(2)}) %collective-permute-start.27) | collective-permute-done | bytes 65568 | tf_op jit(solution)/shard_map/ppermute | solution.py:24
  140.4 2.9 %collective-permute-done.29 = f32[4,128,128]{2,1,0:T(8,128)S(1)} collective-permute-done((f32[4,128,128]{2,1,0:T(8,128)S(1)}, f32[4,128,128]{2,1,0:T(8,128)S(1)}, u32[]{:S(2)}, u32[]{:S(2)}) %collective-permute-start.29) | collective-permute-done | bytes 262176 | tf_op jit(solution)/shard_map/ppermute | solution.py:24
  143.3 1.6 %collective-permute-start.30 = (f32[128,128]{1,0:T(8,128)S(1)}, f32[128,128]{1,0:T(8,128)S(1)}, u32[]{:S(2)}, u32[]{:S(2)}) collective-permute-start(f32[128,128]{1,0:T(8,128)S(1)} %get-tuple-element.153), channel_id=1, source_target_pairs={{0,2},{1,3},{2,0},{3,1},{4,6},{5,7},{6,4},{7,5},{8,10},{9,11},{10,... | collective-permute-start | bytes 196616 | tf_op jit(solution)/shard_map/ppermute | solution.py:24
  145.0 2.6 %collective-permute-start.31 = (f32[128,128]{1,0:T(8,128)S(1)}, f32[128,128]{1,0:T(8,128)S(1)}, u32[]{:S(2)}, u32[]{:S(2)}) collective-permute-start(f32[128,128]{1,0:T(8,128)S(1)} %get-tuple-element.152), channel_id=1, source_target_pairs={{0,4},{1,5},{2,6},{3,7},{4,0},{5,1},{6,2},{7,3},{8,12},{9,13},{10,... | collective-permute-start | bytes 196616 | tf_op jit(solution)/shard_map/ppermute | solution.py:24
  147.9 1.6 %assemble.2.refs_0_ = f32[4,256,256]{2,1,0:T(8,128)} custom-call(s32[1]{0:T(128)} %bitcast.own_ref, f32[4,3,128,128]{3,2,1,0:T(8,128)S(1)} %pad_maximum_fusion.parts_ref), custom_call_target="tpu_custom_call" | custom-call | flops 1 | bytes 1 | tf_op jit(solution)/shard_map/assemble/pallas_call | solution.py:351
  149.5 2.0 %collective-permute-done.31 = f32[128,128]{1,0:T(8,128)S(1)} collective-permute-done((f32[128,128]{1,0:T(8,128)S(1)}, f32[128,128]{1,0:T(8,128)S(1)}, u32[]{:S(2)}, u32[]{:S(2)}) %collective-permute-start.31) | collective-permute-done | bytes 65568 | tf_op jit(solution)/shard_map/ppermute | solution.py:24
  151.5 2.2 %collective-permute-done.32 = f32[128,128]{1,0:T(8,128)S(1)} collective-permute-done((f32[128,128]{1,0:T(8,128)S(1)}, f32[128,128]{1,0:T(8,128)S(1)}, u32[]{:S(2)}, u32[]{:S(2)}) %collective-permute-start.32) | collective-permute-done | bytes 65568 | tf_op jit(solution)/shard_map/ppermute | solution.py:24
  155.2 2.8 %collective-permute-done.33 = f32[1,128,128]{2,1,0:T(8,128)S(1)} collective-permute-done((f32[1,128,128]{2,1,0:T(8,128)S(1)}, f32[1,128,128]{2,1,0:T(8,128)S(1)}, u32[]{:S(2)}, u32[]{:S(2)}) %collective-permute-start.33) | collective-permute-done | bytes 65568 | tf_op jit(solution)/shard_map/ppermute | solution.py:24
  (100 shorter events, 32.1 us)
Async XLA Ops:
  3.4 46.9 %collective-permute-start = (f32[2048,256]{1,0:T(8,128)}, f32[2048,256]{1,0:T(8,128)}, u32[]{:S(2)}, u32[]{:S(2)}) collective-permute-start(f32[2048,256]{1,0:T(8,128)} %get-tuple-element.88), channel_id=1, source_target_pairs={{0,16},{1,17},{2,18},{3,19},{4,20},{5,21},{6,22},{7,23}} | collective-permute-start | bytes 6291464 | tf_op jit(solution)/shard_map/ppermute | solution.py:443
  9.7 40.7 %collective-permute-start.1 = (f32[3,256,256]{2,1,0:T(8,128)}, f32[3,256,256]{2,1,0:T(8,128)S(1)}, u32[]{:S(2)}, u32[]{:S(2)}) collective-permute-start(f32[3,256,256]{2,1,0:T(8,128)} %get-tuple-element.77), channel_id=1, source_target_pairs={{0,8},{8,16},{16,24},{1,9},{9,17},{17,25},{2,10},{10,18},{18,26},{... | collective-permute-start | bytes 2359304 | tf_op jit(solution)/shard_map/ppermute | solution.py:444
  54.7 9.2 %collective-permute-start.3 = (f32[2,4,128,128]{3,2,1,0:T(8,128)S(1)}, f32[2,4,128,128]{3,2,1,0:T(8,128)S(1)}, u32[]{:S(2)}, u32[]{:S(2)}) collective-permute-start(f32[2,4,128,128]{3,2,1,0:T(8,128)S(1)} %pad_maximum_fusion.1), channel_id=1, source_target_pairs={{0,1},{1,0},{2,3},{3,2},{4,5},{5,4},{6,7},{7,6},{8,24},{9,25},{10,... | collective-permute-start | bytes 1572872 | tf_op jit(solution)/shard_map/ppermute | solution.py:410
  65.0 9.0 %collective-permute-start.5 = (f32[2048,256]{1,0:T(8,128)S(1)}, f32[2048,256]{1,0:T(8,128)S(1)}, u32[]{:S(2)}, u32[]{:S(2)}) collective-permute-start(f32[2048,256]{1,0:T(8,128)S(1)} %broadcast_select_fusion.m_ref), channel_id=1, source_target_pairs={{0,8},{16,24},{1,9},{17,25},{2,10},{18,26},{3,11},{19,27},{4,12},{... | collective-permute-start | bytes 6291464 | tf_op jit(solution)/shard_map/ppermute | solution.py:465
  66.4 7.6 %collective-permute-start.7 = (f32[2,1024,128]{2,1,0:T(8,128)S(1)}, f32[2,1024,128]{2,1,0:T(8,128)S(1)}, u32[]{:S(2)}, u32[]{:S(2)}) collective-permute-start(f32[2,1024,128]{2,1,0:T(8,128)S(1)} %get-tuple-element.105), channel_id=1, source_target_pairs={{0,8},{8,0},{16,24},{24,16},{1,9},{9,1},{17,25},{25,17},{2,10},{10... | collective-permute-start | bytes 3145736 | tf_op jit(solution)/shard_map/ppermute | solution.py:24
  66.5 6.4 %collective-permute-start.4 = (f32[1,4,128,128]{3,2,1,0:T(8,128)S(1)}, f32[1,4,128,128]{3,2,1,0:T(8,128)S(1)}, u32[]{:S(2)}, u32[]{:S(2)}) collective-permute-start(f32[1,4,128,128]{3,2,1,0:T(8,128)S(1)} %slice_add_fusion.2), channel_id=1, source_target_pairs={{0,16},{1,17},{2,18},{3,19},{4,20},{5,21},{6,22},{7,23},{8,9},{9,8... | collective-permute-start | bytes 786440 | tf_op jit(solution)/shard_map/ppermute | solution.py:410
  74.0 10.5 %collective-permute-start.6 = (f32[2,1024,128]{2,1,0:T(8,128)S(1)}, f32[2,1024,128]{2,1,0:T(8,128)S(1)}, u32[]{:S(2)}, u32[]{:S(2)}) collective-permute-start(f32[2,1024,128]{2,1,0:T(8,128)S(1)} %get-tuple-element.102), channel_id=1, source_target_pairs={{0,8},{8,0},{16,24},{24,16},{1,9},{9,1},{17,25},{25,17},{2,10},{10... | collective-permute-start | bytes 3145736 | tf_op jit(solution)/shard_map/ppermute | solution.py:24
  74.3 14.4 %collective-permute-start.8 = (f32[1,1024,128]{2,1,0:T(8,128)S(1)}, f32[1,1024,128]{2,1,0:T(8,128)S(1)}, u32[]{:S(2)}, u32[]{:S(2)}) collective-permute-start(f32[1,1024,128]{2,1,0:T(8,128)S(1)} %get-tuple-element.149), channel_id=1, source_target_pairs={{0,16},{8,24},{16,0},{24,8},{1,17},{9,25},{17,1},{25,9},{2,18},{10... | collective-permute-start | bytes 1572872 | tf_op jit(solution)/shard_map/ppermute | solution.py:24
  74.4 14.3 %collective-permute-start.10 = (f32[128,128]{1,0:T(8,128)S(1)}, f32[128,128]{1,0:T(8,128)S(1)}, u32[]{:S(2)}, u32[]{:S(2)}) collective-permute-start(f32[128,128]{1,0:T(8,128)S(1)} %get-tuple-element.109), channel_id=1, source_target_pairs={{0,4},{1,5},{2,6},{3,7},{4,0},{5,1},{6,2},{7,3},{8,12},{9,13},{10,... | collective-permute-start | bytes 196616 | tf_op jit(solution)/shard_map/ppermute | solution.py:24
  77.0 11.6 %collective-permute-start.11 = (f32[128,128]{1,0:T(8,128)S(1)}, f32[128,128]{1,0:T(8,128)S(1)}, u32[]{:S(2)}, u32[]{:S(2)}) collective-permute-start(f32[128,128]{1,0:T(8,128)S(1)} %get-tuple-element.110), channel_id=1, source_target_pairs={{0,6},{1,7},{2,4},{3,5},{4,2},{5,3},{6,0},{7,1},{8,14},{9,15},{10,... | collective-permute-start | bytes 196616 | tf_op jit(solution)/shard_map/ppermute | solution.py:24
  78.4 10.3 %collective-permute-start.9 = (f32[128,128]{1,0:T(8,128)S(1)}, f32[128,128]{1,0:T(8,128)S(1)}, u32[]{:S(2)}, u32[]{:S(2)}) collective-permute-start(f32[128,128]{1,0:T(8,128)S(1)} %get-tuple-element.108), channel_id=1, source_target_pairs={{0,2},{1,3},{2,0},{3,1},{4,6},{5,7},{6,4},{7,5},{8,10},{9,11},{10,... | collective-permute-start | bytes 196616 | tf_op jit(solution)/shard_map/ppermute | solution.py:24
  90.3 6.3 %collective-permute-start.13 = (f32[2048,256]{1,0:T(8,128)S(1)}, f32[2048,256]{1,0:T(8,128)S(1)}, u32[]{:S(2)}, u32[]{:S(2)}) collective-permute-start(f32[2048,256]{1,0:T(8,128)S(1)} %copy-done), channel_id=1, source_target_pairs={{0,8},{1,9},{2,10},{3,11},{4,12},{5,13},{6,14},{7,15}} | collective-permute-start | bytes 6291464 | tf_op jit(solution)/shard_map/ppermute | solution.py:501
  92.0 13.3 %collective-permute-start.19 = (f32[2,1024,128]{2,1,0:T(8,128)S(1)}, f32[2,1024,128]{2,1,0:T(8,128)S(1)}, u32[]{:S(2)}, u32[]{:S(2)}) collective-permute-start(f32[2,1024,128]{2,1,0:T(8,128)S(1)} %get-tuple-element.129), channel_id=1, source_target_pairs={{0,8},{8,0},{16,24},{24,16},{1,9},{9,1},{17,25},{25,17},{2,10},{10... | collective-permute-start | bytes 3145736 | tf_op jit(solution)/shard_map/ppermute | solution.py:24
  92.1 4.5 %collective-permute-start.12 = (f32[1,128,128]{2,1,0:T(8,128)S(1)}, f32[1,128,128]{2,1,0:T(8,128)S(1)}, u32[]{:S(2)}, u32[]{:S(2)}) collective-permute-start(f32[1,128,128]{2,1,0:T(8,128)S(1)} %bitcast.66), channel_id=1, source_target_pairs={{0,16},{8,24},{16,0},{24,8},{1,17},{9,25},{17,1},{25,9},{2,18},{10... | collective-permute-start | bytes 196616 | tf_op jit(solution)/shard_map/ppermute | solution.py:24
  92.2 8.6 %collective-permute-start.15 = (f32[4,128,128]{2,1,0:T(8,128)S(1)}, f32[4,128,128]{2,1,0:T(8,128)S(1)}, u32[]{:S(2)}, u32[]{:S(2)}) collective-permute-start(f32[4,128,128]{2,1,0:T(8,128)S(1)} %get-tuple-element.125), channel_id=1, source_target_pairs={{0,1},{1,0},{2,3},{3,2},{4,5},{5,4},{6,7},{7,6},{8,9},{9,8},{10,11... | collective-permute-start | bytes 786440 | tf_op jit(solution)/shard_map/ppermute | solution.py:24
  98.2 13.6 %collective-permute-start.14 = (f32[1,1024,128]{2,1,0:T(8,128)S(1)}, f32[1,1024,128]{2,1,0:T(8,128)S(1)}, u32[]{:S(2)}, u32[]{:S(2)}) collective-permute-start(f32[1,1024,128]{2,1,0:T(8,128)S(1)} %get-tuple-element.147), channel_id=1, source_target_pairs={{0,16},{8,24},{16,0},{24,8},{1,17},{9,25},{17,1},{25,9},{2,18},{10... | collective-permute-start | bytes 1572872 | tf_op jit(solution)/shard_map/ppermute | solution.py:24
  100.8 4.6 %collective-permute-start.16 = (f32[128,128]{1,0:T(8,128)S(1)}, f32[128,128]{1,0:T(8,128)S(1)}, u32[]{:S(2)}, u32[]{:S(2)}) collective-permute-start(f32[128,128]{1,0:T(8,128)S(1)} %get-tuple-element.161), channel_id=1, source_target_pairs={{0,2},{1,3},{2,0},{3,1},{4,6},{5,7},{6,4},{7,5},{8,10},{9,11},{10,... | collective-permute-start | bytes 196616 | tf_op jit(solution)/shard_map/ppermute | solution.py:24
  102.5 7.0 %collective-permute-start.17 = (f32[128,128]{1,0:T(8,128)S(1)}, f32[128,128]{1,0:T(8,128)S(1)}, u32[]{:S(2)}, u32[]{:S(2)}) collective-permute-start(f32[128,128]{1,0:T(8,128)S(1)} %get-tuple-element.160), channel_id=1, source_target_pairs={{0,4},{1,5},{2,6},{3,7},{4,0},{5,1},{6,2},{7,3},{8,12},{9,13},{10,... | collective-permute-start | bytes 196616 | tf_op jit(solution)/shard_map/ppermute | solution.py:24
  105.1 6.1 %collective-permute-start.18 = (f32[128,128]{1,0:T(8,128)S(1)}, f32[128,128]{1,0:T(8,128)S(1)}, u32[]{:S(2)}, u32[]{:S(2)}) collective-permute-start(f32[128,128]{1,0:T(8,128)S(1)} %get-tuple-element.159), channel_id=1, source_target_pairs={{0,6},{1,7},{2,4},{3,5},{4,2},{5,3},{6,0},{7,1},{8,14},{9,15},{10,... | collective-permute-start | bytes 196616 | tf_op jit(solution)/shard_map/ppermute | solution.py:24
  113.3 5.8 %collective-permute-start.21 = (f32[2048,256]{1,0:T(8,128)S(1)}, f32[2048,256]{1,0:T(8,128)S(1)}, u32[]{:S(2)}, u32[]{:S(2)}) collective-permute-start(f32[2048,256]{1,0:T(8,128)S(1)} %copy-done.1), channel_id=1, source_target_pairs={{0,8},{1,9},{2,10},{3,11},{4,12},{5,13},{6,14},{7,15}} | collective-permute-start | bytes 6291464 | tf_op jit(solution)/shard_map/ppermute | solution.py:501
  114.8 4.3 %collective-permute-start.20 = (f32[1,128,128]{2,1,0:T(8,128)S(1)}, f32[1,128,128]{2,1,0:T(8,128)S(1)}, u32[]{:S(2)}, u32[]{:S(2)}) collective-permute-start(f32[1,128,128]{2,1,0:T(8,128)S(1)} %bitcast.68), channel_id=1, source_target_pairs={{0,16},{8,24},{16,0},{24,8},{1,17},{9,25},{17,1},{25,9},{2,18},{10... | collective-permute-start | bytes 196616 | tf_op jit(solution)/shard_map/ppermute | solution.py:24
  115.4 6.4 %collective-permute-start.23 = (f32[4,128,128]{2,1,0:T(8,128)S(1)}, f32[4,128,128]{2,1,0:T(8,128)S(1)}, u32[]{:S(2)}, u32[]{:S(2)}) collective-permute-start(f32[4,128,128]{2,1,0:T(8,128)S(1)} %get-tuple-element.134), channel_id=1, source_target_pairs={{0,1},{1,0},{2,3},{3,2},{4,5},{5,4},{6,7},{7,6},{8,9},{9,8},{10,11... | collective-permute-start | bytes 786440 | tf_op jit(solution)/shard_map/ppermute | solution.py:24
  121.4 13.5 %collective-permute-start.22 = (f32[1,1024,128]{2,1,0:T(8,128)S(1)}, f32[1,1024,128]{2,1,0:T(8,128)S(1)}, u32[]{:S(2)}, u32[]{:S(2)}) collective-permute-start(f32[1,1024,128]{2,1,0:T(8,128)S(1)} %get-tuple-element.145), channel_id=1, source_target_pairs={{0,16},{8,24},{16,0},{24,8},{1,17},{9,25},{17,1},{25,9},{2,18},{10... | collective-permute-start | bytes 1572872 | tf_op jit(solution)/shard_map/ppermute | solution.py:24
  121.8 4.5 %collective-permute-start.24 = (f32[128,128]{1,0:T(8,128)S(1)}, f32[128,128]{1,0:T(8,128)S(1)}, u32[]{:S(2)}, u32[]{:S(2)}) collective-permute-start(f32[128,128]{1,0:T(8,128)S(1)} %get-tuple-element.157), channel_id=1, source_target_pairs={{0,2},{1,3},{2,0},{3,1},{4,6},{5,7},{6,4},{7,5},{8,10},{9,11},{10,... | collective-permute-start | bytes 196616 | tf_op jit(solution)/shard_map/ppermute | solution.py:24
  123.5 6.8 %collective-permute-start.25 = (f32[128,128]{1,0:T(8,128)S(1)}, f32[128,128]{1,0:T(8,128)S(1)}, u32[]{:S(2)}, u32[]{:S(2)}) collective-permute-start(f32[128,128]{1,0:T(8,128)S(1)} %get-tuple-element.156), channel_id=1, source_target_pairs={{0,4},{1,5},{2,6},{3,7},{4,0},{5,1},{6,2},{7,3},{8,12},{9,13},{10,... | collective-permute-start | bytes 196616 | tf_op jit(solution)/shard_map/ppermute | solution.py:24
  126.0 6.1 %collective-permute-start.26 = (f32[128,128]{1,0:T(8,128)S(1)}, f32[128,128]{1,0:T(8,128)S(1)}, u32[]{:S(2)}, u32[]{:S(2)}) collective-permute-start(f32[128,128]{1,0:T(8,128)S(1)} %get-tuple-element.155), channel_id=1, source_target_pairs={{0,6},{1,7},{2,4},{3,5},{4,2},{5,3},{6,0},{7,1},{8,14},{9,15},{10,... | collective-permute-start | bytes 196616 | tf_op jit(solution)/shard_map/ppermute | solution.py:24
  136.3 7.0 %collective-permute-start.29 = (f32[4,128,128]{2,1,0:T(8,128)S(1)}, f32[4,128,128]{2,1,0:T(8,128)S(1)}, u32[]{:S(2)}, u32[]{:S(2)}) collective-permute-start(f32[4,128,128]{2,1,0:T(8,128)S(1)} %get-tuple-element.137), channel_id=1, source_target_pairs={{0,1},{1,0},{2,3},{3,2},{4,5},{5,4},{6,7},{7,6},{8,9},{9,8},{10,11... | collective-permute-start | bytes 786440 | tf_op jit(solution)/shard_map/ppermute | solution.py:24
  140.3 7.5 %collective-permute-start.28 = (f32[2,3,128,128]{3,2,1,0:T(8,128)S(1)}, f32[2,3,128,128]{3,2,1,0:T(8,128)S(1)}, u32[]{:S(2)}, u32[]{:S(2)}) collective-permute-start(f32[2,3,128,128]{3,2,1,0:T(8,128)S(1)} %pad_maximum_fusion.2), channel_id=1, source_target_pairs={{0,8},{8,0},{16,24},{24,16},{1,9},{9,1},{17,25},{25,17},{2,10},{10... | collective-permute-start | bytes 1179656 | tf_op jit(solution)/shard_map/ppermute | solution.py:24
  143.3 6.1 %collective-permute-start.30 = (f32[128,128]{1,0:T(8,128)S(1)}, f32[128,128]{1,0:T(8,128)S(1)}, u32[]{:S(2)}, u32[]{:S(2)}) collective-permute-start(f32[128,128]{1,0:T(8,128)S(1)} %get-tuple-element.153), channel_id=1, source_target_pairs={{0,2},{1,3},{2,0},{3,1},{4,6},{5,7},{6,4},{7,5},{8,10},{9,11},{10,... | collective-permute-start | bytes 196616 | tf_op jit(solution)/shard_map/ppermute | solution.py:24
  145.0 6.5 %collective-permute-start.31 = (f32[128,128]{1,0:T(8,128)S(1)}, f32[128,128]{1,0:T(8,128)S(1)}, u32[]{:S(2)}, u32[]{:S(2)}) collective-permute-start(f32[128,128]{1,0:T(8,128)S(1)} %get-tuple-element.152), channel_id=1, source_target_pairs={{0,4},{1,5},{2,6},{3,7},{4,0},{5,1},{6,2},{7,3},{8,12},{9,13},{10,... | collective-permute-start | bytes 196616 | tf_op jit(solution)/shard_map/ppermute | solution.py:24
  147.6 6.1 %collective-permute-start.32 = (f32[128,128]{1,0:T(8,128)S(1)}, f32[128,128]{1,0:T(8,128)S(1)}, u32[]{:S(2)}, u32[]{:S(2)}) collective-permute-start(f32[128,128]{1,0:T(8,128)S(1)} %get-tuple-element.151), channel_id=1, source_target_pairs={{0,6},{1,7},{2,4},{3,5},{4,2},{5,3},{6,0},{7,1},{8,14},{9,15},{10,... | collective-permute-start | bytes 196616 | tf_op jit(solution)/shard_map/ppermute | solution.py:24
  153.7 4.3 %collective-permute-start.33 = (f32[1,128,128]{2,1,0:T(8,128)S(1)}, f32[1,128,128]{2,1,0:T(8,128)S(1)}, u32[]{:S(2)}, u32[]{:S(2)}) collective-permute-start(f32[1,128,128]{2,1,0:T(8,128)S(1)} %fusion.2), channel_id=1, source_target_pairs={{0,16},{8,24},{16,0},{24,8},{1,17},{9,25},{17,1},{25,9},{2,18},{10... | collective-permute-start | bytes 196616 | tf_op jit(solution)/shard_map/ppermute | solution.py:24
  (14 other events, 56.5 us)

commit v5 on v4

--- a/solution.py
+++ b/solution.py
@@ -89,10 +89,11 @@
     return along(0) - along(-1)
 
 
-def prepare_sources(kinds, get, own, slices, groups, hi_ref, lo_ref):
+def prepare_sources(kinds, get, ready, own, slices, groups, hi_ref, lo_ref):
     block = hi_ref.shape[1] // groups
-    for i, (outer, inner) in enumerate(kinds):
-        for g in range(groups):
+    for g in range(groups):
+        ready(g)
+        for i, (outer, inner) in enumerate(kinds):
             hi, lo = split(flipped(source_sums(get, outer, inner, 4 * g), own, slices))
             hi_ref[i, g * block : (g + 1) * block, :] = hi
             lo_ref[i, g * block : (g + 1) * block, :] = lo
@@ -146,7 +147,7 @@
 
 
 def bulk_kernel(own_ref, history_ref, a_ref, *refs, slices, block):
-    outs, (second_ref, third_ref, hi_ref, lo_ref, tiles_ref, sems) = refs[:-6], refs[-6:]
+    outs, (second_ref, third_ref, hi_ref, lo_ref, tiles_ref, past_ref, sems, past_sems) = refs[:-8], refs[-8:]
     step, steps = pl.program_id(0), pl.num_programs(0)
     tile = tiles_ref.shape[4]
 
@@ -154,22 +155,29 @@
         rows = pl.ds(pl.multiple_of(i * tile, tile), tile)
         return pltpu.make_async_copy(a_ref.at[:, :, :, rows, :], tiles_ref.at[i % 2], sems.at[i % 2])
 
+    def fetch_past(g):
+        lags = pl.ds(4 * g, 4)
+        return pltpu.make_async_copy(history_ref.at[lags], past_ref.at[lags], past_sems.at[g])
+
     @pl.when(step == 0)
     def _():
+        for g in range(a_ref.shape[0]):
+            fetch_past(g).start()
         fetch(0).start()
+
+    @pl.when(step == 0)
+    def _():
+        def get(i):
+            return past_ref[i] if i >= 0 else jnp.zeros(past_ref.shape[1:], F32)
+
+        prepare_sources(KINDS, get, lambda g: fetch_past(g).wait(), owner_of(own_ref), slices, a_ref.shape[0], hi_ref, lo_ref)
+
+    fetch(step).wait()
 
     @pl.when(step + 1 < steps)
     def _():
         fetch(step + 1).start()
 
-    @pl.when(step == 0)
-    def _():
-        def get(i):
-            return history_ref[i] if i >= 0 else jnp.zeros(history_ref.shape[1:], F32)
-
-        prepare_sources(KINDS, get, owner_of(own_ref), slices, a_ref.shape[0], hi_ref, lo_ref)
-
-    fetch(step).wait()
     a_ref = tiles_ref.at[step % 2]
     second_ref[...] = a_ref[0, 0, 1]
     third_ref[...] = a_ref[0, 1, 0]
@@ -234,7 +242,7 @@
         grid=(tiles,),
         in_specs=[
             smem(),
-            pl.BlockSpec(history.shape, lambda i: (0, 0, 0)),
+            pl.BlockSpec(memory_space=pl.ANY),
             pl.BlockSpec(memory_space=pl.ANY),
         ],
         out_specs=[slots_spec] * 2 + [flat_spec] * (2 * steps - 2) + [pl.BlockSpec((tile, block), lambda i: (i, 0))] * 2,
@@ -242,7 +250,9 @@
         scratch_shapes=[
             *[pltpu.VMEM((len(KINDS), groups * block, cols), BF)] * 2,
             pltpu.VMEM((2, groups, 2, 2, tile, block), F32),
+            pltpu.VMEM(history.shape, F32),
             pltpu.SemaphoreType.DMA((2,)),
+            pltpu.SemaphoreType.DMA((groups,)),
         ],
         compiler_params=pltpu.CompilerParams(vmem_limit_bytes=61 << 20),
         cost_estimate=pl.CostEstimate(

time: 161 us -> 160 us (level)
  no operation moved by 1% of the time
where the time goes in v5:
time: 160 us; the launch traced here: 159 us
  Pallas kernels  64.8 us (40%)
  waiting for transfers between devices  48.1 us (30%)
  starting transfers between devices  39 us (24%)
  other arithmetic  4.18 us (3%)
  local copies, waits for them, and re-layouts  2.78 us (2%)
    ppermute x28, waiting for transfers between devices, exchanged(): return lax.ppermute(value, axis, swap_pairs(axis, bit))  41.7 us
    pallas_call x1, Pallas kernels, bulk(): pl.pallas_call(functools.partial(bulk_kernel, slices=slices, block=block)...  38.3 us
    ppermute x28, starting transfers between devices, exchanged(): return lax.ppermute(value, axis, swap_pairs(axis, bit))  25.3 us
    pallas_call x3, Pallas kernels, with_carried(): pl.pallas_call(functools.partial(carried_kernel, slices=slices), grid=(1,...  13.1 us
    pallas_call x7, Pallas kernels, whole_call(): pl.pallas_call(kernel, in_specs=[smem()] + [vmem] * (len(args) - 1), out_...  7.39 us
    ppermute x2, waiting for transfers between devices, taken(): got = lax.ppermute(offer, ('lag', 'col'), stage_pairs(stage))  6.39 us
    ppermute x1, starting transfers between devices, local(): lax.ppermute(newest, 'lag', [(0, top)])  6.23 us
    pallas_call x1, Pallas kernels, staged(): pl.pallas_call(stage_kernel, grid=(1,), in_specs=[smem(), pl.BlockSpec((1...  3.44 us
  transfers between devices with their start and end apart: 35, of which 20 were waited for; matrix products, arithmetic and copies ran while one was open for 1% of the time, Pallas kernels for 36%

profile of v5, /device:TPU:0, one launch (start us, length us, event | category | flops | bytes accessed | tf_op | source)
XLA Modules:
  0.0 159.4 jit_solution(13827199988999822601)
XLA Ops:
  0.0 3.4 %stage.1 = (f32[2048,256]{1,0:T(8,128)}, f32[3,256,256]{2,1,0:T(8,128)}) custom-call(s32[1]{0:T(128)} %bitcast.own_ref, f32[16,2048,256]{2,1,0:T(8,128)} %refs_2_.3, f32[16,256,256]{2,1,0:T(8,128)} %refs_2_.2, f32[16,256,256]{2,1,0:T(8,128)} %refs_2_.2, f32[16,256,256]{2,1,0:T(8,128)} %refs_2_.2), custom_call_target="tpu_custom_call" | custom-call | flops 1 | bytes 1 | tf_op jit(solution)/shard_map/stage/pallas_call | solution.py:278
  3.4 6.2 %collective-permute-start = (f32[2048,256]{1,0:T(8,128)}, f32[2048,256]{1,0:T(8,128)}, u32[]{:S(2)}, u32[]{:S(2)}) collective-permute-start(f32[2048,256]{1,0:T(8,128)} %get-tuple-element.88), channel_id=1, source_target_pairs={{0,16},{1,17},{2,18},{3,19},{4,20},{5,21},{6,22},{7,23}} | collective-permute-start | bytes 6291464 | tf_op jit(solution)/shard_map/ppermute | solution.py:453
  11.0 38.3 %bulk.1 = (f32[4,4,128,128]{3,2,1,0:T(8,128)}, f32[4,4,128,128]{3,2,1,0:T(8,128)}, f32[2,1024,128]{2,1,0:T(8,128)}, f32[2,1024,128]{2,1,0:T(8,128)}, f32[2,1024,...) custom-call(s32[1]{0:T(128)} %bitcast.own_ref, ...), custom_call_target="tpu_custom_call" | custom-call | flops 38654705664 | bytes 33554432 | tf_op jit(solution)/shard_map/bulk/pallas_call | solution.py:240
  55.2 3.0 %carried.3 = (f32[2,1024,128]{2,1,0:T(8,128)S(1)}, f32[2,1024,128]{2,1,0:T(8,128)S(1)}) custom-call(s32[1]{0:T(128)} %bitcast.own_ref, f32[3,256,256]{2,1,0:T(8,128)S(1)} %collective-permute-done.1.tail_ref, f32[2,1024,128]{2,1,0:T(8,128)S(1)} %copy-done.4, f32[2,1024,128]{2,1,0:T(8,128)S(1)} %copy-done.5, f32[16,2048,256]{2,1,0:T(8,128)} %refs_2_.3), custom_call_target="tpu_custom_call" | custom-call | flops 1 | bytes 1 | tf_op jit(solution)/shard_map/carried/pallas_call | solution.py:211
  58.5 4.4 %collective-permute-done.3 = f32[2,4,128,128]{3,2,1,0:T(8,128)S(1)} collective-permute-done((f32[2,4,128,128]{3,2,1,0:T(8,128)S(1)}, f32[2,4,128,128]{3,2,1,0:T(8,128)S(1)}, u32[]{:S(2)}, u32[]{:S(2)}) %collective-permute-start.3) | collective-permute-done | bytes 524320 | tf_op jit(solution)/shard_map/ppermute | solution.py:420
  65.6 4.3 %carried.4 = (f32[2,1024,128]{2,1,0:T(8,128)S(1)}, f32[2,1024,128]{2,1,0:T(8,128)S(1)}) custom-call(s32[1]{0:T(128)} %bitcast.own_ref, f32[3,256,256]{2,1,0:T(8,128)S(1)} %collective-permute-done.1.tail_ref, f32[2,1024,128]{2,1,0:T(8,128)S(1)} %copy-done.7, f32[2,1024,128]{2,1,0:T(8,128)S(1)} %copy-done.8, f32[16,2048,256]{2,1,0:T(8,128)} %refs_2_.3, ...), custom_call_target="tpu_custom_call" | custom-call | flops 1 | bytes 1 | tf_op jit(solution)/shard_map/carried/pallas_call | solution.py:211
  69.9 2.0 %collective-permute-done.4 = f32[1,4,128,128]{3,2,1,0:T(8,128)S(1)} collective-permute-done((f32[1,4,128,128]{3,2,1,0:T(8,128)S(1)}, f32[1,4,128,128]{3,2,1,0:T(8,128)S(1)}, u32[]{:S(2)}, u32[]{:S(2)}) %collective-permute-start.4) | collective-permute-done | bytes 262176 | tf_op jit(solution)/shard_map/ppermute | solution.py:420
  73.3 2.7 %collective-permute-start.10 = (f32[128,128]{1,0:T(8,128)S(1)}, f32[128,128]{1,0:T(8,128)S(1)}, u32[]{:S(2)}, u32[]{:S(2)}) collective-permute-start(f32[128,128]{1,0:T(8,128)S(1)} %get-tuple-element.109), channel_id=1, source_target_pairs={{0,4},{1,5},{2,6},{3,7},{4,0},{5,1},{6,2},{7,3},{8,12},{9,13},{10,... | collective-permute-start | bytes 196616 | tf_op jit(solution)/shard_map/ppermute | solution.py:24
  77.6 5.8 %carried.5 = (f32[2,1024,128]{2,1,0:T(8,128)S(1)}, f32[2,1024,128]{2,1,0:T(8,128)S(1)}) custom-call(s32[1]{0:T(128)} %bitcast.own_ref, f32[3,256,256]{2,1,0:T(8,128)S(1)} %collective-permute-done.1.tail_ref, f32[2,1024,128]{2,1,0:T(8,128)S(1)} %copy-done.2, f32[2,1024,128]{2,1,0:T(8,128)S(1)} %copy-done.3, f32[16,2048,256]{2,1,0:T(8,128)} %refs_2_.3, ...), custom_call_target="tpu_custom_call" | custom-call | flops 1 | bytes 1 | tf_op jit(solution)/shard_map/carried/pallas_call | solution.py:211
  83.5 4.1 %collective-permute-done.8 = f32[1,1024,128]{2,1,0:T(8,128)S(1)} collective-permute-done((f32[1,1024,128]{2,1,0:T(8,128)S(1)}, f32[1,1024,128]{2,1,0:T(8,128)S(1)}, u32[]{:S(2)}, u32[]{:S(2)}) %collective-permute-start.8) | collective-permute-done | bytes 524320 | tf_op jit(solution)/shard_map/ppermute | solution.py:24
  89.2 1.7 %collective-permute-start.13 = (f32[2048,256]{1,0:T(8,128)S(1)}, f32[2048,256]{1,0:T(8,128)S(1)}, u32[]{:S(2)}, u32[]{:S(2)}) collective-permute-start(f32[2048,256]{1,0:T(8,128)S(1)} %copy-done), channel_id=1, source_target_pairs={{0,8},{1,9},{2,10},{3,11},{4,12},{5,13},{6,14},{7,15}} | collective-permute-start | bytes 6291464 | tf_op jit(solution)/shard_map/ppermute | solution.py:511
  92.7 2.9 %collective-permute-done.12 = f32[1,128,128]{2,1,0:T(8,128)S(1)} collective-permute-done((f32[1,128,128]{2,1,0:T(8,128)S(1)}, f32[1,128,128]{2,1,0:T(8,128)S(1)}, u32[]{:S(2)}, u32[]{:S(2)}) %collective-permute-start.12) | collective-permute-done | bytes 65568 | tf_op jit(solution)/shard_map/ppermute | solution.py:24
  97.2 2.5 %collective-permute-done.15 = f32[4,128,128]{2,1,0:T(8,128)S(1)} collective-permute-done((f32[4,128,128]{2,1,0:T(8,128)S(1)}, f32[4,128,128]{2,1,0:T(8,128)S(1)}, u32[]{:S(2)}, u32[]{:S(2)}) %collective-permute-start.15) | collective-permute-done | bytes 262176 | tf_op jit(solution)/shard_map/ppermute | solution.py:24
  99.8 1.6 %collective-permute-start.16 = (f32[128,128]{1,0:T(8,128)S(1)}, f32[128,128]{1,0:T(8,128)S(1)}, u32[]{:S(2)}, u32[]{:S(2)}) collective-permute-start(f32[128,128]{1,0:T(8,128)S(1)} %get-tuple-element.161), channel_id=1, source_target_pairs={{0,2},{1,3},{2,0},{3,1},{4,6},{5,7},{6,4},{7,5},{8,10},{9,11},{10,... | collective-permute-start | bytes 196616 | tf_op jit(solution)/shard_map/ppermute | solution.py:24
  101.4 2.6 %collective-permute-start.17 = (f32[128,128]{1,0:T(8,128)S(1)}, f32[128,128]{1,0:T(8,128)S(1)}, u32[]{:S(2)}, u32[]{:S(2)}) collective-permute-start(f32[128,128]{1,0:T(8,128)S(1)} %get-tuple-element.160), channel_id=1, source_target_pairs={{0,4},{1,5},{2,6},{3,7},{4,0},{5,1},{6,2},{7,3},{8,12},{9,13},{10,... | collective-permute-start | bytes 196616 | tf_op jit(solution)/shard_map/ppermute | solution.py:24
  104.4 4.0 %collective-permute-done.17.refs_2_ = f32[128,128]{1,0:T(8,128)S(1)} collective-permute-done((f32[128,128]{1,0:T(8,128)S(1)}, f32[128,128]{1,0:T(8,128)S(1)}, u32[]{:S(2)}, u32[]{:S(2)}) %collective-permute-start.17) | collective-permute-done | bytes 65568 | tf_op jit(solution)/shard_map/ppermute | solution.py:24
  108.4 1.7 %collective-permute-done.18.refs_3_ = f32[128,128]{1,0:T(8,128)S(1)} collective-permute-done((f32[128,128]{1,0:T(8,128)S(1)}, f32[128,128]{1,0:T(8,128)S(1)}, u32[]{:S(2)}, u32[]{:S(2)}) %collective-permute-start.18) | collective-permute-done | bytes 65568 | tf_op jit(solution)/shard_map/ppermute | solution.py:24
  115.8 2.3 %collective-permute-done.20 = f32[1,128,128]{2,1,0:T(8,128)S(1)} collective-permute-done((f32[1,128,128]{2,1,0:T(8,128)S(1)}, f32[1,128,128]{2,1,0:T(8,128)S(1)}, u32[]{:S(2)}, u32[]{:S(2)}) %collective-permute-start.20) | collective-permute-done | bytes 65568 | tf_op jit(solution)/shard_map/ppermute | solution.py:24
  118.1 2.2 %late.3 = f32[2,1024,128]{2,1,0:T(8,128)S(1)} custom-call(s32[1]{0:T(128)} %bitcast.own_ref, f32[2,1024,128]{2,1,0:T(8,128)S(1)} %add.72.acc_ref, f32[2048,256]{1,0:T(8,128)S(1)} %copy-done, f32[2048,256]{1,0:T(8,128)S(1)} %collective-permute-done.13.refs_1_, f32[2,128,128]{2,1,0:T(8,128)S(1)} %get-tuple-element.169.refs_2_, f32[2048,256]{1,0:T(8,128)S(1)} %copy-done.1, ...), custom_call_target="tpu_custom_call" | custom-call | flops 1 | bytes 1 | tf_op jit(solution)/shard_map/late/pallas_call | solution.py:377
  120.8 1.6 %collective-permute-start.24 = (f32[128,128]{1,0:T(8,128)S(1)}, f32[128,128]{1,0:T(8,128)S(1)}, u32[]{:S(2)}, u32[]{:S(2)}) collective-permute-start(f32[128,128]{1,0:T(8,128)S(1)} %get-tuple-element.157), channel_id=1, source_target_pairs={{0,2},{1,3},{2,0},{3,1},{4,6},{5,7},{6,4},{7,5},{8,10},{9,11},{10,... | collective-permute-start | bytes 196616 | tf_op jit(solution)/shard_map/ppermute | solution.py:24
  122.4 2.6 %collective-permute-start.25 = (f32[128,128]{1,0:T(8,128)S(1)}, f32[128,128]{1,0:T(8,128)S(1)}, u32[]{:S(2)}, u32[]{:S(2)}) collective-permute-start(f32[128,128]{1,0:T(8,128)S(1)} %get-tuple-element.156), channel_id=1, source_target_pairs={{0,4},{1,5},{2,6},{3,7},{4,0},{5,1},{6,2},{7,3},{8,12},{9,13},{10,... | collective-permute-start | bytes 196616 | tf_op jit(solution)/shard_map/ppermute | solution.py:24
  125.2 4.0 %collective-permute-done.25.refs_2_ = f32[128,128]{1,0:T(8,128)S(1)} collective-permute-done((f32[128,128]{1,0:T(8,128)S(1)}, f32[128,128]{1,0:T(8,128)S(1)}, u32[]{:S(2)}, u32[]{:S(2)}) %collective-permute-start.25) | collective-permute-done | bytes 65568 | tf_op jit(solution)/shard_map/ppermute | solution.py:24
  129.2 1.8 %collective-permute-done.26.refs_3_ = f32[128,128]{1,0:T(8,128)S(1)} collective-permute-done((f32[128,128]{1,0:T(8,128)S(1)}, f32[128,128]{1,0:T(8,128)S(1)}, u32[]{:S(2)}, u32[]{:S(2)}) %collective-permute-start.26) | collective-permute-done | bytes 65568 | tf_op jit(solution)/shard_map/ppermute | solution.py:24
  131.1 2.8 %collective-permute-done.22 = f32[1,1024,128]{2,1,0:T(8,128)S(1)} collective-permute-done((f32[1,1024,128]{2,1,0:T(8,128)S(1)}, f32[1,1024,128]{2,1,0:T(8,128)S(1)}, u32[]{:S(2)}, u32[]{:S(2)}) %collective-permute-start.22) | collective-permute-done | bytes 524320 | tf_op jit(solution)/shard_map/ppermute | solution.py:24
  136.8 2.5 %collective-permute-done.27 = f32[1,128,128]{2,1,0:T(8,128)S(1)} collective-permute-done((f32[1,128,128]{2,1,0:T(8,128)S(1)}, f32[1,128,128]{2,1,0:T(8,128)S(1)}, u32[]{:S(2)}, u32[]{:S(2)}) %collective-permute-start.27) | collective-permute-done | bytes 65568 | tf_op jit(solution)/shard_map/ppermute | solution.py:24
  139.4 2.9 %collective-permute-done.29 = f32[4,128,128]{2,1,0:T(8,128)S(1)} collective-permute-done((f32[4,128,128]{2,1,0:T(8,128)S(1)}, f32[4,128,128]{2,1,0:T(8,128)S(1)}, u32[]{:S(2)}, u32[]{:S(2)}) %collective-permute-start.29) | collective-permute-done | bytes 262176 | tf_op jit(solution)/shard_map/ppermute | solution.py:24
  142.3 1.6 %collective-permute-start.30 = (f32[128,128]{1,0:T(8,128)S(1)}, f32[128,128]{1,0:T(8,128)S(1)}, u32[]{:S(2)}, u32[]{:S(2)}) collective-permute-start(f32[128,128]{1,0:T(8,128)S(1)} %get-tuple-element.153), channel_id=1, source_target_pairs={{0,2},{1,3},{2,0},{3,1},{4,6},{5,7},{6,4},{7,5},{8,10},{9,11},{10,... | collective-permute-start | bytes 196616 | tf_op jit(solution)/shard_map/ppermute | solution.py:24
  143.9 2.6 %collective-permute-start.31 = (f32[128,128]{1,0:T(8,128)S(1)}, f32[128,128]{1,0:T(8,128)S(1)}, u32[]{:S(2)}, u32[]{:S(2)}) collective-permute-start(f32[128,128]{1,0:T(8,128)S(1)} %get-tuple-element.152), channel_id=1, source_target_pairs={{0,4},{1,5},{2,6},{3,7},{4,0},{5,1},{6,2},{7,3},{8,12},{9,13},{10,... | collective-permute-start | bytes 196616 | tf_op jit(solution)/shard_map/ppermute | solution.py:24
  146.8 1.6 %assemble.2.refs_0_ = f32[4,256,256]{2,1,0:T(8,128)} custom-call(s32[1]{0:T(128)} %bitcast.own_ref, f32[4,3,128,128]{3,2,1,0:T(8,128)S(1)} %pad_maximum_fusion.parts_ref), custom_call_target="tpu_custom_call" | custom-call | flops 1 | bytes 1 | tf_op jit(solution)/shard_map/assemble/pallas_call | solution.py:361
  148.4 2.0 %collective-permute-done.31 = f32[128,128]{1,0:T(8,128)S(1)} collective-permute-done((f32[128,128]{1,0:T(8,128)S(1)}, f32[128,128]{1,0:T(8,128)S(1)}, u32[]{:S(2)}, u32[]{:S(2)}) %collective-permute-start.31) | collective-permute-done | bytes 65568 | tf_op jit(solution)/shard_map/ppermute | solution.py:24
  150.4 2.2 %collective-permute-done.32 = f32[128,128]{1,0:T(8,128)S(1)} collective-permute-done((f32[128,128]{1,0:T(8,128)S(1)}, f32[128,128]{1,0:T(8,128)S(1)}, u32[]{:S(2)}, u32[]{:S(2)}) %collective-permute-start.32) | collective-permute-done | bytes 65568 | tf_op jit(solution)/shard_map/ppermute | solution.py:24
  154.1 2.8 %collective-permute-done.33 = f32[1,128,128]{2,1,0:T(8,128)S(1)} collective-permute-done((f32[1,128,128]{2,1,0:T(8,128)S(1)}, f32[1,128,128]{2,1,0:T(8,128)S(1)}, u32[]{:S(2)}, u32[]{:S(2)}) %collective-permute-start.33) | collective-permute-done | bytes 65568 | tf_op jit(solution)/shard_map/ppermute | solution.py:24
  (100 shorter events, 32.1 us)
Async XLA Ops:
  3.4 45.9 %collective-permute-start = (f32[2048,256]{1,0:T(8,128)}, f32[2048,256]{1,0:T(8,128)}, u32[]{:S(2)}, u32[]{:S(2)}) collective-permute-start(f32[2048,256]{1,0:T(8,128)} %get-tuple-element.88), channel_id=1, source_target_pairs={{0,16},{1,17},{2,18},{3,19},{4,20},{5,21},{6,22},{7,23}} | collective-permute-start | bytes 6291464 | tf_op jit(solution)/shard_map/ppermute | solution.py:453
  9.7 39.6 %collective-permute-start.1 = (f32[3,256,256]{2,1,0:T(8,128)}, f32[3,256,256]{2,1,0:T(8,128)S(1)}, u32[]{:S(2)}, u32[]{:S(2)}) collective-permute-start(f32[3,256,256]{2,1,0:T(8,128)} %get-tuple-element.77), channel_id=1, source_target_pairs={{0,8},{8,16},{16,24},{1,9},{9,17},{17,25},{2,10},{10,18},{18,26},{... | collective-permute-start | bytes 2359304 | tf_op jit(solution)/shard_map/ppermute | solution.py:454
  53.7 9.2 %collective-permute-start.3 = (f32[2,4,128,128]{3,2,1,0:T(8,128)S(1)}, f32[2,4,128,128]{3,2,1,0:T(8,128)S(1)}, u32[]{:S(2)}, u32[]{:S(2)}) collective-permute-start(f32[2,4,128,128]{3,2,1,0:T(8,128)S(1)} %pad_maximum_fusion.1), channel_id=1, source_target_pairs={{0,1},{1,0},{2,3},{3,2},{4,5},{5,4},{6,7},{7,6},{8,24},{9,25},{10,... | collective-permute-start | bytes 1572872 | tf_op jit(solution)/shard_map/ppermute | solution.py:420
  63.9 9.0 %collective-permute-start.5 = (f32[2048,256]{1,0:T(8,128)S(1)}, f32[2048,256]{1,0:T(8,128)S(1)}, u32[]{:S(2)}, u32[]{:S(2)}) collective-permute-start(f32[2048,256]{1,0:T(8,128)S(1)} %broadcast_select_fusion.m_ref), channel_id=1, source_target_pairs={{0,8},{16,24},{1,9},{17,25},{2,10},{18,26},{3,11},{19,27},{4,12},{... | collective-permute-start | bytes 6291464 | tf_op jit(solution)/shard_map/ppermute | solution.py:475
  65.4 7.6 %collective-permute-start.7 = (f32[2,1024,128]{2,1,0:T(8,128)S(1)}, f32[2,1024,128]{2,1,0:T(8,128)S(1)}, u32[]{:S(2)}, u32[]{:S(2)}) collective-permute-start(f32[2,1024,128]{2,1,0:T(8,128)S(1)} %get-tuple-element.105), channel_id=1, source_target_pairs={{0,8},{8,0},{16,24},{24,16},{1,9},{9,1},{17,25},{25,17},{2,10},{10... | collective-permute-start | bytes 3145736 | tf_op jit(solution)/shard_map/ppermute | solution.py:24
  65.5 6.4 %collective-permute-start.4 = (f32[1,4,128,128]{3,2,1,0:T(8,128)S(1)}, f32[1,4,128,128]{3,2,1,0:T(8,128)S(1)}, u32[]{:S(2)}, u32[]{:S(2)}) collective-permute-start(f32[1,4,128,128]{3,2,1,0:T(8,128)S(1)} %slice_add_fusion.2), channel_id=1, source_target_pairs={{0,16},{1,17},{2,18},{3,19},{4,20},{5,21},{6,22},{7,23},{8,9},{9,8... | collective-permute-start | bytes 786440 | tf_op jit(solution)/shard_map/ppermute | solution.py:420
  72.9 10.5 %collective-permute-start.6 = (f32[2,1024,128]{2,1,0:T(8,128)S(1)}, f32[2,1024,128]{2,1,0:T(8,128)S(1)}, u32[]{:S(2)}, u32[]{:S(2)}) collective-permute-start(f32[2,1024,128]{2,1,0:T(8,128)S(1)} %get-tuple-element.102), channel_id=1, source_target_pairs={{0,8},{8,0},{16,24},{24,16},{1,9},{9,1},{17,25},{25,17},{2,10},{10... | collective-permute-start | bytes 3145736 | tf_op jit(solution)/shard_map/ppermute | solution.py:24
  73.2 14.4 %collective-permute-start.8 = (f32[1,1024,128]{2,1,0:T(8,128)S(1)}, f32[1,1024,128]{2,1,0:T(8,128)S(1)}, u32[]{:S(2)}, u32[]{:S(2)}) collective-permute-start(f32[1,1024,128]{2,1,0:T(8,128)S(1)} %get-tuple-element.149), channel_id=1, source_target_pairs={{0,16},{8,24},{16,0},{24,8},{1,17},{9,25},{17,1},{25,9},{2,18},{10... | collective-permute-start | bytes 1572872 | tf_op jit(solution)/shard_map/ppermute | solution.py:24
  73.3 14.3 %collective-permute-start.10 = (f32[128,128]{1,0:T(8,128)S(1)}, f32[128,128]{1,0:T(8,128)S(1)}, u32[]{:S(2)}, u32[]{:S(2)}) collective-permute-start(f32[128,128]{1,0:T(8,128)S(1)} %get-tuple-element.109), channel_id=1, source_target_pairs={{0,4},{1,5},{2,6},{3,7},{4,0},{5,1},{6,2},{7,3},{8,12},{9,13},{10,... | collective-permute-start | bytes 196616 | tf_op jit(solution)/shard_map/ppermute | solution.py:24
  76.0 11.6 %collective-permute-start.11 = (f32[128,128]{1,0:T(8,128)S(1)}, f32[128,128]{1,0:T(8,128)S(1)}, u32[]{:S(2)}, u32[]{:S(2)}) collective-permute-start(f32[128,128]{1,0:T(8,128)S(1)} %get-tuple-element.110), channel_id=1, source_target_pairs={{0,6},{1,7},{2,4},{3,5},{4,2},{5,3},{6,0},{7,1},{8,14},{9,15},{10,... | collective-permute-start | bytes 196616 | tf_op jit(solution)/shard_map/ppermute | solution.py:24
  77.3 10.3 %collective-permute-start.9 = (f32[128,128]{1,0:T(8,128)S(1)}, f32[128,128]{1,0:T(8,128)S(1)}, u32[]{:S(2)}, u32[]{:S(2)}) collective-permute-start(f32[128,128]{1,0:T(8,128)S(1)} %get-tuple-element.108), channel_id=1, source_target_pairs={{0,2},{1,3},{2,0},{3,1},{4,6},{5,7},{6,4},{7,5},{8,10},{9,11},{10,... | collective-permute-start | bytes 196616 | tf_op jit(solution)/shard_map/ppermute | solution.py:24
  89.2 6.3 %collective-permute-start.13 = (f32[2048,256]{1,0:T(8,128)S(1)}, f32[2048,256]{1,0:T(8,128)S(1)}, u32[]{:S(2)}, u32[]{:S(2)}) collective-permute-start(f32[2048,256]{1,0:T(8,128)S(1)} %copy-done), channel_id=1, source_target_pairs={{0,8},{1,9},{2,10},{3,11},{4,12},{5,13},{6,14},{7,15}} | collective-permute-start | bytes 6291464 | tf_op jit(solution)/shard_map/ppermute | solution.py:511
  90.9 13.3 %collective-permute-start.19 = (f32[2,1024,128]{2,1,0:T(8,128)S(1)}, f32[2,1024,128]{2,1,0:T(8,128)S(1)}, u32[]{:S(2)}, u32[]{:S(2)}) collective-permute-start(f32[2,1024,128]{2,1,0:T(8,128)S(1)} %get-tuple-element.129), channel_id=1, source_target_pairs={{0,8},{8,0},{16,24},{24,16},{1,9},{9,1},{17,25},{25,17},{2,10},{10... | collective-permute-start | bytes 3145736 | tf_op jit(solution)/shard_map/ppermute | solution.py:24
  91.0 4.5 %collective-permute-start.12 = (f32[1,128,128]{2,1,0:T(8,128)S(1)}, f32[1,128,128]{2,1,0:T(8,128)S(1)}, u32[]{:S(2)}, u32[]{:S(2)}) collective-permute-start(f32[1,128,128]{2,1,0:T(8,128)S(1)} %bitcast.66), channel_id=1, source_target_pairs={{0,16},{8,24},{16,0},{24,8},{1,17},{9,25},{17,1},{25,9},{2,18},{10... | collective-permute-start | bytes 196616 | tf_op jit(solution)/shard_map/ppermute | solution.py:24
  91.1 8.6 %collective-permute-start.15 = (f32[4,128,128]{2,1,0:T(8,128)S(1)}, f32[4,128,128]{2,1,0:T(8,128)S(1)}, u32[]{:S(2)}, u32[]{:S(2)}) collective-permute-start(f32[4,128,128]{2,1,0:T(8,128)S(1)} %get-tuple-element.125), channel_id=1, source_target_pairs={{0,1},{1,0},{2,3},{3,2},{4,5},{5,4},{6,7},{7,6},{8,9},{9,8},{10,11... | collective-permute-start | bytes 786440 | tf_op jit(solution)/shard_map/ppermute | solution.py:24
  97.1 13.6 %collective-permute-start.14 = (f32[1,1024,128]{2,1,0:T(8,128)S(1)}, f32[1,1024,128]{2,1,0:T(8,128)S(1)}, u32[]{:S(2)}, u32[]{:S(2)}) collective-permute-start(f32[1,1024,128]{2,1,0:T(8,128)S(1)} %get-tuple-element.147), channel_id=1, source_target_pairs={{0,16},{8,24},{16,0},{24,8},{1,17},{9,25},{17,1},{25,9},{2,18},{10... | collective-permute-start | bytes 1572872 | tf_op jit(solution)/shard_map/ppermute | solution.py:24
  99.8 4.6 %collective-permute-start.16 = (f32[128,128]{1,0:T(8,128)S(1)}, f32[128,128]{1,0:T(8,128)S(1)}, u32[]{:S(2)}, u32[]{:S(2)}) collective-permute-start(f32[128,128]{1,0:T(8,128)S(1)} %get-tuple-element.161), channel_id=1, source_target_pairs={{0,2},{1,3},{2,0},{3,1},{4,6},{5,7},{6,4},{7,5},{8,10},{9,11},{10,... | collective-permute-start | bytes 196616 | tf_op jit(solution)/shard_map/ppermute | solution.py:24
  101.4 7.0 %collective-permute-start.17 = (f32[128,128]{1,0:T(8,128)S(1)}, f32[128,128]{1,0:T(8,128)S(1)}, u32[]{:S(2)}, u32[]{:S(2)}) collective-permute-start(f32[128,128]{1,0:T(8,128)S(1)} %get-tuple-element.160), channel_id=1, source_target_pairs={{0,4},{1,5},{2,6},{3,7},{4,0},{5,1},{6,2},{7,3},{8,12},{9,13},{10,... | collective-permute-start | bytes 196616 | tf_op jit(solution)/shard_map/ppermute | solution.py:24
  104.0 6.1 %collective-permute-start.18 = (f32[128,128]{1,0:T(8,128)S(1)}, f32[128,128]{1,0:T(8,128)S(1)}, u32[]{:S(2)}, u32[]{:S(2)}) collective-permute-start(f32[128,128]{1,0:T(8,128)S(1)} %get-tuple-element.159), channel_id=1, source_target_pairs={{0,6},{1,7},{2,4},{3,5},{4,2},{5,3},{6,0},{7,1},{8,14},{9,15},{10,... | collective-permute-start | bytes 196616 | tf_op jit(solution)/shard_map/ppermute | solution.py:24
  112.3 5.8 %collective-permute-start.21 = (f32[2048,256]{1,0:T(8,128)S(1)}, f32[2048,256]{1,0:T(8,128)S(1)}, u32[]{:S(2)}, u32[]{:S(2)}) collective-permute-start(f32[2048,256]{1,0:T(8,128)S(1)} %copy-done.1), channel_id=1, source_target_pairs={{0,8},{1,9},{2,10},{3,11},{4,12},{5,13},{6,14},{7,15}} | collective-permute-start | bytes 6291464 | tf_op jit(solution)/shard_map/ppermute | solution.py:511
  113.7 4.3 %collective-permute-start.20 = (f32[1,128,128]{2,1,0:T(8,128)S(1)}, f32[1,128,128]{2,1,0:T(8,128)S(1)}, u32[]{:S(2)}, u32[]{:S(2)}) collective-permute-start(f32[1,128,128]{2,1,0:T(8,128)S(1)} %bitcast.68), channel_id=1, source_target_pairs={{0,16},{8,24},{16,0},{24,8},{1,17},{9,25},{17,1},{25,9},{2,18},{10... | collective-permute-start | bytes 196616 | tf_op jit(solution)/shard_map/ppermute | solution.py:24
  114.3 6.4 %collective-permute-start.23 = (f32[4,128,128]{2,1,0:T(8,128)S(1)}, f32[4,128,128]{2,1,0:T(8,128)S(1)}, u32[]{:S(2)}, u32[]{:S(2)}) collective-permute-start(f32[4,128,128]{2,1,0:T(8,128)S(1)} %get-tuple-element.134), channel_id=1, source_target_pairs={{0,1},{1,0},{2,3},{3,2},{4,5},{5,4},{6,7},{7,6},{8,9},{9,8},{10,11... | collective-permute-start | bytes 786440 | tf_op jit(solution)/shard_map/ppermute | solution.py:24
  120.4 13.5 %collective-permute-start.22 = (f32[1,1024,128]{2,1,0:T(8,128)S(1)}, f32[1,1024,128]{2,1,0:T(8,128)S(1)}, u32[]{:S(2)}, u32[]{:S(2)}) collective-permute-start(f32[1,1024,128]{2,1,0:T(8,128)S(1)} %get-tuple-element.145), channel_id=1, source_target_pairs={{0,16},{8,24},{16,0},{24,8},{1,17},{9,25},{17,1},{25,9},{2,18},{10... | collective-permute-start | bytes 1572872 | tf_op jit(solution)/shard_map/ppermute | solution.py:24
  120.8 4.5 %collective-permute-start.24 = (f32[128,128]{1,0:T(8,128)S(1)}, f32[128,128]{1,0:T(8,128)S(1)}, u32[]{:S(2)}, u32[]{:S(2)}) collective-permute-start(f32[128,128]{1,0:T(8,128)S(1)} %get-tuple-element.157), channel_id=1, source_target_pairs={{0,2},{1,3},{2,0},{3,1},{4,6},{5,7},{6,4},{7,5},{8,10},{9,11},{10,... | collective-permute-start | bytes 196616 | tf_op jit(solution)/shard_map/ppermute | solution.py:24
  122.4 6.8 %collective-permute-start.25 = (f32[128,128]{1,0:T(8,128)S(1)}, f32[128,128]{1,0:T(8,128)S(1)}, u32[]{:S(2)}, u32[]{:S(2)}) collective-permute-start(f32[128,128]{1,0:T(8,128)S(1)} %get-tuple-element.156), channel_id=1, source_target_pairs={{0,4},{1,5},{2,6},{3,7},{4,0},{5,1},{6,2},{7,3},{8,12},{9,13},{10,... | collective-permute-start | bytes 196616 | tf_op jit(solution)/shard_map/ppermute | solution.py:24
  125.0 6.1 %collective-permute-start.26 = (f32[128,128]{1,0:T(8,128)S(1)}, f32[128,128]{1,0:T(8,128)S(1)}, u32[]{:S(2)}, u32[]{:S(2)}) collective-permute-start(f32[128,128]{1,0:T(8,128)S(1)} %get-tuple-element.155), channel_id=1, source_target_pairs={{0,6},{1,7},{2,4},{3,5},{4,2},{5,3},{6,0},{7,1},{8,14},{9,15},{10,... | collective-permute-start | bytes 196616 | tf_op jit(solution)/shard_map/ppermute | solution.py:24
  135.3 7.0 %collective-permute-start.29 = (f32[4,128,128]{2,1,0:T(8,128)S(1)}, f32[4,128,128]{2,1,0:T(8,128)S(1)}, u32[]{:S(2)}, u32[]{:S(2)}) collective-permute-start(f32[4,128,128]{2,1,0:T(8,128)S(1)} %get-tuple-element.137), channel_id=1, source_target_pairs={{0,1},{1,0},{2,3},{3,2},{4,5},{5,4},{6,7},{7,6},{8,9},{9,8},{10,11... | collective-permute-start | bytes 786440 | tf_op jit(solution)/shard_map/ppermute | solution.py:24
  139.3 7.5 %collective-permute-start.28 = (f32[2,3,128,128]{3,2,1,0:T(8,128)S(1)}, f32[2,3,128,128]{3,2,1,0:T(8,128)S(1)}, u32[]{:S(2)}, u32[]{:S(2)}) collective-permute-start(f32[2,3,128,128]{3,2,1,0:T(8,128)S(1)} %pad_maximum_fusion.2), channel_id=1, source_target_pairs={{0,8},{8,0},{16,24},{24,16},{1,9},{9,1},{17,25},{25,17},{2,10},{10... | collective-permute-start | bytes 1179656 | tf_op jit(solution)/shard_map/ppermute | solution.py:24
  142.3 6.1 %collective-permute-start.30 = (f32[128,128]{1,0:T(8,128)S(1)}, f32[128,128]{1,0:T(8,128)S(1)}, u32[]{:S(2)}, u32[]{:S(2)}) collective-permute-start(f32[128,128]{1,0:T(8,128)S(1)} %get-tuple-element.153), channel_id=1, source_target_pairs={{0,2},{1,3},{2,0},{3,1},{4,6},{5,7},{6,4},{7,5},{8,10},{9,11},{10,... | collective-permute-start | bytes 196616 | tf_op jit(solution)/shard_map/ppermute | solution.py:24
  143.9 6.5 %collective-permute-start.31 = (f32[128,128]{1,0:T(8,128)S(1)}, f32[128,128]{1,0:T(8,128)S(1)}, u32[]{:S(2)}, u32[]{:S(2)}) collective-permute-start(f32[128,128]{1,0:T(8,128)S(1)} %get-tuple-element.152), channel_id=1, source_target_pairs={{0,4},{1,5},{2,6},{3,7},{4,0},{5,1},{6,2},{7,3},{8,12},{9,13},{10,... | collective-permute-start | bytes 196616 | tf_op jit(solution)/shard_map/ppermute | solution.py:24
  146.5 6.1 %collective-permute-start.32 = (f32[128,128]{1,0:T(8,128)S(1)}, f32[128,128]{1,0:T(8,128)S(1)}, u32[]{:S(2)}, u32[]{:S(2)}) collective-permute-start(f32[128,128]{1,0:T(8,128)S(1)} %get-tuple-element.151), channel_id=1, source_target_pairs={{0,6},{1,7},{2,4},{3,5},{4,2},{5,3},{6,0},{7,1},{8,14},{9,15},{10,... | collective-permute-start | bytes 196616 | tf_op jit(solution)/shard_map/ppermute | solution.py:24
  152.6 4.3 %collective-permute-start.33 = (f32[1,128,128]{2,1,0:T(8,128)S(1)}, f32[1,128,128]{2,1,0:T(8,128)S(1)}, u32[]{:S(2)}, u32[]{:S(2)}) collective-permute-start(f32[1,128,128]{2,1,0:T(8,128)S(1)} %fusion.2), channel_id=1, source_target_pairs={{0,16},{8,24},{16,0},{24,8},{1,17},{9,25},{17,1},{25,9},{2,18},{10... | collective-permute-start | bytes 196616 | tf_op jit(solution)/shard_map/ppermute | solution.py:24
  (14 other events, 56.5 us)

commit v6 on v5

--- a/solution.py
+++ b/solution.py
@@ -501,14 +501,11 @@
         if n + 1 < steps:
             if n == 1:
                 held["x"] = x
-                sealed(held, "x", "lag2", "send3")
+                sealed(held, "x", "lag2", "lag3", "send3")
                 x = held["x"]
                 held["past3"] = partner_sum(3)
-            else:
-                held["x"] = x
-                sealed(held, "x", "lag3", "past3")
-                x = held["x"]
-            held[f"odd{n + 1}"] = lax.ppermute(held[f"lag{n + 1}"], "lag", [(0, 1)])
+                for k in (2, 3):
+                    held[f"odd{k}"] = lax.ppermute(held[f"lag{k}"], "lag", [(0, 1)])
             shown.append(gathered(x[None]))
             terms = [v for k in range(2, n + 2) for v in (held[f"lag{k}"], held[f"odd{k}"], shown[n + 1 - k])]
             past = whole_call(

time: 160 us -> 157 us (0.981)
  waiting for transfers between devices: 48.1 us -> 39.4 us
  starting transfers between devices: 39 us -> 45.2 us
    ppermute x28, waiting for transfers between devices: 41.7 us -> 33 us  [exchanged(): return lax.ppermute(value, axis, swap_pairs(axis, bit))]
    ppermute x28, starting transfers between devices: 25.3 us -> 31.4 us  [exchanged(): return lax.ppermute(value, axis, swap_pairs(axis, bit))]
  transfers between devices with their start and end apart: 35 -> 35, of which waited for: 20 -> 21; matrix products, arithmetic and copies ran while one was open for 1% -> 1% of each run, Pallas kernels for 36% -> 37%
where the time goes in v6:
time: 157 us; the launch traced here: 156 us
  Pallas kernels  64.8 us (41%)
  starting transfers between devices  45.2 us (29%)
  waiting for transfers between devices  39.4 us (25%)
  other arithmetic  4.18 us (3%)
  local copies, waits for them, and re-layouts  2.21 us (1%)
    pallas_call x1, Pallas kernels, bulk(): pl.pallas_call(functools.partial(bulk_kernel, slices=slices, block=block)...  38.3 us
    ppermute x28, waiting for transfers between devices, exchanged(): return lax.ppermute(value, axis, swap_pairs(axis, bit))  33 us
    ppermute x28, starting transfers between devices, exchanged(): return lax.ppermute(value, axis, swap_pairs(axis, bit))  31.4 us
    pallas_call x3, Pallas kernels, with_carried(): pl.pallas_call(functools.partial(carried_kernel, slices=slices), grid=(1,...  13.1 us
    pallas_call x7, Pallas kernels, whole_call(): pl.pallas_call(kernel, in_specs=[smem()] + [vmem] * (len(args) - 1), out_...  7.39 us
    ppermute x2, waiting for transfers between devices, taken(): got = lax.ppermute(offer, ('lag', 'col'), stage_pairs(stage))  6.39 us
    ppermute x1, starting transfers between devices, local(): lax.ppermute(newest, 'lag', [(0, top)])  6.23 us
    pallas_call x1, Pallas kernels, staged(): pl.pallas_call(stage_kernel, grid=(1,), in_specs=[smem(), pl.BlockSpec((1...  3.44 us
  transfers between devices with their start and end apart: 35, of which 21 were waited for; matrix products, arithmetic and copies ran while one was open for 1% of the time, Pallas kernels for 37%

profile of v6, /device:TPU:0, one launch (start us, length us, event | category | flops | bytes accessed | tf_op | source)
XLA Modules:
  0.0 156.2 jit_solution(10824317508573737441)
XLA Ops:
  0.0 3.4 %stage.1 = (f32[2048,256]{1,0:T(8,128)}, f32[3,256,256]{2,1,0:T(8,128)}) custom-call(s32[1]{0:T(128)} %bitcast.own_ref, f32[16,2048,256]{2,1,0:T(8,128)} %refs_2_.3, f32[16,256,256]{2,1,0:T(8,128)} %refs_2_.2, f32[16,256,256]{2,1,0:T(8,128)} %refs_2_.2, f32[16,256,256]{2,1,0:T(8,128)} %refs_2_.2), custom_call_target="tpu_custom_call" | custom-call | flops 1 | bytes 1 | tf_op jit(solution)/shard_map/stage/pallas_call | solution.py:278
  3.4 6.2 %collective-permute-start = (f32[2048,256]{1,0:T(8,128)}, f32[2048,256]{1,0:T(8,128)}, u32[]{:S(2)}, u32[]{:S(2)}) collective-permute-start(f32[2048,256]{1,0:T(8,128)} %get-tuple-element.86), channel_id=1, source_target_pairs={{0,16},{1,17},{2,18},{3,19},{4,20},{5,21},{6,22},{7,23}} | collective-permute-start | bytes 6291464 | tf_op jit(solution)/shard_map/ppermute | solution.py:453
  11.0 38.3 %bulk.1 = (f32[4,4,128,128]{3,2,1,0:T(8,128)}, f32[4,4,128,128]{3,2,1,0:T(8,128)}, f32[2,1024,128]{2,1,0:T(8,128)}, f32[2,1024,128]{2,1,0:T(8,128)}, f32[2,1024,...) custom-call(s32[1]{0:T(128)} %bitcast.own_ref, ...), custom_call_target="tpu_custom_call" | custom-call | flops 38654705664 | bytes 33554432 | tf_op jit(solution)/shard_map/bulk/pallas_call | solution.py:240
  53.7 1.6 collective-permute-start.3
  55.2 3.0 %carried.3 = (f32[2,1024,128]{2,1,0:T(8,128)S(1)}, f32[2,1024,128]{2,1,0:T(8,128)S(1)}) custom-call(s32[1]{0:T(128)} %bitcast.own_ref, f32[3,256,256]{2,1,0:T(8,128)S(1)} %collective-permute-done.1.tail_ref, f32[2,1024,128]{2,1,0:T(8,128)S(1)} %copy-done.4, f32[2,1024,128]{2,1,0:T(8,128)S(1)} %copy-done.5, f32[16,2048,256]{2,1,0:T(8,128)} %refs_2_.3), custom_call_target="tpu_custom_call" | custom-call | flops 1 | bytes 1 | tf_op jit(solution)/shard_map/carried/pallas_call | solution.py:211
  58.5 4.4 %collective-permute-done.3 = f32[2,4,128,128]{3,2,1,0:T(8,128)S(1)} collective-permute-done((f32[2,4,128,128]{3,2,1,0:T(8,128)S(1)}, f32[2,4,128,128]{3,2,1,0:T(8,128)S(1)}, u32[]{:S(2)}, u32[]{:S(2)}) %collective-permute-start.3) | collective-permute-done | bytes 524320 | tf_op jit(solution)/shard_map/ppermute | solution.py:420
  65.6 4.3 %carried.4 = (f32[2,1024,128]{2,1,0:T(8,128)S(1)}, f32[2,1024,128]{2,1,0:T(8,128)S(1)}) custom-call(s32[1]{0:T(128)} %bitcast.own_ref, f32[3,256,256]{2,1,0:T(8,128)S(1)} %collective-permute-done.1.tail_ref, f32[2,1024,128]{2,1,0:T(8,128)S(1)} %copy-done.7, f32[2,1024,128]{2,1,0:T(8,128)S(1)} %copy-done.8, f32[16,2048,256]{2,1,0:T(8,128)} %refs_2_.3, ...), custom_call_target="tpu_custom_call" | custom-call | flops 1 | bytes 1 | tf_op jit(solution)/shard_map/carried/pallas_call | solution.py:211
  69.9 2.0 %collective-permute-done.4 = f32[1,4,128,128]{3,2,1,0:T(8,128)S(1)} collective-permute-done((f32[1,4,128,128]{3,2,1,0:T(8,128)S(1)}, f32[1,4,128,128]{3,2,1,0:T(8,128)S(1)}, u32[]{:S(2)}, u32[]{:S(2)}) %collective-permute-start.4) | collective-permute-done | bytes 262176 | tf_op jit(solution)/shard_map/ppermute | solution.py:420
  73.3 2.7 %collective-permute-start.10 = (f32[128,128]{1,0:T(8,128)S(1)}, f32[128,128]{1,0:T(8,128)S(1)}, u32[]{:S(2)}, u32[]{:S(2)}) collective-permute-start(f32[128,128]{1,0:T(8,128)S(1)} %get-tuple-element.107), channel_id=1, source_target_pairs={{0,4},{1,5},{2,6},{3,7},{4,0},{5,1},{6,2},{7,3},{8,12},{9,13},{10,... | collective-permute-start | bytes 196616 | tf_op jit(solution)/shard_map/ppermute | solution.py:24
  77.6 5.8 %carried.5 = (f32[2,1024,128]{2,1,0:T(8,128)S(1)}, f32[2,1024,128]{2,1,0:T(8,128)S(1)}) custom-call(s32[1]{0:T(128)} %bitcast.own_ref, f32[3,256,256]{2,1,0:T(8,128)S(1)} %collective-permute-done.1.tail_ref, f32[2,1024,128]{2,1,0:T(8,128)S(1)} %copy-done.2, f32[2,1024,128]{2,1,0:T(8,128)S(1)} %copy-done.3, f32[16,2048,256]{2,1,0:T(8,128)} %refs_2_.3, ...), custom_call_target="tpu_custom_call" | custom-call | flops 1 | bytes 1 | tf_op jit(solution)/shard_map/carried/pallas_call | solution.py:211
  83.5 4.1 %collective-permute-done.8 = f32[1,1024,128]{2,1,0:T(8,128)S(1)} collective-permute-done((f32[1,1024,128]{2,1,0:T(8,128)S(1)}, f32[1,1024,128]{2,1,0:T(8,128)S(1)}, u32[]{:S(2)}, u32[]{:S(2)}) %collective-permute-start.8) | collective-permute-done | bytes 524320 | tf_op jit(solution)/shard_map/ppermute | solution.py:24
  89.2 1.7 %collective-permute-start.13 = (f32[2048,256]{1,0:T(8,128)S(1)}, f32[2048,256]{1,0:T(8,128)S(1)}, u32[]{:S(2)}, u32[]{:S(2)}) collective-permute-start(f32[2048,256]{1,0:T(8,128)S(1)} %copy-done), channel_id=1, source_target_pairs={{0,8},{1,9},{2,10},{3,11},{4,12},{5,13},{6,14},{7,15}} | collective-permute-start | bytes 6291464 | tf_op jit(solution)/shard_map/ppermute | solution.py:508
  92.5 1.6 collective-permute-start.15
  94.1 2.9 %collective-permute-done.12 = f32[1,128,128]{2,1,0:T(8,128)S(1)} collective-permute-done((f32[1,128,128]{2,1,0:T(8,128)S(1)}, f32[1,128,128]{2,1,0:T(8,128)S(1)}, u32[]{:S(2)}, u32[]{:S(2)}) %collective-permute-start.12) | collective-permute-done | bytes 65568 | tf_op jit(solution)/shard_map/ppermute | solution.py:24
  98.7 2.5 %collective-permute-done.15 = f32[4,128,128]{2,1,0:T(8,128)S(1)} collective-permute-done((f32[4,128,128]{2,1,0:T(8,128)S(1)}, f32[4,128,128]{2,1,0:T(8,128)S(1)}, u32[]{:S(2)}, u32[]{:S(2)}) %collective-permute-start.15) | collective-permute-done | bytes 262176 | tf_op jit(solution)/shard_map/ppermute | solution.py:24
  101.2 1.6 %collective-permute-start.16 = (f32[128,128]{1,0:T(8,128)S(1)}, f32[128,128]{1,0:T(8,128)S(1)}, u32[]{:S(2)}, u32[]{:S(2)}) collective-permute-start(f32[128,128]{1,0:T(8,128)S(1)} %get-tuple-element.157), channel_id=1, source_target_pairs={{0,2},{1,3},{2,0},{3,1},{4,6},{5,7},{6,4},{7,5},{8,10},{9,11},{10,... | collective-permute-start | bytes 196616 | tf_op jit(solution)/shard_map/ppermute | solution.py:24
  102.9 2.6 %collective-permute-start.17 = (f32[128,128]{1,0:T(8,128)S(1)}, f32[128,128]{1,0:T(8,128)S(1)}, u32[]{:S(2)}, u32[]{:S(2)}) collective-permute-start(f32[128,128]{1,0:T(8,128)S(1)} %get-tuple-element.156), channel_id=1, source_target_pairs={{0,4},{1,5},{2,6},{3,7},{4,0},{5,1},{6,2},{7,3},{8,12},{9,13},{10,... | collective-permute-start | bytes 196616 | tf_op jit(solution)/shard_map/ppermute | solution.py:24
  105.6 4.0 %collective-permute-start.18 = (f32[128,128]{1,0:T(8,128)S(1)}, f32[128,128]{1,0:T(8,128)S(1)}, u32[]{:S(2)}, u32[]{:S(2)}) collective-permute-start(f32[128,128]{1,0:T(8,128)S(1)} %get-tuple-element.155), channel_id=1, source_target_pairs={{0,6},{1,7},{2,4},{3,5},{4,2},{5,3},{6,0},{7,1},{8,14},{9,15},{10,... | collective-permute-start | bytes 196616 | tf_op jit(solution)/shard_map/ppermute | solution.py:24
  109.9 1.9 %collective-permute-done.18.refs_3_ = f32[128,128]{1,0:T(8,128)S(1)} collective-permute-done((f32[128,128]{1,0:T(8,128)S(1)}, f32[128,128]{1,0:T(8,128)S(1)}, u32[]{:S(2)}, u32[]{:S(2)}) %collective-permute-start.18) | collective-permute-done | bytes 65568 | tf_op jit(solution)/shard_map/ppermute | solution.py:24
  113.2 1.9 %collective-permute-start.19 = (f32[1,128,128]{2,1,0:T(8,128)S(1)}, f32[1,128,128]{2,1,0:T(8,128)S(1)}, u32[]{:S(2)}, u32[]{:S(2)}) collective-permute-start(f32[1,128,128]{2,1,0:T(8,128)S(1)} %bitcast.68), channel_id=1, source_target_pairs={{0,16},{8,24},{16,0},{24,8},{1,17},{9,25},{17,1},{25,9},{2,18},{10... | collective-permute-start | bytes 196616 | tf_op jit(solution)/shard_map/ppermute | solution.py:24
  115.2 1.6 collective-permute-start.23
  117.5 2.2 %late.3 = f32[2,1024,128]{2,1,0:T(8,128)S(1)} custom-call(s32[1]{0:T(128)} %bitcast.own_ref, f32[2,1024,128]{2,1,0:T(8,128)S(1)} %add.72.acc_ref, f32[2048,256]{1,0:T(8,128)S(1)} %copy-done, f32[2048,256]{1,0:T(8,128)S(1)} %collective-permute-done.13.refs_1_, f32[2,128,128]{2,1,0:T(8,128)S(1)} %get-tuple-element.165.refs_2_, f32[2048,256]{1,0:T(8,128)S(1)} %copy-done.1, ...), custom_call_target="tpu_custom_call" | custom-call | flops 1 | bytes 1 | tf_op jit(solution)/shard_map/late/pallas_call | solution.py:377
  119.9 1.8 %collective-permute-done.23 = f32[4,128,128]{2,1,0:T(8,128)S(1)} collective-permute-done((f32[4,128,128]{2,1,0:T(8,128)S(1)}, f32[4,128,128]{2,1,0:T(8,128)S(1)}, u32[]{:S(2)}, u32[]{:S(2)}) %collective-permute-start.23) | collective-permute-done | bytes 262176 | tf_op jit(solution)/shard_map/ppermute | solution.py:24
  122.4 3.0 %collective-permute-start.25 = (f32[128,128]{1,0:T(8,128)S(1)}, f32[128,128]{1,0:T(8,128)S(1)}, u32[]{:S(2)}, u32[]{:S(2)}) collective-permute-start(f32[128,128]{1,0:T(8,128)S(1)} %get-tuple-element.152), channel_id=1, source_target_pairs={{0,4},{1,5},{2,6},{3,7},{4,0},{5,1},{6,2},{7,3},{8,12},{9,13},{10,... | collective-permute-start | bytes 196616 | tf_op jit(solution)/shard_map/ppermute | solution.py:24
  127.7 3.8 %collective-permute-done.26.refs_3_ = f32[128,128]{1,0:T(8,128)S(1)} collective-permute-done((f32[128,128]{1,0:T(8,128)S(1)}, f32[128,128]{1,0:T(8,128)S(1)}, u32[]{:S(2)}, u32[]{:S(2)}) %collective-permute-start.26) | collective-permute-done | bytes 65568 | tf_op jit(solution)/shard_map/ppermute | solution.py:24
  135.1 1.8 %collective-permute-done.27 = f32[1,128,128]{2,1,0:T(8,128)S(1)} collective-permute-done((f32[1,128,128]{2,1,0:T(8,128)S(1)}, f32[1,128,128]{2,1,0:T(8,128)S(1)}, u32[]{:S(2)}, u32[]{:S(2)}) %collective-permute-start.27) | collective-permute-done | bytes 65568 | tf_op jit(solution)/shard_map/ppermute | solution.py:24
  137.0 2.9 %collective-permute-done.29 = f32[4,128,128]{2,1,0:T(8,128)S(1)} collective-permute-done((f32[4,128,128]{2,1,0:T(8,128)S(1)}, f32[4,128,128]{2,1,0:T(8,128)S(1)}, u32[]{:S(2)}, u32[]{:S(2)}) %collective-permute-start.29) | collective-permute-done | bytes 262176 | tf_op jit(solution)/shard_map/ppermute | solution.py:24
  140.8 2.6 %collective-permute-start.31 = (f32[128,128]{1,0:T(8,128)S(1)}, f32[128,128]{1,0:T(8,128)S(1)}, u32[]{:S(2)}, u32[]{:S(2)}) collective-permute-start(f32[128,128]{1,0:T(8,128)S(1)} %get-tuple-element.148), channel_id=1, source_target_pairs={{0,4},{1,5},{2,6},{3,7},{4,0},{5,1},{6,2},{7,3},{8,12},{9,13},{10,... | collective-permute-start | bytes 196616 | tf_op jit(solution)/shard_map/ppermute | solution.py:24
  144.5 1.6 %assemble.2.refs_0_ = f32[4,256,256]{2,1,0:T(8,128)} custom-call(s32[1]{0:T(128)} %bitcast.own_ref, f32[4,3,128,128]{3,2,1,0:T(8,128)S(1)} %pad_maximum_fusion.parts_ref), custom_call_target="tpu_custom_call" | custom-call | flops 1 | bytes 1 | tf_op jit(solution)/shard_map/assemble/pallas_call | solution.py:361
  147.3 2.1 %collective-permute-done.32 = f32[128,128]{1,0:T(8,128)S(1)} collective-permute-done((f32[128,128]{1,0:T(8,128)S(1)}, f32[128,128]{1,0:T(8,128)S(1)}, u32[]{:S(2)}, u32[]{:S(2)}) %collective-permute-start.32) | collective-permute-done | bytes 65568 | tf_op jit(solution)/shard_map/ppermute | solution.py:24
  149.5 1.8 %collective-permute-start.33 = (f32[1,128,128]{2,1,0:T(8,128)S(1)}, f32[1,128,128]{2,1,0:T(8,128)S(1)}, u32[]{:S(2)}, u32[]{:S(2)}) collective-permute-start(f32[1,128,128]{2,1,0:T(8,128)S(1)} %fusion.2), channel_id=1, source_target_pairs={{0,16},{8,24},{16,0},{24,8},{1,17},{9,25},{17,1},{25,9},{2,18},{10... | collective-permute-start | bytes 196616 | tf_op jit(solution)/shard_map/ppermute | solution.py:24
  151.3 2.5 %collective-permute-done.33 = f32[1,128,128]{2,1,0:T(8,128)S(1)} collective-permute-done((f32[1,128,128]{2,1,0:T(8,128)S(1)}, f32[1,128,128]{2,1,0:T(8,128)S(1)}, u32[]{:S(2)}, u32[]{:S(2)}) %collective-permute-start.33) | collective-permute-done | bytes 65568 | tf_op jit(solution)/shard_map/ppermute | solution.py:24
  (100 shorter events, 31.5 us)
Async XLA Ops:
  3.4 45.9 %collective-permute-start = (f32[2048,256]{1,0:T(8,128)}, f32[2048,256]{1,0:T(8,128)}, u32[]{:S(2)}, u32[]{:S(2)}) collective-permute-start(f32[2048,256]{1,0:T(8,128)} %get-tuple-element.86), channel_id=1, source_target_pairs={{0,16},{1,17},{2,18},{3,19},{4,20},{5,21},{6,22},{7,23}} | collective-permute-start | bytes 6291464 | tf_op jit(solution)/shard_map/ppermute | solution.py:453
  9.7 39.6 %collective-permute-start.1 = (f32[3,256,256]{2,1,0:T(8,128)}, f32[3,256,256]{2,1,0:T(8,128)S(1)}, u32[]{:S(2)}, u32[]{:S(2)}) collective-permute-start(f32[3,256,256]{2,1,0:T(8,128)} %get-tuple-element.75), channel_id=1, source_target_pairs={{0,8},{8,16},{16,24},{1,9},{9,17},{17,25},{2,10},{10,18},{18,26},{... | collective-permute-start | bytes 2359304 | tf_op jit(solution)/shard_map/ppermute | solution.py:454
  53.7 9.2 %collective-permute-start.3 = (f32[2,4,128,128]{3,2,1,0:T(8,128)S(1)}, f32[2,4,128,128]{3,2,1,0:T(8,128)S(1)}, u32[]{:S(2)}, u32[]{:S(2)}) collective-permute-start(f32[2,4,128,128]{3,2,1,0:T(8,128)S(1)} %pad_maximum_fusion.1), channel_id=1, source_target_pairs={{0,1},{1,0},{2,3},{3,2},{4,5},{5,4},{6,7},{7,6},{8,24},{9,25},{10,... | collective-permute-start | bytes 1572872 | tf_op jit(solution)/shard_map/ppermute | solution.py:420
  63.9 9.0 %collective-permute-start.5 = (f32[2048,256]{1,0:T(8,128)S(1)}, f32[2048,256]{1,0:T(8,128)S(1)}, u32[]{:S(2)}, u32[]{:S(2)}) collective-permute-start(f32[2048,256]{1,0:T(8,128)S(1)} %broadcast_select_fusion.m_ref), channel_id=1, source_target_pairs={{0,8},{16,24},{1,9},{17,25},{2,10},{18,26},{3,11},{19,27},{4,12},{... | collective-permute-start | bytes 6291464 | tf_op jit(solution)/shard_map/ppermute | solution.py:475
  65.4 7.6 %collective-permute-start.7 = (f32[2,1024,128]{2,1,0:T(8,128)S(1)}, f32[2,1024,128]{2,1,0:T(8,128)S(1)}, u32[]{:S(2)}, u32[]{:S(2)}) collective-permute-start(f32[2,1024,128]{2,1,0:T(8,128)S(1)} %get-tuple-element.103), channel_id=1, source_target_pairs={{0,8},{8,0},{16,24},{24,16},{1,9},{9,1},{17,25},{25,17},{2,10},{10... | collective-permute-start | bytes 3145736 | tf_op jit(solution)/shard_map/ppermute | solution.py:24
  65.5 6.4 %collective-permute-start.4 = (f32[1,4,128,128]{3,2,1,0:T(8,128)S(1)}, f32[1,4,128,128]{3,2,1,0:T(8,128)S(1)}, u32[]{:S(2)}, u32[]{:S(2)}) collective-permute-start(f32[1,4,128,128]{3,2,1,0:T(8,128)S(1)} %slice_add_fusion.2), channel_id=1, source_target_pairs={{0,16},{1,17},{2,18},{3,19},{4,20},{5,21},{6,22},{7,23},{8,9},{9,8... | collective-permute-start | bytes 786440 | tf_op jit(solution)/shard_map/ppermute | solution.py:420
  72.9 10.5 %collective-permute-start.6 = (f32[2,1024,128]{2,1,0:T(8,128)S(1)}, f32[2,1024,128]{2,1,0:T(8,128)S(1)}, u32[]{:S(2)}, u32[]{:S(2)}) collective-permute-start(f32[2,1024,128]{2,1,0:T(8,128)S(1)} %get-tuple-element.100), channel_id=1, source_target_pairs={{0,8},{8,0},{16,24},{24,16},{1,9},{9,1},{17,25},{25,17},{2,10},{10... | collective-permute-start | bytes 3145736 | tf_op jit(solution)/shard_map/ppermute | solution.py:24
  73.2 14.4 %collective-permute-start.8 = (f32[1,1024,128]{2,1,0:T(8,128)S(1)}, f32[1,1024,128]{2,1,0:T(8,128)S(1)}, u32[]{:S(2)}, u32[]{:S(2)}) collective-permute-start(f32[1,1024,128]{2,1,0:T(8,128)S(1)} %get-tuple-element.145), channel_id=1, source_target_pairs={{0,16},{8,24},{16,0},{24,8},{1,17},{9,25},{17,1},{25,9},{2,18},{10... | collective-permute-start | bytes 1572872 | tf_op jit(solution)/shard_map/ppermute | solution.py:24
  73.3 14.3 %collective-permute-start.10 = (f32[128,128]{1,0:T(8,128)S(1)}, f32[128,128]{1,0:T(8,128)S(1)}, u32[]{:S(2)}, u32[]{:S(2)}) collective-permute-start(f32[128,128]{1,0:T(8,128)S(1)} %get-tuple-element.107), channel_id=1, source_target_pairs={{0,4},{1,5},{2,6},{3,7},{4,0},{5,1},{6,2},{7,3},{8,12},{9,13},{10,... | collective-permute-start | bytes 196616 | tf_op jit(solution)/shard_map/ppermute | solution.py:24
  76.0 11.6 %collective-permute-start.11 = (f32[128,128]{1,0:T(8,128)S(1)}, f32[128,128]{1,0:T(8,128)S(1)}, u32[]{:S(2)}, u32[]{:S(2)}) collective-permute-start(f32[128,128]{1,0:T(8,128)S(1)} %get-tuple-element.108), channel_id=1, source_target_pairs={{0,6},{1,7},{2,4},{3,5},{4,2},{5,3},{6,0},{7,1},{8,14},{9,15},{10,... | collective-permute-start | bytes 196616 | tf_op jit(solution)/shard_map/ppermute | solution.py:24
  77.3 10.3 %collective-permute-start.9 = (f32[128,128]{1,0:T(8,128)S(1)}, f32[128,128]{1,0:T(8,128)S(1)}, u32[]{:S(2)}, u32[]{:S(2)}) collective-permute-start(f32[128,128]{1,0:T(8,128)S(1)} %get-tuple-element.106), channel_id=1, source_target_pairs={{0,2},{1,3},{2,0},{3,1},{4,6},{5,7},{6,4},{7,5},{8,10},{9,11},{10,... | collective-permute-start | bytes 196616 | tf_op jit(solution)/shard_map/ppermute | solution.py:24
  89.2 7.8 %collective-permute-start.13 = (f32[2048,256]{1,0:T(8,128)S(1)}, f32[2048,256]{1,0:T(8,128)S(1)}, u32[]{:S(2)}, u32[]{:S(2)}) collective-permute-start(f32[2048,256]{1,0:T(8,128)S(1)} %copy-done), channel_id=1, source_target_pairs={{0,8},{1,9},{2,10},{3,11},{4,12},{5,13},{6,14},{7,15}} | collective-permute-start | bytes 6291464 | tf_op jit(solution)/shard_map/ppermute | solution.py:508
  91.0 26.6 %collective-permute-start.21 = (f32[2048,256]{1,0:T(8,128)S(1)}, f32[2048,256]{1,0:T(8,128)S(1)}, u32[]{:S(2)}, u32[]{:S(2)}) collective-permute-start(f32[2048,256]{1,0:T(8,128)S(1)} %copy-done.1), channel_id=1, source_target_pairs={{0,8},{1,9},{2,10},{3,11},{4,12},{5,13},{6,14},{7,15}} | collective-permute-start | bytes 6291464 | tf_op jit(solution)/shard_map/ppermute | solution.py:508
  92.4 22.7 %collective-permute-start.20 = (f32[2,1024,128]{2,1,0:T(8,128)S(1)}, f32[2,1024,128]{2,1,0:T(8,128)S(1)}, u32[]{:S(2)}, u32[]{:S(2)}) collective-permute-start(f32[2,1024,128]{2,1,0:T(8,128)S(1)} %get-tuple-element.127), channel_id=1, source_target_pairs={{0,8},{8,0},{16,24},{24,16},{1,9},{9,1},{17,25},{25,17},{2,10},{10... | collective-permute-start | bytes 3145736 | tf_op jit(solution)/shard_map/ppermute | solution.py:24
  92.5 4.5 %collective-permute-start.12 = (f32[1,128,128]{2,1,0:T(8,128)S(1)}, f32[1,128,128]{2,1,0:T(8,128)S(1)}, u32[]{:S(2)}, u32[]{:S(2)}) collective-permute-start(f32[1,128,128]{2,1,0:T(8,128)S(1)} %bitcast.66), channel_id=1, source_target_pairs={{0,16},{8,24},{16,0},{24,8},{1,17},{9,25},{17,1},{25,9},{2,18},{10... | collective-permute-start | bytes 196616 | tf_op jit(solution)/shard_map/ppermute | solution.py:24
  92.5 8.6 %collective-permute-start.15 = (f32[4,128,128]{2,1,0:T(8,128)S(1)}, f32[4,128,128]{2,1,0:T(8,128)S(1)}, u32[]{:S(2)}, u32[]{:S(2)}) collective-permute-start(f32[4,128,128]{2,1,0:T(8,128)S(1)} %get-tuple-element.124), channel_id=1, source_target_pairs={{0,1},{1,0},{2,3},{3,2},{4,5},{5,4},{6,7},{7,6},{8,9},{9,8},{10,11... | collective-permute-start | bytes 786440 | tf_op jit(solution)/shard_map/ppermute | solution.py:24
  98.6 13.6 %collective-permute-start.14 = (f32[1,1024,128]{2,1,0:T(8,128)S(1)}, f32[1,1024,128]{2,1,0:T(8,128)S(1)}, u32[]{:S(2)}, u32[]{:S(2)}) collective-permute-start(f32[1,1024,128]{2,1,0:T(8,128)S(1)} %get-tuple-element.143), channel_id=1, source_target_pairs={{0,16},{8,24},{16,0},{24,8},{1,17},{9,25},{17,1},{25,9},{2,18},{10... | collective-permute-start | bytes 1572872 | tf_op jit(solution)/shard_map/ppermute | solution.py:24
  102.9 7.0 %collective-permute-start.17 = (f32[128,128]{1,0:T(8,128)S(1)}, f32[128,128]{1,0:T(8,128)S(1)}, u32[]{:S(2)}, u32[]{:S(2)}) collective-permute-start(f32[128,128]{1,0:T(8,128)S(1)} %get-tuple-element.156), channel_id=1, source_target_pairs={{0,4},{1,5},{2,6},{3,7},{4,0},{5,1},{6,2},{7,3},{8,12},{9,13},{10,... | collective-permute-start | bytes 196616 | tf_op jit(solution)/shard_map/ppermute | solution.py:24
  105.6 6.2 %collective-permute-start.18 = (f32[128,128]{1,0:T(8,128)S(1)}, f32[128,128]{1,0:T(8,128)S(1)}, u32[]{:S(2)}, u32[]{:S(2)}) collective-permute-start(f32[128,128]{1,0:T(8,128)S(1)} %get-tuple-element.155), channel_id=1, source_target_pairs={{0,6},{1,7},{2,4},{3,5},{4,2},{5,3},{6,0},{7,1},{8,14},{9,15},{10,... | collective-permute-start | bytes 196616 | tf_op jit(solution)/shard_map/ppermute | solution.py:24
  113.2 4.3 %collective-permute-start.19 = (f32[1,128,128]{2,1,0:T(8,128)S(1)}, f32[1,128,128]{2,1,0:T(8,128)S(1)}, u32[]{:S(2)}, u32[]{:S(2)}) collective-permute-start(f32[1,128,128]{2,1,0:T(8,128)S(1)} %bitcast.68), channel_id=1, source_target_pairs={{0,16},{8,24},{16,0},{24,8},{1,17},{9,25},{17,1},{25,9},{2,18},{10... | collective-permute-start | bytes 196616 | tf_op jit(solution)/shard_map/ppermute | solution.py:24
  115.2 6.4 %collective-permute-start.23 = (f32[4,128,128]{2,1,0:T(8,128)S(1)}, f32[4,128,128]{2,1,0:T(8,128)S(1)}, u32[]{:S(2)}, u32[]{:S(2)}) collective-permute-start(f32[4,128,128]{2,1,0:T(8,128)S(1)} %get-tuple-element.130), channel_id=1, source_target_pairs={{0,1},{1,0},{2,3},{3,2},{4,5},{5,4},{6,7},{7,6},{8,9},{9,8},{10,11... | collective-permute-start | bytes 786440 | tf_op jit(solution)/shard_map/ppermute | solution.py:24
  119.8 11.7 %collective-permute-start.22 = (f32[1,1024,128]{2,1,0:T(8,128)S(1)}, f32[1,1024,128]{2,1,0:T(8,128)S(1)}, u32[]{:S(2)}, u32[]{:S(2)}) collective-permute-start(f32[1,1024,128]{2,1,0:T(8,128)S(1)} %get-tuple-element.141), channel_id=1, source_target_pairs={{0,16},{8,24},{16,0},{24,8},{1,17},{9,25},{17,1},{25,9},{2,18},{10... | collective-permute-start | bytes 1572872 | tf_op jit(solution)/shard_map/ppermute | solution.py:24
  121.7 5.0 %collective-permute-start.24 = (f32[128,128]{1,0:T(8,128)S(1)}, f32[128,128]{1,0:T(8,128)S(1)}, u32[]{:S(2)}, u32[]{:S(2)}) collective-permute-start(f32[128,128]{1,0:T(8,128)S(1)} %get-tuple-element.153), channel_id=1, source_target_pairs={{0,2},{1,3},{2,0},{3,1},{4,6},{5,7},{6,4},{7,5},{8,10},{9,11},{10,... | collective-permute-start | bytes 196616 | tf_op jit(solution)/shard_map/ppermute | solution.py:24
  122.4 5.3 %collective-permute-start.25 = (f32[128,128]{1,0:T(8,128)S(1)}, f32[128,128]{1,0:T(8,128)S(1)}, u32[]{:S(2)}, u32[]{:S(2)}) collective-permute-start(f32[128,128]{1,0:T(8,128)S(1)} %get-tuple-element.152), channel_id=1, source_target_pairs={{0,4},{1,5},{2,6},{3,7},{4,0},{5,1},{6,2},{7,3},{8,12},{9,13},{10,... | collective-permute-start | bytes 196616 | tf_op jit(solution)/shard_map/ppermute | solution.py:24
  125.5 6.1 %collective-permute-start.26 = (f32[128,128]{1,0:T(8,128)S(1)}, f32[128,128]{1,0:T(8,128)S(1)}, u32[]{:S(2)}, u32[]{:S(2)}) collective-permute-start(f32[128,128]{1,0:T(8,128)S(1)} %get-tuple-element.151), channel_id=1, source_target_pairs={{0,6},{1,7},{2,4},{3,5},{4,2},{5,3},{6,0},{7,1},{8,14},{9,15},{10,... | collective-permute-start | bytes 196616 | tf_op jit(solution)/shard_map/ppermute | solution.py:24
  132.6 4.3 %collective-permute-start.27 = (f32[1,128,128]{2,1,0:T(8,128)S(1)}, f32[1,128,128]{2,1,0:T(8,128)S(1)}, u32[]{:S(2)}, u32[]{:S(2)}) collective-permute-start(f32[1,128,128]{2,1,0:T(8,128)S(1)} %bitcast.70), channel_id=1, source_target_pairs={{0,16},{8,24},{16,0},{24,8},{1,17},{9,25},{17,1},{25,9},{2,18},{10... | collective-permute-start | bytes 196616 | tf_op jit(solution)/shard_map/ppermute | solution.py:24
  133.6 6.4 %collective-permute-start.29 = (f32[4,128,128]{2,1,0:T(8,128)S(1)}, f32[4,128,128]{2,1,0:T(8,128)S(1)}, u32[]{:S(2)}, u32[]{:S(2)}) collective-permute-start(f32[4,128,128]{2,1,0:T(8,128)S(1)} %get-tuple-element.133), channel_id=1, source_target_pairs={{0,1},{1,0},{2,3},{3,2},{4,5},{5,4},{6,7},{7,6},{8,9},{9,8},{10,11... | collective-permute-start | bytes 786440 | tf_op jit(solution)/shard_map/ppermute | solution.py:24
  136.9 7.5 %collective-permute-start.28 = (f32[2,3,128,128]{3,2,1,0:T(8,128)S(1)}, f32[2,3,128,128]{3,2,1,0:T(8,128)S(1)}, u32[]{:S(2)}, u32[]{:S(2)}) collective-permute-start(f32[2,3,128,128]{3,2,1,0:T(8,128)S(1)} %pad_maximum_fusion.2), channel_id=1, source_target_pairs={{0,8},{8,0},{16,24},{24,16},{1,9},{9,1},{17,25},{25,17},{2,10},{10... | collective-permute-start | bytes 1179656 | tf_op jit(solution)/shard_map/ppermute | solution.py:24
  140.0 6.1 %collective-permute-start.30 = (f32[128,128]{1,0:T(8,128)S(1)}, f32[128,128]{1,0:T(8,128)S(1)}, u32[]{:S(2)}, u32[]{:S(2)}) collective-permute-start(f32[128,128]{1,0:T(8,128)S(1)} %get-tuple-element.149), channel_id=1, source_target_pairs={{0,2},{1,3},{2,0},{3,1},{4,6},{5,7},{6,4},{7,5},{8,10},{9,11},{10,... | collective-permute-start | bytes 196616 | tf_op jit(solution)/shard_map/ppermute | solution.py:24
  140.8 6.6 %collective-permute-start.31 = (f32[128,128]{1,0:T(8,128)S(1)}, f32[128,128]{1,0:T(8,128)S(1)}, u32[]{:S(2)}, u32[]{:S(2)}) collective-permute-start(f32[128,128]{1,0:T(8,128)S(1)} %get-tuple-element.148), channel_id=1, source_target_pairs={{0,4},{1,5},{2,6},{3,7},{4,0},{5,1},{6,2},{7,3},{8,12},{9,13},{10,... | collective-permute-start | bytes 196616 | tf_op jit(solution)/shard_map/ppermute | solution.py:24
  143.4 6.1 %collective-permute-start.32 = (f32[128,128]{1,0:T(8,128)S(1)}, f32[128,128]{1,0:T(8,128)S(1)}, u32[]{:S(2)}, u32[]{:S(2)}) collective-permute-start(f32[128,128]{1,0:T(8,128)S(1)} %get-tuple-element.147), channel_id=1, source_target_pairs={{0,6},{1,7},{2,4},{3,5},{4,2},{5,3},{6,0},{7,1},{8,14},{9,15},{10,... | collective-permute-start | bytes 196616 | tf_op jit(solution)/shard_map/ppermute | solution.py:24
  149.5 4.3 %collective-permute-start.33 = (f32[1,128,128]{2,1,0:T(8,128)S(1)}, f32[1,128,128]{2,1,0:T(8,128)S(1)}, u32[]{:S(2)}, u32[]{:S(2)}) collective-permute-start(f32[1,128,128]{2,1,0:T(8,128)S(1)} %fusion.2), channel_id=1, source_target_pairs={{0,16},{8,24},{16,0},{24,8},{1,17},{9,25},{17,1},{25,9},{2,18},{10... | collective-permute-start | bytes 196616 | tf_op jit(solution)/shard_map/ppermute | solution.py:24
  (14 other events, 58.2 us)
